TPU v7x, 512 devices: a whole 4x8x8 slice. The times are simulated.
512 devices in a mesh: seq: 64 (over y, x, core), tp: 8 (over z).
Axes of the slice: x: 4, y: 8, z: 8, core: 2. Of those that a mesh axis runs over, the one named last changes fastest.
Arguments:
- byte_acts: bfloat16 [12288, 4096], P('seq', 'tp'), may hold values from -6 to 6
- upstream: bfloat16 [12288, 4096], P('seq', 'tp'), may hold values from -6 to 6
- segment_ids: int32 [12288], P('seq'), may hold values from 0 to 6143, never falling along the last dimension, each value on 1 to 40 neighbouring positions
- first_weight: bfloat16 [4096, 6144], P('seq', 'tp'), may hold values from -0.09375 to 0.09375
- second_weight: bfloat16 [4096, 6144], P('seq', 'tp'), may hold values from -0.078125 to 0.078125
Outputs:
- byte_grad: bfloat16 [12288, 4096], P('seq', 'tp')
Inputs may be any that keep to these rules, and one draw needn't show every extreme that they name: `segment_ids`: segment numbers never fall along the bytes; every number is used; each segment holds 1 to 40 bytes, one exactly 40.
All inputs are finite; a program needn't handle non-finite values.
Results may differ from a plain program's by a relative error of at most 0.009.
Values may be sent and summed in bfloat16 or wider, within the bound.
No kernel may reach another device: no remote copies, remote signals or barrier semaphores. Data moves between devices by JAX's collectives and lax.ppermute only.
A program may use at most 64 MiB of HBM per device.

v0:
```python
import jax
import jax.numpy as jnp
from jax import lax
from jax.sharding import PartitionSpec as P

epsilon = 1e-06


def shifted(shard, axis, by):
    count = lax.axis_size(axis)
    pairs = [(i, i + by) for i in range(count) if 0 <= i + by < count]
    return lax.ppermute(shard, axis, pairs)


def body(byte_acts, upstream, segment_ids, first_weight, second_weight):
    byte_rows = segment_ids.shape[0]
    model_width = byte_acts.shape[1] * lax.axis_size("tp")
    base_id = segment_ids[0]
    last_id = segment_ids[byte_rows - 1]
    slot_of = segment_ids - base_id
    slot_index = jnp.arange(byte_rows, dtype=jnp.int32)
    member = slot_index[:, None] == slot_of[None, :]
    member_b = member.astype(jnp.bfloat16)
    seg_sums = jnp.dot(member_b, byte_acts, preferred_element_type=jnp.float32)
    grad_sums = jnp.dot(member_b, upstream, preferred_element_type=jnp.float32)
    counts = jnp.sum(member.astype(jnp.float32), axis=1)
    head_tag = (base_id + 1).astype(jnp.float32).reshape(1)
    tail_x, tail_grad, tail_count, tail_tag = shifted(
        (seg_sums[:1], grad_sums[:1], counts[:1], head_tag), "seq", -1
    )
    matched = tail_tag[0] == (last_id + 1).astype(jnp.float32)
    tail_pick = ((slot_index == last_id - base_id) & matched).astype(jnp.float32)
    seg_sums = seg_sums + tail_pick[:, None] * tail_x
    grad_sums = grad_sums + tail_pick[:, None] * tail_grad
    counts = counts + tail_pick * tail_count[0]
    safe_counts = jnp.maximum(counts, 1.0)
    pooled = seg_sums / safe_counts[:, None]
    square_sums = lax.psum(jnp.sum(pooled * pooled, axis=1), "tp")
    inv_rms = lax.rsqrt(square_sums / model_width + epsilon)
    normed = pooled * inv_rms[:, None]
    normed_b, grad_b = (
        lax.all_gather(normed.astype(jnp.bfloat16), "tp", axis=1, tiled=True),
        lax.all_gather(grad_sums.astype(jnp.bfloat16), "tp", axis=1, tiled=True),
    )
    first_full = lax.all_gather(first_weight, "seq", axis=0, tiled=True)
    back_proj = jnp.dot(
        grad_b,
        lax.all_gather(second_weight, "seq", axis=0, tiled=True),
        preferred_element_type=jnp.float32,
    )
    up_proj = jnp.dot(normed_b, first_full, preferred_element_type=jnp.float32)
    sigmoid_up = jax.nn.sigmoid(up_proj)
    grad_hidden = (back_proj * sigmoid_up * (1.0 + up_proj * (1.0 - sigmoid_up))).astype(
        jnp.bfloat16
    )
    partial_grad = lax.dot_general(
        grad_hidden, first_full, (((1,), (1,)), ((), ())), preferred_element_type=jnp.float32
    )
    norm_grad = lax.psum_scatter(
        partial_grad.astype(jnp.bfloat16), "tp", scatter_dimension=1, tiled=True
    ).astype(jnp.float32)
    norm_dot = lax.psum(jnp.sum(norm_grad * normed, axis=1), "tp")
    pooled_grad = grad_sums + inv_rms[:, None] * (
        norm_grad - normed * (norm_dot / model_width)[:, None]
    )
    byte_share = pooled_grad / safe_counts[:, None]
    tail_row = lax.dynamic_slice_in_dim(byte_share, last_id - base_id, 1, 0)
    tail_mark = (last_id + 1).astype(jnp.float32).reshape(1)
    head_row, head_mark = shifted((tail_row, tail_mark), "seq", 1)
    joined = head_mark[0] == (base_id + 1).astype(jnp.float32)
    first_fix = (slot_index == 0) & joined
    byte_share = jnp.where(first_fix[:, None], head_row, byte_share)
    spread = jnp.dot(
        member.astype(jnp.float32).T,
        byte_share,
        precision=lax.Precision.HIGHEST,
        preferred_element_type=jnp.float32,
    )
    return (upstream.astype(jnp.float32) + spread).astype(jnp.bfloat16)


def solution(mesh):
    return jax.shard_map(
        body,
        mesh=mesh,
        in_specs=(P("seq", "tp"), P("seq", "tp"), P("seq"), P("seq", "tp"), P("seq", "tp")),
        out_specs=P("seq", "tp"),
        check_vma=False,
    )
```

profile of v0, /device:TPU:1, one launch (start us, length us, event | category | flops | bytes accessed | tf_op | source)
XLA Modules:
  0.0 391.3 jit_solution(1465758358438963785)
XLA Ops:
  6.5 1.3 fusion.19
  7.9 1.3 broadcast_subtract_fusion
  9.2 0.1 convert_reduce_fusion
  9.3 0.5 slice.19
  9.8 8.8 %collective-permute-start.4 = (f32[1]{0:T(128)}, f32[1]{0:T(128)}, u32[]{:S(2)}, u32[]{:S(2)}) collective-permute-start(f32[1]{0:T(128)} %slice.19), channel_id=1, source_target_pairs={{8,0},{16,8},{24,16},{32,24},{40,32},{48,40},{56,48},{64,56},{72,6... | collective-permute-start | bytes 20 | tf_op jit(solution)/shard_map/ppermute | solution.py:12
  19.2 2.9 collective-permute-start.1
  22.1 1.1 fusion.12
  23.2 1.9 collective-permute-start.2
  25.2 0.2 fusion.11
  25.4 1.9 collective-permute-start.3
  29.9 0.7 add_maximum_fusion
  30.6 0.9 multiply_reduce_fusion
  31.5 14.4 %psum.14 = f32[192]{0:T(256)S(1)} all-reduce(f32[192]{0:T(256)S(1)} %get-tuple-element.5), channel_id=1, replica_groups=mesh['seq'=64,'tp'=8] {'tp'}, use_global_device_ids=true, to_apply=%region_2.0 | all-reduce | flops 192 | bytes 1536 | tf_op jit(solution)/shard_map/psum | solution.py:38
  45.9 0.8 multiply_convert_fusion
  46.7 0.7 all-gather.11.cloned.1.call-update
  47.4 0.7 all-gather.5.cloned.1.call-update
  48.2 0.5 all-gather.7.cloned.1.call-update
  48.8 39.7 %all-gather.9.cloned.1.call-done = bf16[192,4096]{1,0:T(8,128)(2,1)} async-done(((bf16[192,512]{1,0:T(8,128)(2,1)}), bf16[192,4096]{1,0:T(8,128)(2,1)}) %all-gather.9.cloned.1.call-update) | async-done | bytes 1572880 | tf_op jit(solution)/shard_map/all_gather | solution.py:42
  88.5 92.1 %all-gather.11.cloned.1.call-done = bf16[4096,768]{1,0:T(8,128)(2,1)} async-done(((bf16[64,768]{1,0:T(8,128)(2,1)}), bf16[4096,768]{1,0:T(8,128)(2,1)}) %all-gather.11.cloned.1.call-update) | async-done | bytes 6291472 | tf_op jit(solution)/shard_map/all_gather | solution.py:45
  180.6 4.7 %fusion.20 = f32[192,768]{1,0:T(8,128)S(1)} fusion(bf16[192,4096]{1,0:T(8,128)(2,1)} %all-gather.9.cloned.1.call-done, bf16[4096,768]{1,0:T(8,128)(2,1)} %all-gather.11.cloned.1.call-done), kind=kOutput, calls=%fused_computation.38 | convolution fusion | flops 1207959552 | bytes 8454144 | tf_op jit(solution)/shard_map/dot_general | solution.py:51
  185.3 33.5 %all-gather.5.cloned.1.call-done = bf16[192,4096]{1,0:T(8,128)(2,1)} async-done(((bf16[192,512]{1,0:T(8,128)(2,1)}), bf16[192,4096]{1,0:T(8,128)(2,1)}) %all-gather.5.cloned.1.call-update) | async-done | bytes 1572880 | tf_op jit(solution)/shard_map/all_gather | solution.py:43
  218.8 92.0 %all-gather.7.cloned.1.call-done = bf16[4096,768]{1,0:T(8,128)(2,1)} async-done(((bf16[64,768]{1,0:T(8,128)(2,1)}), bf16[4096,768]{1,0:T(8,128)(2,1)}) %all-gather.7.cloned.1.call-update) | async-done | bytes 6291472 | tf_op jit(solution)/shard_map/all_gather | solution.py:48
  310.8 10.1 %convolution_convert_fusion = bf16[192,4096]{1,0:T(8,128)(2,1)} fusion(bf16[4096,768]{1,0:T(8,128)(2,1)} %all-gather.11.cloned.1.call-done, bf16[192,4096]{1,0:T(8,128)(2,1)} %all-gather.5.cloned.1.call-done, bf16[4096,768]{1,0:T(8,128)(2,1)} %all-gather.7.cloned.1.call-done, f32[192,768]{1,0:T(8,128)S(1)} %fusion.20), kind=kOutput, calls=%fused_computation | convolution fusion | flops 2418032640 | bytes 16318464 | tf_op jit(solution)/shard_map/dot_general | solution.py:56
  321.0 3.0 collective-permute-start
  323.9 0.2 collective-permute-done
  324.7 32.8 %reduce-scatter.2.cloned.1.call-done = bf16[192,512]{1,0:T(8,128)(2,1)} async-done(((bf16[192,4096]{1,0:T(8,128)(2,1)}), bf16[192,512]{1,0:T(8,128)(2,1)}) %reduce-scatter.2.cloned.1.call-update) | async-done | bytes 196624 | tf_op jit(solution)/shard_map/reduce_scatter | solution.py:59
  357.5 1.1 fusion.3
  358.6 12.4 %psum.15 = f32[192]{0:T(256)S(1)} all-reduce(f32[192]{0:T(256)S(1)} %fusion.3), channel_id=1, replica_groups=mesh['seq'=64,'tp'=8] {'tp'}, use_global_device_ids=true, to_apply=%region_5.0 | all-reduce | flops 192 | bytes 1536 | tf_op jit(solution)/shard_map/psum | solution.py:62
  371.0 1.1 fusion.6
  372.2 10.6 %collective-permute-start.5 = (f32[1,512]{1,0:T(1,128)S(1)}, f32[1,512]{1,0:T(1,128)S(1)}, u32[]{:S(2)}, u32[]{:S(2)}) collective-permute-start(f32[1,512]{1,0:T(1,128)S(1)} %constant_dynamic-slice_fusion), channel_id=1, source_target_pairs={{0,8},{8,16},{16,24},{24,32},{32,40},{40,48},{48,56},{56,64},{64,7... | collective-permute-start | bytes 6152 | tf_op jit(solution)/shard_map/ppermute | solution.py:12
  382.9 0.7 collective-permute-done.5
  383.6 1.2 fusion.2
  (22 shorter events, 0.3 us)
Async XLA Ops:
  6.5 18.6 %copy-start = (bf16[192,512]{1,0:T(8,128)(2,1)S(1)}, bf16[192,512]{1,0:T(8,128)(2,1)}, u32[]{:S(2)}) copy-start(bf16[192,512]{1,0:T(8,128)(2,1)} %param.5) | copy-start | bytes 589828
  6.5 82.0 %all-gather.9.cloned.1.call-start = ((), (), s32[]{:S(2)}) async-start(), calls=%async_computation.3 | async-start | bytes 1769472 | tf_op jit(solution)/shard_map/all_gather | solution.py:42
  9.8 20.1 %collective-permute-start.4 = (f32[1]{0:T(128)}, f32[1]{0:T(128)}, u32[]{:S(2)}, u32[]{:S(2)}) collective-permute-start(f32[1]{0:T(128)} %slice.19), channel_id=1, source_target_pairs={{8,0},{16,8},{24,16},{32,24},{40,32},{48,40},{56,48},{64,56},{72,6... | collective-permute-start | bytes 20 | tf_op jit(solution)/shard_map/ppermute | solution.py:12
  19.2 10.0 %collective-permute-start.1 = (f32[1]{0:T(128)}, f32[1]{0:T(128)}, u32[]{:S(2)}, u32[]{:S(2)}) collective-permute-start(f32[1]{0:T(128)} %bitcast.4), channel_id=1, source_target_pairs={{8,0},{16,8},{24,16},{32,24},{40,32},{48,40},{56,48},{64,56},{72,6... | collective-permute-start | bytes 20 | tf_op jit(solution)/shard_map/ppermute | solution.py:12
  23.2 7.4 %collective-permute-start.2 = (f32[1,512]{1,0:T(1,128)S(1)}, f32[1,512]{1,0:T(1,128)S(1)}, u32[]{:S(2)}, u32[]{:S(2)}) collective-permute-start(f32[1,512]{1,0:T(1,128)S(1)} %slice.20), channel_id=1, source_target_pairs={{8,0},{16,8},{24,16},{32,24},{40,32},{48,40},{56,48},{64,56},{72,6... | collective-permute-start | bytes 6152 | tf_op jit(solution)/shard_map/ppermute | solution.py:12
  25.4 5.2 %collective-permute-start.3 = (f32[1,512]{1,0:T(1,128)S(1)}, f32[1,512]{1,0:T(1,128)S(1)}, u32[]{:S(2)}, u32[]{:S(2)}) collective-permute-start(f32[1,512]{1,0:T(1,128)S(1)} %slice.21), channel_id=1, source_target_pairs={{8,0},{16,8},{24,16},{32,24},{40,32},{48,40},{56,48},{64,56},{72,6... | collective-permute-start | bytes 6152 | tf_op jit(solution)/shard_map/ppermute | solution.py:12
  46.6 134.0 %all-gather.11.cloned.1.call-start = ((), (), s32[]{:S(2)}) async-start(), calls=%async_computation.4 | async-start | bytes 6389760 | tf_op jit(solution)/shard_map/all_gather | solution.py:45
  47.4 171.4 %all-gather.5.cloned.1.call-start = ((), (), s32[]{:S(2)}) async-start(), calls=%async_computation.1 | async-start | bytes 1769472 | tf_op jit(solution)/shard_map/all_gather | solution.py:43
  48.1 262.7 %all-gather.7.cloned.1.call-start = ((), (), s32[]{:S(2)}) async-start(), calls=%async_computation.2 | async-start | bytes 6389760 | tf_op jit(solution)/shard_map/all_gather | solution.py:48
  48.7 308.8 %reduce-scatter.2.cloned.1.call-start = ((), (), s32[]{:S(2)}) async-start(), calls=%async_computation.5 | async-start | bytes 1769472 | tf_op jit(solution)/shard_map/reduce_scatter | solution.py:59
  185.3 198.3 %copy-start.1 = (bf16[192,512]{1,0:T(8,128)(2,1)S(1)}, bf16[192,512]{1,0:T(8,128)(2,1)}, u32[]{:S(2)}) copy-start(bf16[192,512]{1,0:T(8,128)(2,1)} %param.6) | copy-start | bytes 589828
  321.0 3.1 collective-permute-start
  372.2 11.4 %collective-permute-start.5 = (f32[1,512]{1,0:T(1,128)S(1)}, f32[1,512]{1,0:T(1,128)S(1)}, u32[]{:S(2)}, u32[]{:S(2)}) collective-permute-start(f32[1,512]{1,0:T(1,128)S(1)} %constant_dynamic-slice_fusion), channel_id=1, source_target_pairs={{0,8},{8,16},{16,24},{24,32},{32,40},{40,48},{48,56},{56,64},{64,7... | collective-permute-start | bytes 6152 | tf_op jit(solution)/shard_map/ppermute | solution.py:12
Sparse Core Ops, SparseCore 0:
  46.8 41.6 all-gather.8
  91.8 88.7 all-gather.10
  182.7 36.0 all-gather.4
  222.0 88.7 all-gather.6
  321.1 36.3 reduce-scatter.1
where the time goes:
time: 394 us; the launch traced here: 391 us
  waiting for transfers between devices  293 us (74%)
  starting transfers between devices  29.2 us (7%)
  blocking collectives  26.7 us (7%)
  matrix products  17.3 us (4%)
  between operations  17.1 us (4%)
  other arithmetic  6.01 us (2%)
    all_gather x1, waiting for transfers between devices, body(): first_full = lax.all_gather(first_weight, 'seq', axis=0, tiled=True)  92.1 us
    all_gather x1, waiting for transfers between devices, body(): lax.all_gather(second_weight, 'seq', axis=0, tiled=True)  92 us
    all_gather x1, waiting for transfers between devices, body(): lax.all_gather(normed.astype(jnp.bfloat16), 'tp', axis=1, tiled=True)  39.7 us
    all_gather x1, waiting for transfers between devices, body(): lax.all_gather(grad_sums.astype(jnp.bfloat16), 'tp', axis=1, tiled=True)  33.5 us
    reduce_scatter x1, waiting for transfers between devices, body(): lax.psum_scatter(partial_grad.astype(jnp.bfloat16), 'tp', scatter_dimensi...  32.8 us
    ppermute x6, starting transfers between devices, shifted(): return lax.ppermute(shard, axis, pairs)  29.1 us
    psum x1, blocking collectives, body(): square_sums = lax.psum(jnp.sum(pooled * pooled, axis=1), 'tp')  14.4 us
    psum x1, blocking collectives, body(): norm_dot = lax.psum(jnp.sum(norm_grad * normed, axis=1), 'tp')  12.4 us
  transfers between devices with their start and end apart: 11, of which 7 were waited for; matrix products, arithmetic and copies ran while one was open for 2% of the time, Pallas kernels for 0%

commit v1 on v0

v1 whole, which is shorter than its diff:
```python
import jax
import jax.numpy as jnp
from jax import lax
from jax.sharding import PartitionSpec as P

epsilon = 1e-06


def shifted(shard, axis, by):
    count = lax.axis_size(axis)
    pairs = [(i, i + by) for i in range(count) if 0 <= i + by < count]
    return lax.ppermute(shard, axis, pairs)


def turned(shard, by):
    count = lax.axis_size("tp")
    return lax.ppermute(shard, "tp", [(i, (i + by) % count) for i in range(count)])


def ring_gather(block):
    count = lax.axis_size("tp")
    me = lax.axis_index("tp")
    rows, width = block.shape
    whole = jnp.zeros((rows, width * count), block.dtype)

    def put(whole, part, row, owner):
        return lax.dynamic_update_slice(whole, part, (row, lax.rem(owner + count, count) * width))

    whole = put(whole, block, 0, me)
    right = left = block
    for step in range(1, count // 2):
        right, left = turned(right, 1), turned(left, -1)
        whole = put(whole, right, 0, me - step)
        whole = put(whole, left, 0, me + step)
    half = rows // 2
    top, bottom = turned(right[:half], 1), turned(left[half:], -1)
    whole = put(whole, top, 0, me + count // 2)
    return put(whole, bottom, half, me + count // 2)


def body(byte_acts, upstream, segment_ids, first_weight, second_weight):
    byte_rows = segment_ids.shape[0]
    width = byte_acts.shape[1]
    hidden = first_weight.shape[1]
    model_width = width * lax.axis_size("tp")
    weights = lax.all_gather(
        jnp.concatenate([first_weight, second_weight], axis=1), "seq", axis=0, tiled=True
    )
    first_full, second_full = weights[:, :hidden], weights[:, hidden:]

    base_id = segment_ids[0]
    last_id = segment_ids[byte_rows - 1]
    slot_of = segment_ids - base_id
    slot_index = jnp.arange(byte_rows, dtype=jnp.int32)
    member = slot_index[:, None] == slot_of[None, :]
    member_b = member.astype(jnp.bfloat16)
    seg_sums = jnp.dot(member_b, byte_acts, preferred_element_type=jnp.float32)
    grad_sums = jnp.dot(member_b, upstream, preferred_element_type=jnp.float32)
    counts = jnp.sum(member.astype(jnp.float32), axis=1)

    last_slot = last_id - base_id

    def packed(slot, segment):
        at = lambda a: lax.dynamic_slice_in_dim(a, slot, 1, 0)
        tag = jnp.zeros((1, 128), jnp.float32) + (segment + 1).astype(jnp.float32)
        count = jnp.zeros((1, 128), jnp.float32) + at(counts)
        return jnp.concatenate([at(seg_sums), at(grad_sums), count, tag], axis=1)

    tail = shifted(packed(0, base_id), "seq", -1)
    head = shifted(packed(last_slot, last_id), "seq", 1)

    def pick(slot, segment, row):
        matched = row[0, 2 * width + 128] == (segment + 1).astype(jnp.float32)
        return ((slot_index == slot) & matched).astype(jnp.float32)

    tail_pick, head_pick = pick(last_slot, last_id, tail), pick(0, base_id, head)

    def joined(own, begin, end):
        return (
            own
            + tail_pick[:, None] * tail[:, begin:end]
            + head_pick[:, None] * head[:, begin:end]
        )

    seg_sums = joined(seg_sums, 0, width)
    grad_sums = joined(grad_sums, width, 2 * width)
    counts = counts + tail_pick * tail[0, 2 * width] + head_pick * head[0, 2 * width]
    safe_counts = jnp.maximum(counts, 1.0)
    pooled = seg_sums / safe_counts[:, None]

    gathered = ring_gather(
        jnp.concatenate([pooled.astype(jnp.bfloat16), grad_sums.astype(jnp.bfloat16)], axis=0)
    )
    pooled_b, grad_b = gathered[:byte_rows], gathered[byte_rows:]
    square_sums = jnp.sum(jnp.square(pooled_b.astype(jnp.float32)), axis=1)
    inv_rms = lax.rsqrt(square_sums / model_width + epsilon)[:, None]

    back_proj = jnp.dot(grad_b, second_full, preferred_element_type=jnp.float32)
    up_proj = inv_rms * jnp.dot(pooled_b, first_full, preferred_element_type=jnp.float32)
    sigmoid_up = jax.nn.sigmoid(up_proj)
    grad_hidden = (back_proj * sigmoid_up * (1.0 + up_proj * (1.0 - sigmoid_up))).astype(
        jnp.bfloat16
    )
    norm_dot = lax.psum(jnp.sum(grad_hidden.astype(jnp.float32) * up_proj, axis=1), "tp")
    partial_grad = lax.dot_general(
        grad_hidden, first_full, (((1,), (1,)), ((), ())), preferred_element_type=jnp.float32
    )
    norm_grad = lax.psum_scatter(
        partial_grad.astype(jnp.bfloat16), "tp", scatter_dimension=1, tiled=True
    ).astype(jnp.float32)
    normed = pooled * inv_rms
    pooled_grad = grad_sums + inv_rms * (
        norm_grad - normed * (norm_dot / model_width)[:, None]
    )
    byte_share = pooled_grad / safe_counts[:, None]
    spread = jnp.dot(
        member.astype(jnp.float32).T,
        byte_share,
        precision=lax.Precision.HIGHEST,
        preferred_element_type=jnp.float32,
    )
    return (upstream.astype(jnp.float32) + spread).astype(jnp.bfloat16)


def solution(mesh):
    return jax.shard_map(
        body,
        mesh=mesh,
        in_specs=(P("seq", "tp"), P("seq", "tp"), P("seq"), P("seq", "tp"), P("seq", "tp")),
        out_specs=P("seq", "tp"),
        check_vma=False,
    )
```

time: 394 us -> 174 us (0.44)
  the two profiles are of different devices: /device:TPU:1 before, /device:TPU:4 now
where the time goes in v1:
time: 174 us; the launch traced here: 173 us
  waiting for transfers between devices  68.6 us (39%)
  starting transfers between devices  38.4 us (22%)
  blocking collectives  18.1 us (10%)
  between operations  17.8 us (10%)
  matrix products  16 us (9%)
  local copies, waits for them, and re-layouts  9.14 us (5%)
  other arithmetic  5.09 us (3%)
    ppermute x8, starting transfers between devices, turned(): lax.ppermute(shard, 'tp', [(i, (i + by) % count) for i in range(count)])  34 us
    reduce_scatter x1, waiting for transfers between devices, body(): lax.psum_scatter(partial_grad.astype(jnp.bfloat16), 'tp', scatter_dimensi...  24.8 us
    all_gather x1, waiting for transfers between devices, body(): lax.all_gather(jnp.concatenate([first_weight, second_weight], axis=1), 's...  24.6 us
    psum x1, blocking collectives, body(): lax.psum(jnp.sum(grad_hidden.astype(jnp.float32) * up_proj, axis=1), 'tp')  18.1 us
    ppermute x8, waiting for transfers between devices, turned(): lax.ppermute(shard, 'tp', [(i, (i + by) % count) for i in range(count)])  17.8 us
    dot_general x1, matrix products, body(): back_proj = jnp.dot(grad_b, second_full, preferred_element_type=jnp.float32)  4.49 us
    dynamic_update_slice x8, local copies, waits for them, and re-layouts, put(): lax.dynamic_update_slice(whole, part, (row, lax.rem(owner + count, count)...  4.33 us
    ppermute x2, starting transfers between devices, shifted(): return lax.ppermute(shard, axis, pairs)  4.33 us
  transfers between devices with their start and end apart: 12, of which 8 were waited for; matrix products, arithmetic and copies ran while one was open for 8% of the time, Pallas kernels for 0%

profile of v1, /device:TPU:4, one launch (start us, length us, event | category | flops | bytes accessed | tf_op | source)
XLA Modules:
  0.0 173.1 jit_solution(1000372698193034194)
XLA Ops:
  6.5 1.7 pad_maximum_fusion.1
  8.3 1.4 fusion.62
  11.6 1.4 broadcast_subtract_fusion
  14.6 1.3 fusion.48
  16.0 1.9 %collective-permute-start = (f32[1,1280]{1,0:T(1,128)S(1)}, f32[1,1280]{1,0:T(1,128)S(1)}, u32[]{:S(2)}, u32[]{:S(2)}) collective-permute-start(f32[1,1280]{1,0:T(1,128)S(1)} %reshape_maximum_fusion.2), channel_id=1, source_target_pairs={{8,0},{16,8},{24,16},{32,24},{40,32},{48,40},{56,48},{64,56},{72,6... | collective-permute-start | bytes 15368 | tf_op jit(solution)/shard_map/ppermute | solution.py:12
  19.2 2.4 %collective-permute-start.1 = (f32[1,1280]{1,0:T(1,128)S(1)}, f32[1,1280]{1,0:T(1,128)S(1)}, u32[]{:S(2)}, u32[]{:S(2)}) collective-permute-start(f32[1,1280]{1,0:T(1,128)S(1)} %reshape_maximum_fusion), channel_id=1, source_target_pairs={{0,8},{8,16},{16,24},{24,32},{32,40},{40,48},{48,56},{56,64},{64,7... | collective-permute-start | bytes 15368 | tf_op jit(solution)/shard_map/ppermute | solution.py:12
  22.7 1.4 collective-permute-done.1
  25.4 1.2 add_maximum_fusion
  27.4 4.3 %collective-permute-start.2 = (bf16[384,512]{1,0:T(8,128)(2,1)S(1)}, bf16[384,512]{1,0:T(8,128)(2,1)}, u32[]{:S(2)}, u32[]{:S(2)}) collective-permute-start(bf16[384,512]{1,0:T(8,128)(2,1)S(1)} %get-tuple-element.5), channel_id=1, source_target_pairs={{0,1},{1,2},{2,3},{3,4},{4,5},{5,6},{6,7},{7,0},{8,9},{9,10},{10,1... | collective-permute-start | bytes 1179656 | tf_op jit(solution)/shard_map/ppermute | solution.py:17
  31.6 8.6 %collective-permute-start.3 = (bf16[384,512]{1,0:T(8,128)(2,1)S(1)}, bf16[384,512]{1,0:T(8,128)(2,1)}, u32[]{:S(2)}, u32[]{:S(2)}) collective-permute-start(bf16[384,512]{1,0:T(8,128)(2,1)S(1)} %get-tuple-element.5), channel_id=1, source_target_pairs={{0,7},{1,0},{2,1},{3,2},{4,3},{5,4},{6,5},{7,6},{8,15},{9,8},{10,9... | collective-permute-start | bytes 1179656 | tf_op jit(solution)/shard_map/ppermute | solution.py:17
  40.2 7.1 %collective-permute-done.2 = bf16[384,512]{1,0:T(8,128)(2,1)} collective-permute-done((bf16[384,512]{1,0:T(8,128)(2,1)S(1)}, bf16[384,512]{1,0:T(8,128)(2,1)}, u32[]{:S(2)}, u32[]{:S(2)}) %collective-permute-start.2) | collective-permute-done | bytes 393248 | tf_op jit(solution)/shard_map/ppermute | solution.py:17
  47.4 1.9 %collective-permute-start.4 = (bf16[384,512]{1,0:T(8,128)(2,1)}, bf16[384,512]{1,0:T(8,128)(2,1)}, u32[]{:S(2)}, u32[]{:S(2)}) collective-permute-start(bf16[384,512]{1,0:T(8,128)(2,1)} %collective-permute-done.2), channel_id=1, source_target_pairs={{0,1},{1,2},{2,3},{3,4},{4,5},{5,6},{6,7},{7,0},{8,9},{9,10},{10,1... | collective-permute-start | bytes 1179656 | tf_op jit(solution)/shard_map/ppermute | solution.py:17
  49.3 5.1 %collective-permute-start.5 = (bf16[384,512]{1,0:T(8,128)(2,1)}, bf16[384,512]{1,0:T(8,128)(2,1)}, u32[]{:S(2)}, u32[]{:S(2)}) collective-permute-start(bf16[384,512]{1,0:T(8,128)(2,1)} %collective-permute-done.3), channel_id=1, source_target_pairs={{0,7},{1,0},{2,1},{3,2},{4,3},{5,4},{6,5},{7,6},{8,15},{9,8},{10,9... | collective-permute-start | bytes 1179656 | tf_op jit(solution)/shard_map/ppermute | solution.py:17
  54.5 6.4 %collective-permute-done.4 = bf16[384,512]{1,0:T(8,128)(2,1)} collective-permute-done((bf16[384,512]{1,0:T(8,128)(2,1)}, bf16[384,512]{1,0:T(8,128)(2,1)}, u32[]{:S(2)}, u32[]{:S(2)}) %collective-permute-start.4) | collective-permute-done | bytes 393248 | tf_op jit(solution)/shard_map/ppermute | solution.py:17
  60.9 1.9 %collective-permute-start.6 = (bf16[384,512]{1,0:T(8,128)(2,1)}, bf16[384,512]{1,0:T(8,128)(2,1)S(1)}, u32[]{:S(2)}, u32[]{:S(2)}) collective-permute-start(bf16[384,512]{1,0:T(8,128)(2,1)} %collective-permute-done.4), channel_id=1, source_target_pairs={{0,1},{1,2},{2,3},{3,4},{4,5},{5,6},{6,7},{7,0},{8,9},{9,10},{10,1... | collective-permute-start | bytes 1179656 | tf_op jit(solution)/shard_map/ppermute | solution.py:17
  62.9 5.1 %collective-permute-start.7 = (bf16[384,512]{1,0:T(8,128)(2,1)}, bf16[384,512]{1,0:T(8,128)(2,1)S(1)}, u32[]{:S(2)}, u32[]{:S(2)}) collective-permute-start(bf16[384,512]{1,0:T(8,128)(2,1)} %collective-permute-done.5), channel_id=1, source_target_pairs={{0,7},{1,0},{2,1},{3,2},{4,3},{5,4},{6,5},{7,6},{8,15},{9,8},{10,9... | collective-permute-start | bytes 1179656 | tf_op jit(solution)/shard_map/ppermute | solution.py:17
  68.0 1.0 constant_dynamic-update-slice_fusion.6
  69.0 1.0 constant_dynamic-update-slice_fusion.5
  70.1 1.0 constant_dynamic-update-slice_fusion.4
  71.2 1.1 constant_dynamic-update-slice_fusion.3
  72.2 1.2 collective-permute-done.6
  73.5 1.9 %collective-permute-start.8 = (bf16[192,512]{1,0:T(8,128)(2,1)S(1)}, bf16[192,512]{1,0:T(8,128)(2,1)S(1)}, u32[]{:S(2)}, u32[]{:S(2)}) collective-permute-start(bf16[192,512]{1,0:T(8,128)(2,1)S(1)} %slice.72), channel_id=1, source_target_pairs={{0,1},{1,2},{2,3},{3,4},{4,5},{5,6},{6,7},{7,0},{8,9},{9,10},{10,1... | collective-permute-start | bytes 589832 | tf_op jit(solution)/shard_map/ppermute | solution.py:17
  75.4 5.1 %collective-permute-start.9 = (bf16[192,512]{1,0:T(8,128)(2,1)S(1)}, bf16[192,512]{1,0:T(8,128)(2,1)S(1)}, u32[]{:S(2)}, u32[]{:S(2)}) collective-permute-start(bf16[192,512]{1,0:T(8,128)(2,1)S(1)} %slice.73), channel_id=1, source_target_pairs={{0,7},{1,0},{2,1},{3,2},{4,3},{5,4},{6,5},{7,6},{8,15},{9,8},{10,9... | collective-permute-start | bytes 589832 | tf_op jit(solution)/shard_map/ppermute | solution.py:17
  80.7 1.6 collective-permute-done.8
  82.3 1.5 collective-permute-done.9
  84.2 24.6 %all-gather.2.cloned.1.call-done = bf16[4096,1536]{1,0:T(8,128)(2,1)} async-done(((bf16[64,1536]{1,0:T(8,128)(2,1)}), bf16[4096,1536]{1,0:T(8,128)(2,1)}) %all-gather.2.cloned.1.call-update) | async-done | bytes 12582928 | tf_op jit(solution)/shard_map/all_gather | solution.py:46
  108.7 4.3 %fusion.11 = f32[192,768]{1,0:T(8,128)S(1)} fusion(bf16[4096,1536]{1,0:T(8,128)(2,1)} %all-gather.2.cloned.1.call-done, bf16[384,4096]{1,0:T(8,128)(2,1)S(1)} %constant_dynamic-update-slice_fusion.8, f32[192]{0:T(256)S(1)} %add_rsqrt_fusion), kind=kOutput, calls=%fused_computation.10 | convolution fusion | flops 1208107008 | bytes 8455168 | tf_op jit(solution)/shard_map/dot_general | solution.py:99
  113.1 4.5 %multiply_reduce_fusion.1 = (f32[192]{0:T(256)S(1)}, bf16[192,768]{1,0:T(8,128)(2,1)S(1)}) fusion(f32[192,768]{1,0:T(8,128)S(1)} %fusion.11, bf16[4096,1536]{1,0:T(8,128)(2,1)} %all-gather.2.cloned.1.call-done, bf16[384,4096]{1,0:T(8,128)(2,1)S(1)} %constant_dynamic-update-slice_fusion.8), kind=kOutput, calls=%fused_computation.16 | convolution fusion | flops 1209728768 | bytes 8749824 | tf_op jit(solution)/shard_map/dot_general | solution.py:98
  117.6 3.3 %fusion.6 = bf16[192,4096]{1,0:T(8,128)(2,1)} fusion(bf16[192,768]{1,0:T(8,128)(2,1)S(1)} %get-tuple-element.26, bf16[4096,1536]{1,0:T(8,128)(2,1)S(1)} %bitcast.24), kind=kOutput, calls=%fused_computation.6 | convolution fusion | flops 1208745984 | bytes 8159232 | tf_op jit(solution)/shard_map/dot_general | solution.py:105
  121.0 18.1 %psum.7 = f32[192]{0:T(256)S(1)} all-reduce(f32[192]{0:T(256)S(1)} %get-tuple-element.25), channel_id=1, replica_groups=mesh['seq'=64,'tp'=8] {'tp'}, use_global_device_ids=true, to_apply=%region_4.0 | all-reduce | flops 192 | bytes 1536 | tf_op jit(solution)/shard_map/psum | solution.py:104
  139.1 24.8 %reduce-scatter.2.cloned.1.call-done = bf16[192,512]{1,0:T(8,128)(2,1)} async-done(((bf16[192,4096]{1,0:T(8,128)(2,1)}), bf16[192,512]{1,0:T(8,128)(2,1)}) %reduce-scatter.2.cloned.1.call-update) | async-done | bytes 196624 | tf_op jit(solution)/shard_map/reduce_scatter | solution.py:108
  163.9 2.3 %fusion.31 = bf16[192,512]{1,0:T(8,128)(2,1)} fusion(bf16[192,512]{1,0:T(8,128)(2,1)} %reduce-scatter.2.cloned.1.call-done, bf16[192,512]{1,0:T(8,128)(2,1)S(1)} %copy-done.5, f32[192,512]{1,0:T(8,128)S(1)} %copy-done.4, f32[192]{0:T(256)S(1)} %broadcast_multiply_fusion, f32[192]{0:T(256)S(1)} %add_rsqrt_fusion, f32[192]{0:T(256)S(1)} %add_maximum_fusion, ...), kind=kOutput, calls=%fused_computation.15 | convolution fusion | flops 228397056 | bytes 1389056 | tf_op jit(solution)/shard_map/dot_general | solution.py:116
  (59 shorter events, 4.7 us)
Async XLA Ops:
  6.5 7.9 %copy-start = (bf16[192,512]{1,0:T(8,128)(2,1)S(1)}, bf16[192,512]{1,0:T(8,128)(2,1)}, u32[]{:S(2)}) copy-start(bf16[192,512]{1,0:T(8,128)(2,1)} %param.5) | copy-start | bytes 589828
  6.5 102.2 %all-gather.2.cloned.1.call-start = ((), (), s32[]{:S(2)}) async-start(), calls=%async_computation.1 | async-start | bytes 12779520 | tf_op jit(solution)/shard_map/all_gather | solution.py:46
  8.2 155.7 %reduce-scatter.2.cloned.1.call-start = ((), (), s32[]{:S(2)}) async-start(), calls=%async_computation.2 | async-start | bytes 1769472 | tf_op jit(solution)/shard_map/reduce_scatter | solution.py:108
  14.6 12.3 %copy-start.1 = (f32[192,512]{1,0:T(8,128)}, f32[192,512]{1,0:T(8,128)S(1)}, u32[]{:S(2)}) copy-start(f32[192,512]{1,0:T(8,128)S(1)} %fusion.47) | copy-start | bytes 1179652
  15.9 11.0 %copy-start.3 = (f32[192,512]{1,0:T(8,128)}, f32[192,512]{1,0:T(8,128)S(1)}, u32[]{:S(2)}) copy-start(f32[192,512]{1,0:T(8,128)S(1)} %fusion.48) | copy-start | bytes 1179652
  16.0 5.6 %collective-permute-start = (f32[1,1280]{1,0:T(1,128)S(1)}, f32[1,1280]{1,0:T(1,128)S(1)}, u32[]{:S(2)}, u32[]{:S(2)}) collective-permute-start(f32[1,1280]{1,0:T(1,128)S(1)} %reshape_maximum_fusion.2), channel_id=1, source_target_pairs={{8,0},{16,8},{24,16},{32,24},{40,32},{48,40},{56,48},{64,56},{72,6... | collective-permute-start | bytes 15368 | tf_op jit(solution)/shard_map/ppermute | solution.py:12
  19.2 4.9 %collective-permute-start.1 = (f32[1,1280]{1,0:T(1,128)S(1)}, f32[1,1280]{1,0:T(1,128)S(1)}, u32[]{:S(2)}, u32[]{:S(2)}) collective-permute-start(f32[1,1280]{1,0:T(1,128)S(1)} %reshape_maximum_fusion), channel_id=1, source_target_pairs={{0,8},{8,16},{16,24},{24,32},{32,40},{40,48},{48,56},{56,64},{64,7... | collective-permute-start | bytes 15368 | tf_op jit(solution)/shard_map/ppermute | solution.py:12
  27.4 20.0 %collective-permute-start.2 = (bf16[384,512]{1,0:T(8,128)(2,1)S(1)}, bf16[384,512]{1,0:T(8,128)(2,1)}, u32[]{:S(2)}, u32[]{:S(2)}) collective-permute-start(bf16[384,512]{1,0:T(8,128)(2,1)S(1)} %get-tuple-element.5), channel_id=1, source_target_pairs={{0,1},{1,2},{2,3},{3,4},{4,5},{5,6},{6,7},{7,0},{8,9},{9,10},{10,1... | collective-permute-start | bytes 1179656 | tf_op jit(solution)/shard_map/ppermute | solution.py:17
  31.6 17.7 %collective-permute-start.3 = (bf16[384,512]{1,0:T(8,128)(2,1)S(1)}, bf16[384,512]{1,0:T(8,128)(2,1)}, u32[]{:S(2)}, u32[]{:S(2)}) collective-permute-start(bf16[384,512]{1,0:T(8,128)(2,1)S(1)} %get-tuple-element.5), channel_id=1, source_target_pairs={{0,7},{1,0},{2,1},{3,2},{4,3},{5,4},{6,5},{7,6},{8,15},{9,8},{10,9... | collective-permute-start | bytes 1179656 | tf_op jit(solution)/shard_map/ppermute | solution.py:17
  47.4 13.6 %collective-permute-start.4 = (bf16[384,512]{1,0:T(8,128)(2,1)}, bf16[384,512]{1,0:T(8,128)(2,1)}, u32[]{:S(2)}, u32[]{:S(2)}) collective-permute-start(bf16[384,512]{1,0:T(8,128)(2,1)} %collective-permute-done.2), channel_id=1, source_target_pairs={{0,1},{1,2},{2,3},{3,4},{4,5},{5,6},{6,7},{7,0},{8,9},{9,10},{10,1... | collective-permute-start | bytes 1179656 | tf_op jit(solution)/shard_map/ppermute | solution.py:17
  49.3 13.5 %collective-permute-start.5 = (bf16[384,512]{1,0:T(8,128)(2,1)}, bf16[384,512]{1,0:T(8,128)(2,1)}, u32[]{:S(2)}, u32[]{:S(2)}) collective-permute-start(bf16[384,512]{1,0:T(8,128)(2,1)} %collective-permute-done.3), channel_id=1, source_target_pairs={{0,7},{1,0},{2,1},{3,2},{4,3},{5,4},{6,5},{7,6},{8,15},{9,8},{10,9... | collective-permute-start | bytes 1179656 | tf_op jit(solution)/shard_map/ppermute | solution.py:17
  60.9 12.5 %collective-permute-start.6 = (bf16[384,512]{1,0:T(8,128)(2,1)}, bf16[384,512]{1,0:T(8,128)(2,1)S(1)}, u32[]{:S(2)}, u32[]{:S(2)}) collective-permute-start(bf16[384,512]{1,0:T(8,128)(2,1)} %collective-permute-done.4), channel_id=1, source_target_pairs={{0,1},{1,2},{2,3},{3,4},{4,5},{5,6},{6,7},{7,0},{8,9},{9,10},{10,1... | collective-permute-start | bytes 1179656 | tf_op jit(solution)/shard_map/ppermute | solution.py:17
  62.9 12.5 %collective-permute-start.7 = (bf16[384,512]{1,0:T(8,128)(2,1)}, bf16[384,512]{1,0:T(8,128)(2,1)S(1)}, u32[]{:S(2)}, u32[]{:S(2)}) collective-permute-start(bf16[384,512]{1,0:T(8,128)(2,1)} %collective-permute-done.5), channel_id=1, source_target_pairs={{0,7},{1,0},{2,1},{3,2},{4,3},{5,4},{6,5},{7,6},{8,15},{9,8},{10,9... | collective-permute-start | bytes 1179656 | tf_op jit(solution)/shard_map/ppermute | solution.py:17
  73.5 8.8 %collective-permute-start.8 = (bf16[192,512]{1,0:T(8,128)(2,1)S(1)}, bf16[192,512]{1,0:T(8,128)(2,1)S(1)}, u32[]{:S(2)}, u32[]{:S(2)}) collective-permute-start(bf16[192,512]{1,0:T(8,128)(2,1)S(1)} %slice.72), channel_id=1, source_target_pairs={{0,1},{1,2},{2,3},{3,4},{4,5},{5,6},{6,7},{7,0},{8,9},{9,10},{10,1... | collective-permute-start | bytes 589832 | tf_op jit(solution)/shard_map/ppermute | solution.py:17
  75.4 8.3 %collective-permute-start.9 = (bf16[192,512]{1,0:T(8,128)(2,1)S(1)}, bf16[192,512]{1,0:T(8,128)(2,1)S(1)}, u32[]{:S(2)}, u32[]{:S(2)}) collective-permute-start(bf16[192,512]{1,0:T(8,128)(2,1)S(1)} %slice.73), channel_id=1, source_target_pairs={{0,7},{1,0},{2,1},{3,2},{4,3},{5,4},{6,5},{7,6},{8,15},{9,8},{10,9... | collective-permute-start | bytes 589832 | tf_op jit(solution)/shard_map/ppermute | solution.py:17
  108.7 8.8 %slice-start = ((s8[12582912]{0:T(1024)(128)(4,1)}), s8[4194304]{0:T(1024)(128)(4,1)S(1)}, s32[]{:S(2)}) async-start(s8[12582912]{0:T(1024)(128)(4,1)} %bitcast.23), calls=%async_computation.3 | async-start | bytes 8388608
  108.7 8.8 %slice-start.1 = ((s8[12582912]{0:T(1024)(128)(4,1)}), s8[4194304]{0:T(1024)(128)(4,1)S(1)}, s32[]{:S(2)}) async-start(s8[12582912]{0:T(1024)(128)(4,1)} %bitcast.23), calls=%async_computation.4 | async-start | bytes 8388608
  113.1 4.5 %slice-start.2 = ((s8[12582912]{0:T(1024)(128)(4,1)}), s8[4194304]{0:T(1024)(128)(4,1)S(1)}, s32[]{:S(2)}) async-start(s8[12582912]{0:T(1024)(128)(4,1)} %bitcast.23), calls=%async_computation.5 | async-start | bytes 8388608
  117.6 46.3 %copy-start.2 = (f32[192,512]{1,0:T(8,128)S(1)}, f32[192,512]{1,0:T(8,128)}, u32[]{:S(2)}) copy-start(f32[192,512]{1,0:T(8,128)} %copy-done.1) | copy-start | bytes 1179652
  117.6 46.3 %copy-start.4 = (f32[192,512]{1,0:T(8,128)S(1)}, f32[192,512]{1,0:T(8,128)}, u32[]{:S(2)}) copy-start(f32[192,512]{1,0:T(8,128)} %copy-done.3) | copy-start | bytes 1179652
  117.6 46.3 %copy-start.5 = (bf16[192,512]{1,0:T(8,128)(2,1)S(1)}, bf16[192,512]{1,0:T(8,128)(2,1)}, u32[]{:S(2)}) copy-start(bf16[192,512]{1,0:T(8,128)(2,1)} %param.6) | copy-start | bytes 589828
Sparse Core Ops, SparseCore 0:
  10.7 97.9 all-gather.1
  121.1 42.7 reduce-scatter.1

commit v2 on v1

--- a/solution.py
+++ b/solution.py
@@ -1,6 +1,8 @@
 import jax
 import jax.numpy as jnp
 from jax import lax
+from jax.experimental import pallas as pl
+from jax.experimental.pallas import tpu as pltpu
 from jax.sharding import PartitionSpec as P
 
 epsilon = 1e-06
@@ -38,16 +40,85 @@
     return put(whole, bottom, half, me + count // 2)
 
 
+def block_kernel(acts_ref, weights_ref, inv_rms_ref, out_ref, up_ref, back_ref, first_ref):
+    step, steps = pl.program_id(0), pl.num_programs(0)
+    rows, hidden = up_ref.shape
+
+    @pl.when(step == 0)
+    def _():
+        up_ref[...] = jnp.zeros_like(up_ref)
+        back_ref[...] = jnp.zeros_like(back_ref)
+
+    first_ref[step] = weights_ref[:, :hidden]
+    up_ref[...] += jnp.dot(
+        acts_ref[:rows], weights_ref[:, :hidden], preferred_element_type=jnp.float32
+    )
+    back_ref[...] += jnp.dot(
+        acts_ref[rows:], weights_ref[:, hidden:], preferred_element_type=jnp.float32
+    )
+
+    @pl.when(step == steps - 1)
+    def _():
+        up_proj = up_ref[...] * inv_rms_ref[...]
+        sigmoid_up = jax.nn.sigmoid(up_proj)
+        grad_hidden = (
+            back_ref[...] * sigmoid_up * (1.0 + up_proj * (1.0 - sigmoid_up))
+        ).astype(jnp.bfloat16)
+        dots = lax.dot_general(
+            jnp.ones((8, hidden), jnp.float32),
+            grad_hidden.astype(jnp.float32) * up_proj,
+            (((1,), (1,)), ((), ())),
+            precision=lax.Precision.HIGHEST,
+            preferred_element_type=jnp.float32,
+        )
+        high = dots.astype(jnp.bfloat16).astype(jnp.float32)
+        extra = jnp.concatenate([high, dots - high], axis=0).astype(jnp.bfloat16)
+        for block in range(out_ref.shape[0]):
+            out_ref[block, :rows] = lax.dot_general(
+                grad_hidden,
+                first_ref[block],
+                (((1,), (1,)), ((), ())),
+                preferred_element_type=jnp.float32,
+            ).astype(jnp.bfloat16)
+            out_ref[block, rows:] = jnp.zeros((16, out_ref.shape[2]), jnp.bfloat16)
+            out_ref[block, rows:, :rows] = extra
+
+
+def block_terms(gathered, weights, inv_rms, width):
+    rows, depth = gathered.shape[0] // 2, gathered.shape[1]
+    hidden = weights.shape[1] // 2
+    steps = depth // width
+    return pl.pallas_call(
+        block_kernel,
+        grid=(steps,),
+        in_specs=[
+            pl.BlockSpec((2 * rows, width), lambda k: (0, k)),
+            pl.BlockSpec((width, 2 * hidden), lambda k: (k, 0)),
+            pl.BlockSpec((rows, 1), lambda k: (0, 0)),
+        ],
+        out_specs=pl.BlockSpec((steps, rows + 16, width), lambda k: (0, 0, 0)),
+        out_shape=jax.ShapeDtypeStruct((steps, rows + 16, width), jnp.bfloat16),
+        scratch_shapes=[
+            pltpu.VMEM((rows, hidden), jnp.float32),
+            pltpu.VMEM((rows, hidden), jnp.float32),
+            pltpu.VMEM((steps, width, hidden), jnp.bfloat16),
+        ],
+        compiler_params=pltpu.CompilerParams(vmem_limit_bytes=40 * 1024 * 1024),
+        cost_estimate=pl.CostEstimate(
+            flops=6 * rows * depth * hidden,
+            bytes_accessed=2 * (2 * rows * depth + 2 * depth * hidden + rows * depth),
+            transcendentals=rows * hidden,
+        ),
+    )(gathered, weights, inv_rms)
+
+
 def body(byte_acts, upstream, segment_ids, first_weight, second_weight):
     byte_rows = segment_ids.shape[0]
     width = byte_acts.shape[1]
-    hidden = first_weight.shape[1]
     model_width = width * lax.axis_size("tp")
     weights = lax.all_gather(
         jnp.concatenate([first_weight, second_weight], axis=1), "seq", axis=0, tiled=True
     )
-    first_full, second_full = weights[:, :hidden], weights[:, hidden:]
-
     base_id = segment_ids[0]
     last_id = segment_ids[byte_rows - 1]
     slot_of = segment_ids - base_id
@@ -91,23 +162,14 @@
     gathered = ring_gather(
         jnp.concatenate([pooled.astype(jnp.bfloat16), grad_sums.astype(jnp.bfloat16)], axis=0)
     )
-    pooled_b, grad_b = gathered[:byte_rows], gathered[byte_rows:]
+    pooled_b = gathered[:byte_rows]
     square_sums = jnp.sum(jnp.square(pooled_b.astype(jnp.float32)), axis=1)
     inv_rms = lax.rsqrt(square_sums / model_width + epsilon)[:, None]
 
-    back_proj = jnp.dot(grad_b, second_full, preferred_element_type=jnp.float32)
-    up_proj = inv_rms * jnp.dot(pooled_b, first_full, preferred_element_type=jnp.float32)
-    sigmoid_up = jax.nn.sigmoid(up_proj)
-    grad_hidden = (back_proj * sigmoid_up * (1.0 + up_proj * (1.0 - sigmoid_up))).astype(
-        jnp.bfloat16
-    )
-    norm_dot = lax.psum(jnp.sum(grad_hidden.astype(jnp.float32) * up_proj, axis=1), "tp")
-    partial_grad = lax.dot_general(
-        grad_hidden, first_full, (((1,), (1,)), ((), ())), preferred_element_type=jnp.float32
-    )
-    norm_grad = lax.psum_scatter(
-        partial_grad.astype(jnp.bfloat16), "tp", scatter_dimension=1, tiled=True
-    ).astype(jnp.float32)
+    sent = block_terms(gathered, weights, inv_rms, width)
+    terms = lax.all_to_all(sent, "tp", split_axis=0, concat_axis=0, tiled=True).astype(jnp.float32)
+    norm_grad = jnp.sum(terms[:, :byte_rows], axis=0)
+    norm_dot = jnp.sum(terms[:, byte_rows, :byte_rows] + terms[:, byte_rows + 8, :byte_rows], axis=0)
     normed = pooled * inv_rms
     pooled_grad = grad_sums + inv_rms * (
         norm_grad - normed * (norm_dot / model_width)[:, None]

time: 174 us -> 182 us (1.046)
  the two profiles are of different devices: /device:TPU:4 before, /device:TPU:1 now
where the time goes in v2:
time: 182 us
  blocking collectives  49.2 us (27%)
  waiting for transfers between devices  45 us (25%)
  starting transfers between devices  40.4 us (22%)
  between operations  17.5 us (10%)
  Pallas kernels  11.5 us (6%)
  local copies, waits for them, and re-layouts  9.42 us (5%)
  other arithmetic  5.83 us (3%)
  matrix products  2.87 us (2%)
    all_to_all x1, blocking collectives, body(): lax.all_to_all(sent, 'tp', split_axis=0, concat_axis=0, tiled=True)  49.2 us
    ppermute x8, starting transfers between devices, turned(): lax.ppermute(shard, 'tp', [(i, (i + by) % count) for i in range(count)])  29.6 us
    all_gather x1, waiting for transfers between devices, body(): lax.all_gather(jnp.concatenate([first_weight, second_weight], axis=1), 's...  27.3 us
    ppermute x8, waiting for transfers between devices, turned(): lax.ppermute(shard, 'tp', [(i, (i + by) % count) for i in range(count)])  17.6 us
    pallas_call x1, Pallas kernels, block_terms(): pl.pallas_call(block_kernel, grid=(steps,), in_specs=[pl.BlockSpec((2 * r...  11.5 us
    ppermute x2, starting transfers between devices, shifted(): return lax.ppermute(shard, axis, pairs)  10.7 us
    dynamic_update_slice x8, local copies, waits for them, and re-layouts, put(): lax.dynamic_update_slice(whole, part, (row, lax.rem(owner + count, count)...  4.38 us
  transfers between devices with their start and end apart: 11, of which 7 were waited for; matrix products, arithmetic and copies ran while one was open for 8% of the time, Pallas kernels for 0%

profile of v2, /device:TPU:1, one launch (start us, length us, event | category | flops | bytes accessed | tf_op | source)
XLA Modules:
  0.0 181.6 jit_solution(8301420705874288583)
XLA Ops:
  6.5 1.7 pad_maximum_fusion.1
  8.2 1.3 fusion.31
  11.4 1.3 broadcast_subtract_fusion
  12.8 0.6 fusion.30
  13.4 0.6 add.157
  14.3 1.3 fusion.16
  15.7 8.8 %collective-permute-start = (f32[1,1280]{1,0:T(1,128)S(1)}, f32[1,1280]{1,0:T(1,128)S(1)}, u32[]{:S(2)}, u32[]{:S(2)}) collective-permute-start(f32[1,1280]{1,0:T(1,128)S(1)} %reshape_maximum_fusion.2), channel_id=1, source_target_pairs={{8,0},{16,8},{24,16},{32,24},{40,32},{48,40},{56,48},{64,56},{72,6... | collective-permute-start | bytes 15368 | tf_op jit(solution)/shard_map/ppermute | solution.py:14
  25.0 0.6 add.164
  25.7 1.9 %collective-permute-start.1 = (f32[1,1280]{1,0:T(1,128)S(1)}, f32[1,1280]{1,0:T(1,128)S(1)}, u32[]{:S(2)}, u32[]{:S(2)}) collective-permute-start(f32[1,1280]{1,0:T(1,128)S(1)} %reshape_maximum_fusion), channel_id=1, source_target_pairs={{0,8},{8,16},{16,24},{24,32},{32,40},{40,48},{48,56},{56,64},{64,7... | collective-permute-start | bytes 15368 | tf_op jit(solution)/shard_map/ppermute | solution.py:14
  28.7 0.5 fusion.29
  29.9 1.1 add_maximum_fusion
  31.8 1.9 %collective-permute-start.2 = (bf16[384,512]{1,0:T(8,128)(2,1)S(1)}, bf16[384,512]{1,0:T(8,128)(2,1)}, u32[]{:S(2)}, u32[]{:S(2)}) collective-permute-start(bf16[384,512]{1,0:T(8,128)(2,1)S(1)} %get-tuple-element.5), channel_id=1, source_target_pairs={{0,1},{1,2},{2,3},{3,4},{4,5},{5,6},{6,7},{7,0},{8,9},{9,10},{10,1... | collective-permute-start | bytes 1179656 | tf_op jit(solution)/shard_map/ppermute | solution.py:19
  33.7 6.4 %collective-permute-start.3 = (bf16[384,512]{1,0:T(8,128)(2,1)S(1)}, bf16[384,512]{1,0:T(8,128)(2,1)}, u32[]{:S(2)}, u32[]{:S(2)}) collective-permute-start(bf16[384,512]{1,0:T(8,128)(2,1)S(1)} %get-tuple-element.5), channel_id=1, source_target_pairs={{0,7},{1,0},{2,1},{3,2},{4,3},{5,4},{6,5},{7,6},{8,15},{9,8},{10,9... | collective-permute-start | bytes 1179656 | tf_op jit(solution)/shard_map/ppermute | solution.py:19
  40.1 7.1 %collective-permute-done.2 = bf16[384,512]{1,0:T(8,128)(2,1)} collective-permute-done((bf16[384,512]{1,0:T(8,128)(2,1)S(1)}, bf16[384,512]{1,0:T(8,128)(2,1)}, u32[]{:S(2)}, u32[]{:S(2)}) %collective-permute-start.2) | collective-permute-done | bytes 393248 | tf_op jit(solution)/shard_map/ppermute | solution.py:19
  47.2 1.9 %collective-permute-start.4 = (bf16[384,512]{1,0:T(8,128)(2,1)}, bf16[384,512]{1,0:T(8,128)(2,1)}, u32[]{:S(2)}, u32[]{:S(2)}) collective-permute-start(bf16[384,512]{1,0:T(8,128)(2,1)} %collective-permute-done.2), channel_id=1, source_target_pairs={{0,1},{1,2},{2,3},{3,4},{4,5},{5,6},{6,7},{7,0},{8,9},{9,10},{10,1... | collective-permute-start | bytes 1179656 | tf_op jit(solution)/shard_map/ppermute | solution.py:19
  49.1 5.1 %collective-permute-start.5 = (bf16[384,512]{1,0:T(8,128)(2,1)}, bf16[384,512]{1,0:T(8,128)(2,1)}, u32[]{:S(2)}, u32[]{:S(2)}) collective-permute-start(bf16[384,512]{1,0:T(8,128)(2,1)} %collective-permute-done.3), channel_id=1, source_target_pairs={{0,7},{1,0},{2,1},{3,2},{4,3},{5,4},{6,5},{7,6},{8,15},{9,8},{10,9... | collective-permute-start | bytes 1179656 | tf_op jit(solution)/shard_map/ppermute | solution.py:19
  54.3 6.6 %collective-permute-done.4 = bf16[384,512]{1,0:T(8,128)(2,1)} collective-permute-done((bf16[384,512]{1,0:T(8,128)(2,1)}, bf16[384,512]{1,0:T(8,128)(2,1)}, u32[]{:S(2)}, u32[]{:S(2)}) %collective-permute-start.4) | collective-permute-done | bytes 393248 | tf_op jit(solution)/shard_map/ppermute | solution.py:19
  61.0 1.9 %collective-permute-start.6 = (bf16[384,512]{1,0:T(8,128)(2,1)}, bf16[384,512]{1,0:T(8,128)(2,1)S(1)}, u32[]{:S(2)}, u32[]{:S(2)}) collective-permute-start(bf16[384,512]{1,0:T(8,128)(2,1)} %collective-permute-done.4), channel_id=1, source_target_pairs={{0,1},{1,2},{2,3},{3,4},{4,5},{5,6},{6,7},{7,0},{8,9},{9,10},{10,1... | collective-permute-start | bytes 1179656 | tf_op jit(solution)/shard_map/ppermute | solution.py:19
  62.9 5.3 %collective-permute-start.7 = (bf16[384,512]{1,0:T(8,128)(2,1)}, bf16[384,512]{1,0:T(8,128)(2,1)S(1)}, u32[]{:S(2)}, u32[]{:S(2)}) collective-permute-start(bf16[384,512]{1,0:T(8,128)(2,1)} %collective-permute-done.5), channel_id=1, source_target_pairs={{0,7},{1,0},{2,1},{3,2},{4,3},{5,4},{6,5},{7,6},{8,15},{9,8},{10,9... | collective-permute-start | bytes 1179656 | tf_op jit(solution)/shard_map/ppermute | solution.py:19
  68.2 1.0 constant_dynamic-update-slice_fusion.6
  69.2 1.0 constant_dynamic-update-slice_fusion.5
  70.3 1.0 constant_dynamic-update-slice_fusion.4
  71.3 1.1 constant_dynamic-update-slice_fusion.3
  72.5 1.3 collective-permute-done.6
  73.7 1.9 %collective-permute-start.8 = (bf16[192,512]{1,0:T(8,128)(2,1)S(1)}, bf16[192,512]{1,0:T(8,128)(2,1)S(1)}, u32[]{:S(2)}, u32[]{:S(2)}) collective-permute-start(bf16[192,512]{1,0:T(8,128)(2,1)S(1)} %slice.72), channel_id=1, source_target_pairs={{0,1},{1,2},{2,3},{3,4},{4,5},{5,6},{6,7},{7,0},{8,9},{9,10},{10,1... | collective-permute-start | bytes 589832 | tf_op jit(solution)/shard_map/ppermute | solution.py:19
  75.8 5.2 %collective-permute-start.9 = (bf16[192,512]{1,0:T(8,128)(2,1)S(1)}, bf16[192,512]{1,0:T(8,128)(2,1)S(1)}, u32[]{:S(2)}, u32[]{:S(2)}) collective-permute-start(bf16[192,512]{1,0:T(8,128)(2,1)S(1)} %slice.73), channel_id=1, source_target_pairs={{0,7},{1,0},{2,1},{3,2},{4,3},{5,4},{6,5},{7,6},{8,15},{9,8},{10,9... | collective-permute-start | bytes 589832 | tf_op jit(solution)/shard_map/ppermute | solution.py:19
  81.1 0.6 collective-permute-done.8
  81.8 1.9 %collective-permute-done.9 = bf16[192,512]{1,0:T(8,128)(2,1)S(1)} collective-permute-done((bf16[192,512]{1,0:T(8,128)(2,1)S(1)}, bf16[192,512]{1,0:T(8,128)(2,1)S(1)}, u32[]{:S(2)}, u32[]{:S(2)}) %collective-permute-start.9) | collective-permute-done | bytes 196640 | tf_op jit(solution)/shard_map/ppermute | solution.py:19
  84.2 27.3 %all-gather.2.cloned.1.call-done.weights_ref = bf16[4096,1536]{1,0:T(8,128)(2,1)} async-done(((bf16[64,1536]{1,0:T(8,128)(2,1)}), bf16[4096,1536]{1,0:T(8,128)(2,1)}) %all-gather.2.cloned.1.call-update) | async-done | bytes 12582928 | tf_op jit(solution)/shard_map/all_gather | solution.py:119
  111.5 11.5 %shard_map.55 = bf16[8,208,512]{2,1,0:T(8,128)(2,1)S(1)} custom-call(bf16[384,4096]{1,0:T(8,128)(2,1)S(1)} %constant_dynamic-update-slice_fusion.8.acts_ref, bf16[4096,1536]{1,0:T(8,128)(2,1)} %all-gather.2.cloned.1.call-done.weights_ref, f32[192,1]{1,0:T(8,128)S(1)} %copy.7.inv_rms_ref), custom_call_target="tpu_custom_call" | custom-call | flops 3623878656 | bytes 17301504 | tf_op jit(solution)/shard_map/pallas_call | solution.py:91
  123.0 49.2 %all_to_all.5 = bf16[8,208,512]{2,1,0:T(8,128)(2,1)S(1)} all-to-all(bf16[8,208,512]{2,1,0:T(8,128)(2,1)S(1)} %shard_map.55), channel_id=1, replica_groups=mesh['seq'=64,'tp'=8] {'tp'}, dimensions={0} | all-to-all | bytes 3407872 | tf_op jit(solution)/shard_map/all_to_all | solution.py:170
  173.4 1.4 fusion
  (51 shorter events, 3.6 us)
Async XLA Ops:
  6.5 7.6 %copy-start = (bf16[192,512]{1,0:T(8,128)(2,1)S(1)}, bf16[192,512]{1,0:T(8,128)(2,1)}, u32[]{:S(2)}) copy-start(bf16[192,512]{1,0:T(8,128)(2,1)} %param.5) | copy-start | bytes 589828
  6.5 105.0 %all-gather.2.cloned.1.call-start = ((), (), s32[]{:S(2)}) async-start(), calls=%async_computation.1 | async-start | bytes 12779520 | tf_op jit(solution)/shard_map/all_gather | solution.py:119
  14.3 17.0 %copy-start.1 = (f32[192,512]{1,0:T(8,128)}, f32[192,512]{1,0:T(8,128)S(1)}, u32[]{:S(2)}) copy-start(f32[192,512]{1,0:T(8,128)S(1)} %fusion.15) | copy-start | bytes 1179652
  15.6 15.7 %copy-start.3 = (f32[192,512]{1,0:T(8,128)}, f32[192,512]{1,0:T(8,128)S(1)}, u32[]{:S(2)}) copy-start(f32[192,512]{1,0:T(8,128)S(1)} %fusion.16) | copy-start | bytes 1179652
  15.7 11.9 %collective-permute-start = (f32[1,1280]{1,0:T(1,128)S(1)}, f32[1,1280]{1,0:T(1,128)S(1)}, u32[]{:S(2)}, u32[]{:S(2)}) collective-permute-start(f32[1,1280]{1,0:T(1,128)S(1)} %reshape_maximum_fusion.2), channel_id=1, source_target_pairs={{8,0},{16,8},{24,16},{32,24},{40,32},{48,40},{56,48},{64,56},{72,6... | collective-permute-start | bytes 15368 | tf_op jit(solution)/shard_map/ppermute | solution.py:14
  25.7 3.1 %collective-permute-start.1 = (f32[1,1280]{1,0:T(1,128)S(1)}, f32[1,1280]{1,0:T(1,128)S(1)}, u32[]{:S(2)}, u32[]{:S(2)}) collective-permute-start(f32[1,1280]{1,0:T(1,128)S(1)} %reshape_maximum_fusion), channel_id=1, source_target_pairs={{0,8},{8,16},{16,24},{24,32},{32,40},{40,48},{48,56},{56,64},{64,7... | collective-permute-start | bytes 15368 | tf_op jit(solution)/shard_map/ppermute | solution.py:14
  31.8 15.4 %collective-permute-start.2 = (bf16[384,512]{1,0:T(8,128)(2,1)S(1)}, bf16[384,512]{1,0:T(8,128)(2,1)}, u32[]{:S(2)}, u32[]{:S(2)}) collective-permute-start(bf16[384,512]{1,0:T(8,128)(2,1)S(1)} %get-tuple-element.5), channel_id=1, source_target_pairs={{0,1},{1,2},{2,3},{3,4},{4,5},{5,6},{6,7},{7,0},{8,9},{9,10},{10,1... | collective-permute-start | bytes 1179656 | tf_op jit(solution)/shard_map/ppermute | solution.py:19
  33.7 15.4 %collective-permute-start.3 = (bf16[384,512]{1,0:T(8,128)(2,1)S(1)}, bf16[384,512]{1,0:T(8,128)(2,1)}, u32[]{:S(2)}, u32[]{:S(2)}) collective-permute-start(bf16[384,512]{1,0:T(8,128)(2,1)S(1)} %get-tuple-element.5), channel_id=1, source_target_pairs={{0,7},{1,0},{2,1},{3,2},{4,3},{5,4},{6,5},{7,6},{8,15},{9,8},{10,9... | collective-permute-start | bytes 1179656 | tf_op jit(solution)/shard_map/ppermute | solution.py:19
  47.2 13.8 %collective-permute-start.4 = (bf16[384,512]{1,0:T(8,128)(2,1)}, bf16[384,512]{1,0:T(8,128)(2,1)}, u32[]{:S(2)}, u32[]{:S(2)}) collective-permute-start(bf16[384,512]{1,0:T(8,128)(2,1)} %collective-permute-done.2), channel_id=1, source_target_pairs={{0,1},{1,2},{2,3},{3,4},{4,5},{5,6},{6,7},{7,0},{8,9},{9,10},{10,1... | collective-permute-start | bytes 1179656 | tf_op jit(solution)/shard_map/ppermute | solution.py:19
  49.1 13.8 %collective-permute-start.5 = (bf16[384,512]{1,0:T(8,128)(2,1)}, bf16[384,512]{1,0:T(8,128)(2,1)}, u32[]{:S(2)}, u32[]{:S(2)}) collective-permute-start(bf16[384,512]{1,0:T(8,128)(2,1)} %collective-permute-done.3), channel_id=1, source_target_pairs={{0,7},{1,0},{2,1},{3,2},{4,3},{5,4},{6,5},{7,6},{8,15},{9,8},{10,9... | collective-permute-start | bytes 1179656 | tf_op jit(solution)/shard_map/ppermute | solution.py:19
  61.0 12.7 %collective-permute-start.6 = (bf16[384,512]{1,0:T(8,128)(2,1)}, bf16[384,512]{1,0:T(8,128)(2,1)S(1)}, u32[]{:S(2)}, u32[]{:S(2)}) collective-permute-start(bf16[384,512]{1,0:T(8,128)(2,1)} %collective-permute-done.4), channel_id=1, source_target_pairs={{0,1},{1,2},{2,3},{3,4},{4,5},{5,6},{6,7},{7,0},{8,9},{9,10},{10,1... | collective-permute-start | bytes 1179656 | tf_op jit(solution)/shard_map/ppermute | solution.py:19
  62.9 12.9 %collective-permute-start.7 = (bf16[384,512]{1,0:T(8,128)(2,1)}, bf16[384,512]{1,0:T(8,128)(2,1)S(1)}, u32[]{:S(2)}, u32[]{:S(2)}) collective-permute-start(bf16[384,512]{1,0:T(8,128)(2,1)} %collective-permute-done.5), channel_id=1, source_target_pairs={{0,7},{1,0},{2,1},{3,2},{4,3},{5,4},{6,5},{7,6},{8,15},{9,8},{10,9... | collective-permute-start | bytes 1179656 | tf_op jit(solution)/shard_map/ppermute | solution.py:19
  73.7 8.0 %collective-permute-start.8 = (bf16[192,512]{1,0:T(8,128)(2,1)S(1)}, bf16[192,512]{1,0:T(8,128)(2,1)S(1)}, u32[]{:S(2)}, u32[]{:S(2)}) collective-permute-start(bf16[192,512]{1,0:T(8,128)(2,1)S(1)} %slice.72), channel_id=1, source_target_pairs={{0,1},{1,2},{2,3},{3,4},{4,5},{5,6},{6,7},{7,0},{8,9},{9,10},{10,1... | collective-permute-start | bytes 589832 | tf_op jit(solution)/shard_map/ppermute | solution.py:19
  75.8 7.8 %collective-permute-start.9 = (bf16[192,512]{1,0:T(8,128)(2,1)S(1)}, bf16[192,512]{1,0:T(8,128)(2,1)S(1)}, u32[]{:S(2)}, u32[]{:S(2)}) collective-permute-start(bf16[192,512]{1,0:T(8,128)(2,1)S(1)} %slice.73), channel_id=1, source_target_pairs={{0,7},{1,0},{2,1},{3,2},{4,3},{5,4},{6,5},{7,6},{8,15},{9,8},{10,9... | collective-permute-start | bytes 589832 | tf_op jit(solution)/shard_map/ppermute | solution.py:19
  172.2 1.0 copy-start.2
  172.2 1.1 copy-start.4
  172.2 1.2 copy-start.5
Sparse Core Ops, SparseCore 0:
  10.7 100.7 all-gather.1

commit v3 on v1

--- a/solution.py
+++ b/solution.py
@@ -1,6 +1,8 @@
 import jax
 import jax.numpy as jnp
 from jax import lax
+from jax.experimental import pallas as pl
+from jax.experimental.pallas import tpu as pltpu
 from jax.sharding import PartitionSpec as P
 
 epsilon = 1e-06
@@ -38,16 +40,95 @@
     return put(whole, bottom, half, me + count // 2)
 
 
+def block_kernel(acts_ref, weights_hbm, inv_rms_ref, out_ref, rest_ref, weights_ref, mixed_ref, sems):
+    rows, depth = inv_rms_ref.shape[0], weights_ref.shape[0]
+    hidden = weights_ref.shape[1] // 2
+    blocks, kept, width = out_ref.shape
+    chunk = depth // blocks
+    copies = [
+        pltpu.make_async_copy(
+            weights_hbm.at[pl.ds(k * chunk, chunk)], weights_ref.at[pl.ds(k * chunk, chunk)], sems.at[k]
+        )
+        for k in range(blocks)
+    ]
+    for copy in copies:
+        copy.start()
+    up_proj = back_proj = jnp.zeros((rows, hidden), jnp.float32)
+    for k, copy in enumerate(copies):
+        copy.wait()
+        at = pl.ds(k * chunk, chunk)
+        up_proj += jnp.dot(
+            acts_ref[:rows, at], weights_ref[at, :hidden], preferred_element_type=jnp.float32
+        )
+        back_proj += jnp.dot(
+            acts_ref[rows:, at], weights_ref[at, hidden:], preferred_element_type=jnp.float32
+        )
+    up_proj = up_proj * inv_rms_ref[...]
+    sigmoid_up = jax.nn.sigmoid(up_proj)
+    grad_hidden = (back_proj * sigmoid_up * (1.0 + up_proj * (1.0 - sigmoid_up))).astype(
+        jnp.bfloat16
+    )
+    dots = lax.dot_general(
+        jnp.ones((4, hidden), jnp.float32),
+        grad_hidden.astype(jnp.float32) * up_proj,
+        (((1,), (1,)), ((), ())),
+        precision=lax.Precision.HIGHEST,
+        preferred_element_type=jnp.float32,
+    )
+    high = dots.astype(jnp.bfloat16).astype(jnp.float32)
+    mixed_ref[...] = jnp.zeros_like(mixed_ref)
+    mixed_ref[8:, :rows] = jnp.concatenate([high, dots - high], axis=0)
+    even = kept - 16
+    for block in range(blocks):
+        term = lax.dot_general(
+            grad_hidden,
+            weights_ref[pl.ds(block * width, width), :hidden],
+            (((1,), (1,)), ((), ())),
+            preferred_element_type=jnp.float32,
+        )
+        mixed_ref[:8] = term[even : even + 8]
+        out_ref[block, :even] = term[:even].astype(jnp.bfloat16)
+        out_ref[block, even:] = mixed_ref[...].astype(jnp.bfloat16)
+        rest_ref[block] = term[even:].astype(jnp.bfloat16)
+
+
+def block_terms(gathered, weights, inv_rms, width, kept):
+    rows, depth = gathered.shape[0] // 2, gathered.shape[1]
+    hidden = weights.shape[1] // 2
+    blocks = depth // width
+    return pl.pallas_call(
+        block_kernel,
+        in_specs=[
+            pl.BlockSpec(memory_space=pltpu.VMEM),
+            pl.BlockSpec(memory_space=pl.ANY),
+            pl.BlockSpec(memory_space=pltpu.VMEM),
+        ],
+        out_specs=[pl.BlockSpec(memory_space=pltpu.VMEM)] * 2,
+        out_shape=[
+            jax.ShapeDtypeStruct((blocks, kept, width), jnp.bfloat16),
+            jax.ShapeDtypeStruct((blocks, rows - kept + 16, width), jnp.bfloat16),
+        ],
+        scratch_shapes=[
+            pltpu.VMEM(weights.shape, jnp.bfloat16),
+            pltpu.VMEM((16, width), jnp.float32),
+            pltpu.SemaphoreType.DMA((blocks,)),
+        ],
+        compiler_params=pltpu.CompilerParams(vmem_limit_bytes=40 * 1024 * 1024),
+        cost_estimate=pl.CostEstimate(
+            flops=6 * rows * depth * hidden,
+            bytes_accessed=2 * (2 * rows * depth + 2 * depth * hidden + rows * depth),
+            transcendentals=rows * hidden,
+        ),
+    )(gathered, weights, inv_rms)
+
+
 def body(byte_acts, upstream, segment_ids, first_weight, second_weight):
     byte_rows = segment_ids.shape[0]
     width = byte_acts.shape[1]
-    hidden = first_weight.shape[1]
     model_width = width * lax.axis_size("tp")
     weights = lax.all_gather(
         jnp.concatenate([first_weight, second_weight], axis=1), "seq", axis=0, tiled=True
     )
-    first_full, second_full = weights[:, :hidden], weights[:, hidden:]
-
     base_id = segment_ids[0]
     last_id = segment_ids[byte_rows - 1]
     slot_of = segment_ids - base_id
@@ -91,23 +172,27 @@
     gathered = ring_gather(
         jnp.concatenate([pooled.astype(jnp.bfloat16), grad_sums.astype(jnp.bfloat16)], axis=0)
     )
-    pooled_b, grad_b = gathered[:byte_rows], gathered[byte_rows:]
+    pooled_b = gathered[:byte_rows]
     square_sums = jnp.sum(jnp.square(pooled_b.astype(jnp.float32)), axis=1)
     inv_rms = lax.rsqrt(square_sums / model_width + epsilon)[:, None]
 
-    back_proj = jnp.dot(grad_b, second_full, preferred_element_type=jnp.float32)
-    up_proj = inv_rms * jnp.dot(pooled_b, first_full, preferred_element_type=jnp.float32)
-    sigmoid_up = jax.nn.sigmoid(up_proj)
-    grad_hidden = (back_proj * sigmoid_up * (1.0 + up_proj * (1.0 - sigmoid_up))).astype(
-        jnp.bfloat16
-    )
-    norm_dot = lax.psum(jnp.sum(grad_hidden.astype(jnp.float32) * up_proj, axis=1), "tp")
-    partial_grad = lax.dot_general(
-        grad_hidden, first_full, (((1,), (1,)), ((), ())), preferred_element_type=jnp.float32
-    )
-    norm_grad = lax.psum_scatter(
-        partial_grad.astype(jnp.bfloat16), "tp", scatter_dimension=1, tiled=True
-    ).astype(jnp.float32)
+    kept = 144
+    sent, rest = block_terms(gathered, weights, inv_rms, width, kept)
+
+    def exchanged(a):
+        return lax.all_to_all(a, "tp", split_axis=0, concat_axis=0, tiled=True).astype(jnp.float32)
+
+    terms = exchanged(sent)
+    rest_grad = lax.cond(
+        last_slot >= kept - 8,
+        lambda a: jnp.sum(exchanged(a), axis=0)[8:],
+        lambda a: jnp.zeros((byte_rows - kept + 8, width), jnp.float32),
+        rest,
+    )
+    norm_grad = jnp.concatenate([jnp.sum(terms[:, : kept - 8], axis=0), rest_grad], axis=0)
+    norm_dot = jnp.sum(
+        terms[:, kept - 8, :byte_rows] + terms[:, kept - 4, :byte_rows], axis=0
+    )
     normed = pooled * inv_rms
     pooled_grad = grad_sums + inv_rms * (
         norm_grad - normed * (norm_dot / model_width)[:, None]

time: 174 us -> 169 us (0.971)
  the two profiles are of different devices: /device:TPU:4 before, /device:TPU:1 now
where the time goes in v3:
time: 169 us
  waiting for transfers between devices  45 us (27%)
  starting transfers between devices  40.4 us (24%)
  blocking collectives  38.2 us (23%)
  between operations  17.5 us (10%)
  local copies, waits for them, and re-layouts  10.7 us (6%)
  Pallas kernels  8.44 us (5%)
  other arithmetic  5.56 us (3%)
  matrix products  2.86 us (2%)
    all_to_all x1, blocking collectives, exchanged(): lax.all_to_all(a, 'tp', split_axis=0, concat_axis=0, tiled=True)  38.2 us
    ppermute x8, starting transfers between devices, turned(): lax.ppermute(shard, 'tp', [(i, (i + by) % count) for i in range(count)])  29.6 us
    all_gather x1, waiting for transfers between devices, body(): lax.all_gather(jnp.concatenate([first_weight, second_weight], axis=1), 's...  27.3 us
    ppermute x8, waiting for transfers between devices, turned(): lax.ppermute(shard, 'tp', [(i, (i + by) % count) for i in range(count)])  17.6 us
    ppermute x2, starting transfers between devices, shifted(): return lax.ppermute(shard, axis, pairs)  10.7 us
    pallas_call x1, Pallas kernels, block_terms(): pl.pallas_call(block_kernel, in_specs=[pl.BlockSpec(memory_space=pltpu.VM...  8.44 us
    dynamic_update_slice x8, local copies, waits for them, and re-layouts, put(): lax.dynamic_update_slice(whole, part, (row, lax.rem(owner + count, count)...  4.38 us
  transfers between devices with their start and end apart: 11, of which 7 were waited for; matrix products, arithmetic and copies ran while one was open for 8% of the time, Pallas kernels for 0%

profile of v3, /device:TPU:1, one launch (start us, length us, event | category | flops | bytes accessed | tf_op | source)
XLA Modules:
  0.0 168.6 jit_solution(11461682958252678775)
XLA Ops:
  6.5 1.7 pad_maximum_fusion.1
  8.2 1.3 fusion.34
  11.4 1.3 broadcast_subtract_fusion
  12.8 0.6 fusion.33
  13.4 0.6 add.157
  14.3 1.3 fusion.18
  15.7 8.8 %collective-permute-start = (f32[1,1280]{1,0:T(1,128)S(1)}, f32[1,1280]{1,0:T(1,128)S(1)}, u32[]{:S(2)}, u32[]{:S(2)}) collective-permute-start(f32[1,1280]{1,0:T(1,128)S(1)} %reshape_maximum_fusion.2), channel_id=1, source_target_pairs={{8,0},{16,8},{24,16},{32,24},{40,32},{48,40},{56,48},{64,56},{72,6... | collective-permute-start | bytes 15368 | tf_op jit(solution)/shard_map/ppermute | solution.py:14
  25.0 0.6 add.164
  25.7 1.9 %collective-permute-start.1 = (f32[1,1280]{1,0:T(1,128)S(1)}, f32[1,1280]{1,0:T(1,128)S(1)}, u32[]{:S(2)}, u32[]{:S(2)}) collective-permute-start(f32[1,1280]{1,0:T(1,128)S(1)} %reshape_maximum_fusion), channel_id=1, source_target_pairs={{0,8},{8,16},{16,24},{24,32},{32,40},{40,48},{48,56},{56,64},{64,7... | collective-permute-start | bytes 15368 | tf_op jit(solution)/shard_map/ppermute | solution.py:14
  29.9 1.1 add_maximum_fusion
  31.8 1.9 %collective-permute-start.2 = (bf16[384,512]{1,0:T(8,128)(2,1)S(1)}, bf16[384,512]{1,0:T(8,128)(2,1)}, u32[]{:S(2)}, u32[]{:S(2)}) collective-permute-start(bf16[384,512]{1,0:T(8,128)(2,1)S(1)} %get-tuple-element.13), channel_id=1, source_target_pairs={{0,1},{1,2},{2,3},{3,4},{4,5},{5,6},{6,7},{7,0},{8,9},{9,10},{10,1... | collective-permute-start | bytes 1179656 | tf_op jit(solution)/shard_map/ppermute | solution.py:19
  33.7 6.4 %collective-permute-start.3 = (bf16[384,512]{1,0:T(8,128)(2,1)S(1)}, bf16[384,512]{1,0:T(8,128)(2,1)}, u32[]{:S(2)}, u32[]{:S(2)}) collective-permute-start(bf16[384,512]{1,0:T(8,128)(2,1)S(1)} %get-tuple-element.13), channel_id=1, source_target_pairs={{0,7},{1,0},{2,1},{3,2},{4,3},{5,4},{6,5},{7,6},{8,15},{9,8},{10,9... | collective-permute-start | bytes 1179656 | tf_op jit(solution)/shard_map/ppermute | solution.py:19
  40.1 7.1 %collective-permute-done.2 = bf16[384,512]{1,0:T(8,128)(2,1)} collective-permute-done((bf16[384,512]{1,0:T(8,128)(2,1)S(1)}, bf16[384,512]{1,0:T(8,128)(2,1)}, u32[]{:S(2)}, u32[]{:S(2)}) %collective-permute-start.2) | collective-permute-done | bytes 393248 | tf_op jit(solution)/shard_map/ppermute | solution.py:19
  47.2 1.9 %collective-permute-start.4 = (bf16[384,512]{1,0:T(8,128)(2,1)}, bf16[384,512]{1,0:T(8,128)(2,1)}, u32[]{:S(2)}, u32[]{:S(2)}) collective-permute-start(bf16[384,512]{1,0:T(8,128)(2,1)} %collective-permute-done.2), channel_id=1, source_target_pairs={{0,1},{1,2},{2,3},{3,4},{4,5},{5,6},{6,7},{7,0},{8,9},{9,10},{10,1... | collective-permute-start | bytes 1179656 | tf_op jit(solution)/shard_map/ppermute | solution.py:19
  49.1 5.1 %collective-permute-start.5 = (bf16[384,512]{1,0:T(8,128)(2,1)}, bf16[384,512]{1,0:T(8,128)(2,1)}, u32[]{:S(2)}, u32[]{:S(2)}) collective-permute-start(bf16[384,512]{1,0:T(8,128)(2,1)} %collective-permute-done.3), channel_id=1, source_target_pairs={{0,7},{1,0},{2,1},{3,2},{4,3},{5,4},{6,5},{7,6},{8,15},{9,8},{10,9... | collective-permute-start | bytes 1179656 | tf_op jit(solution)/shard_map/ppermute | solution.py:19
  54.3 6.6 %collective-permute-done.4 = bf16[384,512]{1,0:T(8,128)(2,1)} collective-permute-done((bf16[384,512]{1,0:T(8,128)(2,1)}, bf16[384,512]{1,0:T(8,128)(2,1)}, u32[]{:S(2)}, u32[]{:S(2)}) %collective-permute-start.4) | collective-permute-done | bytes 393248 | tf_op jit(solution)/shard_map/ppermute | solution.py:19
  61.0 1.9 %collective-permute-start.6 = (bf16[384,512]{1,0:T(8,128)(2,1)}, bf16[384,512]{1,0:T(8,128)(2,1)S(1)}, u32[]{:S(2)}, u32[]{:S(2)}) collective-permute-start(bf16[384,512]{1,0:T(8,128)(2,1)} %collective-permute-done.4), channel_id=1, source_target_pairs={{0,1},{1,2},{2,3},{3,4},{4,5},{5,6},{6,7},{7,0},{8,9},{9,10},{10,1... | collective-permute-start | bytes 1179656 | tf_op jit(solution)/shard_map/ppermute | solution.py:19
  62.9 5.3 %collective-permute-start.7 = (bf16[384,512]{1,0:T(8,128)(2,1)}, bf16[384,512]{1,0:T(8,128)(2,1)S(1)}, u32[]{:S(2)}, u32[]{:S(2)}) collective-permute-start(bf16[384,512]{1,0:T(8,128)(2,1)} %collective-permute-done.5), channel_id=1, source_target_pairs={{0,7},{1,0},{2,1},{3,2},{4,3},{5,4},{6,5},{7,6},{8,15},{9,8},{10,9... | collective-permute-start | bytes 1179656 | tf_op jit(solution)/shard_map/ppermute | solution.py:19
  68.2 1.0 constant_dynamic-update-slice_fusion.6
  69.2 1.0 constant_dynamic-update-slice_fusion.5
  70.3 1.0 constant_dynamic-update-slice_fusion.4
  71.3 1.1 constant_dynamic-update-slice_fusion.3
  72.5 1.3 collective-permute-done.6
  73.7 1.9 %collective-permute-start.8 = (bf16[192,512]{1,0:T(8,128)(2,1)S(1)}, bf16[192,512]{1,0:T(8,128)(2,1)S(1)}, u32[]{:S(2)}, u32[]{:S(2)}) collective-permute-start(bf16[192,512]{1,0:T(8,128)(2,1)S(1)} %slice.76), channel_id=1, source_target_pairs={{0,1},{1,2},{2,3},{3,4},{4,5},{5,6},{6,7},{7,0},{8,9},{9,10},{10,1... | collective-permute-start | bytes 589832 | tf_op jit(solution)/shard_map/ppermute | solution.py:19
  75.8 5.2 %collective-permute-start.9 = (bf16[192,512]{1,0:T(8,128)(2,1)S(1)}, bf16[192,512]{1,0:T(8,128)(2,1)S(1)}, u32[]{:S(2)}, u32[]{:S(2)}) collective-permute-start(bf16[192,512]{1,0:T(8,128)(2,1)S(1)} %slice.77), channel_id=1, source_target_pairs={{0,7},{1,0},{2,1},{3,2},{4,3},{5,4},{6,5},{7,6},{8,15},{9,8},{10,9... | collective-permute-start | bytes 589832 | tf_op jit(solution)/shard_map/ppermute | solution.py:19
  81.1 0.6 collective-permute-done.8
  81.8 1.9 %collective-permute-done.9 = bf16[192,512]{1,0:T(8,128)(2,1)S(1)} collective-permute-done((bf16[192,512]{1,0:T(8,128)(2,1)S(1)}, bf16[192,512]{1,0:T(8,128)(2,1)S(1)}, u32[]{:S(2)}, u32[]{:S(2)}) %collective-permute-start.9) | collective-permute-done | bytes 196640 | tf_op jit(solution)/shard_map/ppermute | solution.py:19
  84.2 27.3 %all-gather.2.cloned.1.call-done.weights_hbm = bf16[4096,1536]{1,0:T(8,128)(2,1)} async-done(((bf16[64,1536]{1,0:T(8,128)(2,1)}), bf16[4096,1536]{1,0:T(8,128)(2,1)}) %all-gather.2.cloned.1.call-update) | async-done | bytes 12582928 | tf_op jit(solution)/shard_map/all_gather | solution.py:129
  111.5 8.4 %shard_map.55 = (bf16[8,144,512]{2,1,0:T(8,128)(2,1)S(1)}, bf16[8,64,512]{2,1,0:T(8,128)(2,1)}) custom-call(bf16[384,4096]{1,0:T(8,128)(2,1)S(1)} %constant_dynamic-update-slice_fusion.8.acts_ref, bf16[4096,1536]{1,0:T(8,128)(2,1)} %all-gather.2.cloned.1.call-done.weights_hbm, f32[192,1]{1,0:T(8,128)S(1)} %copy.7.inv_rms_ref), custom_call_target="tpu_custom_call" | custom-call | flops 3623878656 | bytes 17301504 | tf_op jit(solution)/shard_map/pallas_call | solution.py:99
  120.0 1.0 copy-done.1
  121.0 38.2 %all_to_all.10 = bf16[8,144,512]{2,1,0:T(8,128)(2,1)S(1)} all-to-all(bf16[8,144,512]{2,1,0:T(8,128)(2,1)} %copy-done.1), channel_id=1, replica_groups=mesh['seq'=64,'tp'=8] {'tp'}, dimensions={0} | all-to-all | bytes 2359296 | tf_op jit(solution)/shard_map/all_to_all | solution.py:183
  160.4 1.4 fusion
  (55 shorter events, 4.2 us)
Async XLA Ops:
  6.5 7.6 %copy-start = (bf16[192,512]{1,0:T(8,128)(2,1)S(1)}, bf16[192,512]{1,0:T(8,128)(2,1)}, u32[]{:S(2)}) copy-start(bf16[192,512]{1,0:T(8,128)(2,1)} %param.7) | copy-start | bytes 589828
  6.5 105.0 %all-gather.2.cloned.1.call-start = ((), (), s32[]{:S(2)}) async-start(), calls=%async_computation.2 | async-start | bytes 12779520 | tf_op jit(solution)/shard_map/all_gather | solution.py:129
  14.3 17.0 %copy-start.2 = (f32[192,512]{1,0:T(8,128)}, f32[192,512]{1,0:T(8,128)S(1)}, u32[]{:S(2)}) copy-start(f32[192,512]{1,0:T(8,128)S(1)} %fusion.17) | copy-start | bytes 1179652
  15.6 15.7 %copy-start.4 = (f32[192,512]{1,0:T(8,128)}, f32[192,512]{1,0:T(8,128)S(1)}, u32[]{:S(2)}) copy-start(f32[192,512]{1,0:T(8,128)S(1)} %fusion.18) | copy-start | bytes 1179652
  15.7 11.9 %collective-permute-start = (f32[1,1280]{1,0:T(1,128)S(1)}, f32[1,1280]{1,0:T(1,128)S(1)}, u32[]{:S(2)}, u32[]{:S(2)}) collective-permute-start(f32[1,1280]{1,0:T(1,128)S(1)} %reshape_maximum_fusion.2), channel_id=1, source_target_pairs={{8,0},{16,8},{24,16},{32,24},{40,32},{48,40},{56,48},{64,56},{72,6... | collective-permute-start | bytes 15368 | tf_op jit(solution)/shard_map/ppermute | solution.py:14
  25.7 3.1 %collective-permute-start.1 = (f32[1,1280]{1,0:T(1,128)S(1)}, f32[1,1280]{1,0:T(1,128)S(1)}, u32[]{:S(2)}, u32[]{:S(2)}) collective-permute-start(f32[1,1280]{1,0:T(1,128)S(1)} %reshape_maximum_fusion), channel_id=1, source_target_pairs={{0,8},{8,16},{16,24},{24,32},{32,40},{40,48},{48,56},{56,64},{64,7... | collective-permute-start | bytes 15368 | tf_op jit(solution)/shard_map/ppermute | solution.py:14
  31.8 15.4 %collective-permute-start.2 = (bf16[384,512]{1,0:T(8,128)(2,1)S(1)}, bf16[384,512]{1,0:T(8,128)(2,1)}, u32[]{:S(2)}, u32[]{:S(2)}) collective-permute-start(bf16[384,512]{1,0:T(8,128)(2,1)S(1)} %get-tuple-element.13), channel_id=1, source_target_pairs={{0,1},{1,2},{2,3},{3,4},{4,5},{5,6},{6,7},{7,0},{8,9},{9,10},{10,1... | collective-permute-start | bytes 1179656 | tf_op jit(solution)/shard_map/ppermute | solution.py:19
  33.7 15.4 %collective-permute-start.3 = (bf16[384,512]{1,0:T(8,128)(2,1)S(1)}, bf16[384,512]{1,0:T(8,128)(2,1)}, u32[]{:S(2)}, u32[]{:S(2)}) collective-permute-start(bf16[384,512]{1,0:T(8,128)(2,1)S(1)} %get-tuple-element.13), channel_id=1, source_target_pairs={{0,7},{1,0},{2,1},{3,2},{4,3},{5,4},{6,5},{7,6},{8,15},{9,8},{10,9... | collective-permute-start | bytes 1179656 | tf_op jit(solution)/shard_map/ppermute | solution.py:19
  47.2 13.8 %collective-permute-start.4 = (bf16[384,512]{1,0:T(8,128)(2,1)}, bf16[384,512]{1,0:T(8,128)(2,1)}, u32[]{:S(2)}, u32[]{:S(2)}) collective-permute-start(bf16[384,512]{1,0:T(8,128)(2,1)} %collective-permute-done.2), channel_id=1, source_target_pairs={{0,1},{1,2},{2,3},{3,4},{4,5},{5,6},{6,7},{7,0},{8,9},{9,10},{10,1... | collective-permute-start | bytes 1179656 | tf_op jit(solution)/shard_map/ppermute | solution.py:19
  49.1 13.8 %collective-permute-start.5 = (bf16[384,512]{1,0:T(8,128)(2,1)}, bf16[384,512]{1,0:T(8,128)(2,1)}, u32[]{:S(2)}, u32[]{:S(2)}) collective-permute-start(bf16[384,512]{1,0:T(8,128)(2,1)} %collective-permute-done.3), channel_id=1, source_target_pairs={{0,7},{1,0},{2,1},{3,2},{4,3},{5,4},{6,5},{7,6},{8,15},{9,8},{10,9... | collective-permute-start | bytes 1179656 | tf_op jit(solution)/shard_map/ppermute | solution.py:19
  61.0 12.7 %collective-permute-start.6 = (bf16[384,512]{1,0:T(8,128)(2,1)}, bf16[384,512]{1,0:T(8,128)(2,1)S(1)}, u32[]{:S(2)}, u32[]{:S(2)}) collective-permute-start(bf16[384,512]{1,0:T(8,128)(2,1)} %collective-permute-done.4), channel_id=1, source_target_pairs={{0,1},{1,2},{2,3},{3,4},{4,5},{5,6},{6,7},{7,0},{8,9},{9,10},{10,1... | collective-permute-start | bytes 1179656 | tf_op jit(solution)/shard_map/ppermute | solution.py:19
  62.9 12.9 %collective-permute-start.7 = (bf16[384,512]{1,0:T(8,128)(2,1)}, bf16[384,512]{1,0:T(8,128)(2,1)S(1)}, u32[]{:S(2)}, u32[]{:S(2)}) collective-permute-start(bf16[384,512]{1,0:T(8,128)(2,1)} %collective-permute-done.5), channel_id=1, source_target_pairs={{0,7},{1,0},{2,1},{3,2},{4,3},{5,4},{6,5},{7,6},{8,15},{9,8},{10,9... | collective-permute-start | bytes 1179656 | tf_op jit(solution)/shard_map/ppermute | solution.py:19
  73.7 8.0 %collective-permute-start.8 = (bf16[192,512]{1,0:T(8,128)(2,1)S(1)}, bf16[192,512]{1,0:T(8,128)(2,1)S(1)}, u32[]{:S(2)}, u32[]{:S(2)}) collective-permute-start(bf16[192,512]{1,0:T(8,128)(2,1)S(1)} %slice.76), channel_id=1, source_target_pairs={{0,1},{1,2},{2,3},{3,4},{4,5},{5,6},{6,7},{7,0},{8,9},{9,10},{10,1... | collective-permute-start | bytes 589832 | tf_op jit(solution)/shard_map/ppermute | solution.py:19
  75.8 7.8 %collective-permute-start.9 = (bf16[192,512]{1,0:T(8,128)(2,1)S(1)}, bf16[192,512]{1,0:T(8,128)(2,1)S(1)}, u32[]{:S(2)}, u32[]{:S(2)}) collective-permute-start(bf16[192,512]{1,0:T(8,128)(2,1)S(1)} %slice.77), channel_id=1, source_target_pairs={{0,7},{1,0},{2,1},{3,2},{4,3},{5,4},{6,5},{7,6},{8,15},{9,8},{10,9... | collective-permute-start | bytes 589832 | tf_op jit(solution)/shard_map/ppermute | solution.py:19
  120.0 1.0 copy-start.1
  159.2 1.0 copy-start.3
  159.2 1.1 copy-start.5
  159.2 1.2 copy-start.6
Sparse Core Ops, SparseCore 0:
  10.7 100.7 all-gather.1

commit v4 on v3

--- a/solution.py
+++ b/solution.py
@@ -3,9 +3,12 @@
 from jax import lax
 from jax.experimental import pallas as pl
 from jax.experimental.pallas import tpu as pltpu
+from jax.sharding import Mesh
 from jax.sharding import PartitionSpec as P
 
 epsilon = 1e-06
+seq = ("y", "x", "core")
+sizes = (8, 4, 2)
 
 
 def shifted(shard, axis, by):
@@ -45,17 +48,28 @@
     hidden = weights_ref.shape[1] // 2
     blocks, kept, width = out_ref.shape
     chunk = depth // blocks
-    copies = [
-        pltpu.make_async_copy(
-            weights_hbm.at[pl.ds(k * chunk, chunk)], weights_ref.at[pl.ds(k * chunk, chunk)], sems.at[k]
-        )
-        for k in range(blocks)
-    ]
+    count_y, count_x, count_core = sizes
+    part = depth // (count_y * count_x * count_core)
+    copies = []
+    for y in range(count_y):
+        for core in range(count_core):
+            for x in range(count_x):
+                there = ((y * count_core + core) * count_x + x) * part
+                here = ((y * count_x + x) * count_core + core) * part
+                copies.append(
+                    pltpu.make_async_copy(
+                        weights_hbm.at[pl.ds(there, part)],
+                        weights_ref.at[pl.ds(here, part)],
+                        sems.at[len(copies)],
+                    )
+                )
     for copy in copies:
         copy.start()
+    per_chunk = len(copies) // blocks
     up_proj = back_proj = jnp.zeros((rows, hidden), jnp.float32)
-    for k, copy in enumerate(copies):
-        copy.wait()
+    for k in range(blocks):
+        for copy in copies[k * per_chunk : (k + 1) * per_chunk]:
+            copy.wait()
         at = pl.ds(k * chunk, chunk)
         up_proj += jnp.dot(
             acts_ref[:rows, at], weights_ref[at, :hidden], preferred_element_type=jnp.float32
@@ -105,13 +119,13 @@
         ],
         out_specs=[pl.BlockSpec(memory_space=pltpu.VMEM)] * 2,
         out_shape=[
-            jax.ShapeDtypeStruct((blocks, kept, width), jnp.bfloat16),
+            pltpu.VMEM((blocks, kept, width), jnp.bfloat16),
             jax.ShapeDtypeStruct((blocks, rows - kept + 16, width), jnp.bfloat16),
         ],
         scratch_shapes=[
             pltpu.VMEM(weights.shape, jnp.bfloat16),
             pltpu.VMEM((16, width), jnp.float32),
-            pltpu.SemaphoreType.DMA((blocks,)),
+            pltpu.SemaphoreType.DMA((sizes[0] * sizes[1] * sizes[2],)),
         ],
         compiler_params=pltpu.CompilerParams(vmem_limit_bytes=40 * 1024 * 1024),
         cost_estimate=pl.CostEstimate(
@@ -126,9 +140,10 @@
     byte_rows = segment_ids.shape[0]
     width = byte_acts.shape[1]
     model_width = width * lax.axis_size("tp")
-    weights = lax.all_gather(
-        jnp.concatenate([first_weight, second_weight], axis=1), "seq", axis=0, tiled=True
-    )
+    weights = jnp.concatenate([first_weight, second_weight], axis=1)
+    weights = lax.all_gather(weights, "x", axis=0, tiled=True)
+    weights = lax.all_gather(weights, ("y", "core"), axis=0, tiled=True)
+
     base_id = segment_ids[0]
     last_id = segment_ids[byte_rows - 1]
     slot_of = segment_ids - base_id
@@ -147,8 +162,8 @@
         count = jnp.zeros((1, 128), jnp.float32) + at(counts)
         return jnp.concatenate([at(seg_sums), at(grad_sums), count, tag], axis=1)
 
-    tail = shifted(packed(0, base_id), "seq", -1)
-    head = shifted(packed(last_slot, last_id), "seq", 1)
+    tail = shifted(packed(0, base_id), seq, -1)
+    head = shifted(packed(last_slot, last_id), seq, 1)
 
     def pick(slot, segment, row):
         matched = row[0, 2 * width + 128] == (segment + 1).astype(jnp.float32)
@@ -208,10 +223,11 @@
 
 
 def solution(mesh):
+    grid = Mesh(mesh.devices.reshape(sizes + (-1,)), seq + ("tp",))
     return jax.shard_map(
         body,
-        mesh=mesh,
-        in_specs=(P("seq", "tp"), P("seq", "tp"), P("seq"), P("seq", "tp"), P("seq", "tp")),
-        out_specs=P("seq", "tp"),
+        mesh=grid,
+        in_specs=(P(seq, "tp"), P(seq, "tp"), P(seq), P(seq, "tp"), P(seq, "tp")),
+        out_specs=P(seq, "tp"),
         check_vma=False,
     )

time: 169 us -> 165 us (0.976)
  waiting for transfers between devices: 45 us -> 26 us
  blocking collectives: 38.2 us -> 51.5 us
    all_gather x1, waiting for transfers between devices: 27.3 us -> 6.03 us  [body(): weights = lax.all_gather(weights, ('y', 'core'), axis=0, tiled=True)]
    all_gather x0 -> x1, blocking collectives: none -> 13.3 us  [body(): weights = lax.all_gather(weights, 'x', axis=0, tiled=True)]
    ppermute x8, waiting for transfers between devices: 17.6 us -> 20 us  [turned(): lax.ppermute(shard, 'tp', [(i, (i + by) % count) for i in range(count)])]
  transfers between devices with their start and end apart: 11 -> 11, of which waited for: 7 -> 6; matrix products, arithmetic and copies ran while one was open for 8% -> 9% of each run, Pallas kernels for 0% -> 0%
where the time goes in v4:
time: 165 us; the launch traced here: 164 us
  blocking collectives  51.5 us (31%)
  starting transfers between devices  40.3 us (24%)
  waiting for transfers between devices  26 us (16%)
  between operations  17.9 us (11%)
  local copies, waits for them, and re-layouts  11.1 us (7%)
  Pallas kernels  9.03 us (5%)
  other arithmetic  5.11 us (3%)
  matrix products  2.87 us (2%)
    all_to_all x1, blocking collectives, exchanged(): lax.all_to_all(a, 'tp', split_axis=0, concat_axis=0, tiled=True)  38.2 us
    ppermute x8, starting transfers between devices, turned(): lax.ppermute(shard, 'tp', [(i, (i + by) % count) for i in range(count)])  28.2 us
    ppermute x8, waiting for transfers between devices, turned(): lax.ppermute(shard, 'tp', [(i, (i + by) % count) for i in range(count)])  20 us
    all_gather x1, blocking collectives, body(): weights = lax.all_gather(weights, 'x', axis=0, tiled=True)  13.3 us
    ppermute x2, starting transfers between devices, shifted(): return lax.ppermute(shard, axis, pairs)  12 us
    pallas_call x1, Pallas kernels, block_terms(): pl.pallas_call(block_kernel, in_specs=[pl.BlockSpec(memory_space=pltpu.VM...  9.03 us
    all_gather x1, waiting for transfers between devices, body(): weights = lax.all_gather(weights, ('y', 'core'), axis=0, tiled=True)  6.03 us
    dynamic_update_slice x8, local copies, waits for them, and re-layouts, put(): lax.dynamic_update_slice(whole, part, (row, lax.rem(owner + count, count)...  4.42 us
  transfers between devices with their start and end apart: 11, of which 6 were waited for; matrix products, arithmetic and copies ran while one was open for 9% of the time, Pallas kernels for 0%

profile of v4, /device:TPU:1, one launch (start us, length us, event | category | flops | bytes accessed | tf_op | source)
XLA Modules:
  0.0 163.8 jit_solution(2680737218027838479)
XLA Ops:
  6.5 1.0 pad_maximum_fusion.1
  7.5 13.3 %all_gather.6 = bf16[256,1536]{1,0:T(8,128)(2,1)} all-gather(bf16[64,1536]{1,0:T(8,128)(2,1)S(1)} %pad_maximum_fusion.1), channel_id=1, replica_groups=mesh['y'=8,'x'=4,'core'=2,'tp'=8] {'x'}, dimensions={0}, use_global_device_ids=true | all-gather | bytes 983040 | tf_op jit(solution)/shard_map/all_gather | solution.py:144
  20.9 1.4 fusion.34
  24.3 1.3 broadcast_subtract_fusion
  25.8 0.6 fusion.33
  26.4 0.6 add.157
  27.3 1.3 fusion.18
  28.6 10.1 %collective-permute-start = (f32[1,1280]{1,0:T(1,128)S(1)}, f32[1,1280]{1,0:T(1,128)S(1)}, u32[]{:S(2)}, u32[]{:S(2)}) collective-permute-start(f32[1,1280]{1,0:T(1,128)S(1)} %reshape_maximum_fusion.2), channel_id=1, source_target_pairs={{8,0},{16,8},{24,16},{32,24},{40,32},{48,40},{56,48},{64,56},{72,6... | collective-permute-start | bytes 15368 | tf_op jit(solution)/shard_map/ppermute | solution.py:17
  40.2 1.9 %collective-permute-start.1 = (f32[1,1280]{1,0:T(1,128)S(1)}, f32[1,1280]{1,0:T(1,128)S(1)}, u32[]{:S(2)}, u32[]{:S(2)}) collective-permute-start(f32[1,1280]{1,0:T(1,128)S(1)} %reshape_maximum_fusion), channel_id=1, source_target_pairs={{0,8},{8,16},{16,24},{24,32},{32,40},{40,48},{48,56},{56,64},{64,7... | collective-permute-start | bytes 15368 | tf_op jit(solution)/shard_map/ppermute | solution.py:17
  44.6 1.3 add_maximum_fusion
  46.7 1.9 %collective-permute-start.2 = (bf16[384,512]{1,0:T(8,128)(2,1)S(1)}, bf16[384,512]{1,0:T(8,128)(2,1)}, u32[]{:S(2)}, u32[]{:S(2)}) collective-permute-start(bf16[384,512]{1,0:T(8,128)(2,1)S(1)} %get-tuple-element.13), channel_id=1, source_target_pairs={{0,1},{1,2},{2,3},{3,4},{4,5},{5,6},{6,7},{7,0},{8,9},{9,10},{10,1... | collective-permute-start | bytes 1179656 | tf_op jit(solution)/shard_map/ppermute | solution.py:22
  48.6 6.5 %collective-permute-start.3 = (bf16[384,512]{1,0:T(8,128)(2,1)S(1)}, bf16[384,512]{1,0:T(8,128)(2,1)}, u32[]{:S(2)}, u32[]{:S(2)}) collective-permute-start(bf16[384,512]{1,0:T(8,128)(2,1)S(1)} %get-tuple-element.13), channel_id=1, source_target_pairs={{0,7},{1,0},{2,1},{3,2},{4,3},{5,4},{6,5},{7,6},{8,15},{9,8},{10,9... | collective-permute-start | bytes 1179656 | tf_op jit(solution)/shard_map/ppermute | solution.py:22
  55.1 7.0 %collective-permute-done.2 = bf16[384,512]{1,0:T(8,128)(2,1)} collective-permute-done((bf16[384,512]{1,0:T(8,128)(2,1)S(1)}, bf16[384,512]{1,0:T(8,128)(2,1)}, u32[]{:S(2)}, u32[]{:S(2)}) %collective-permute-start.2) | collective-permute-done | bytes 393248 | tf_op jit(solution)/shard_map/ppermute | solution.py:22
  62.1 1.9 %collective-permute-start.4 = (bf16[384,512]{1,0:T(8,128)(2,1)}, bf16[384,512]{1,0:T(8,128)(2,1)}, u32[]{:S(2)}, u32[]{:S(2)}) collective-permute-start(bf16[384,512]{1,0:T(8,128)(2,1)} %collective-permute-done.2), channel_id=1, source_target_pairs={{0,1},{1,2},{2,3},{3,4},{4,5},{5,6},{6,7},{7,0},{8,9},{9,10},{10,1... | collective-permute-start | bytes 1179656 | tf_op jit(solution)/shard_map/ppermute | solution.py:22
  64.1 4.8 %collective-permute-start.5 = (bf16[384,512]{1,0:T(8,128)(2,1)}, bf16[384,512]{1,0:T(8,128)(2,1)}, u32[]{:S(2)}, u32[]{:S(2)}) collective-permute-start(bf16[384,512]{1,0:T(8,128)(2,1)} %collective-permute-done.3), channel_id=1, source_target_pairs={{0,7},{1,0},{2,1},{3,2},{4,3},{5,4},{6,5},{7,6},{8,15},{9,8},{10,9... | collective-permute-start | bytes 1179656 | tf_op jit(solution)/shard_map/ppermute | solution.py:22
  69.0 7.7 %collective-permute-done.4 = bf16[384,512]{1,0:T(8,128)(2,1)} collective-permute-done((bf16[384,512]{1,0:T(8,128)(2,1)}, bf16[384,512]{1,0:T(8,128)(2,1)}, u32[]{:S(2)}, u32[]{:S(2)}) %collective-permute-start.4) | collective-permute-done | bytes 393248 | tf_op jit(solution)/shard_map/ppermute | solution.py:22
  76.6 1.9 %collective-permute-start.6 = (bf16[384,512]{1,0:T(8,128)(2,1)}, bf16[384,512]{1,0:T(8,128)(2,1)S(1)}, u32[]{:S(2)}, u32[]{:S(2)}) collective-permute-start(bf16[384,512]{1,0:T(8,128)(2,1)} %collective-permute-done.4), channel_id=1, source_target_pairs={{0,1},{1,2},{2,3},{3,4},{4,5},{5,6},{6,7},{7,0},{8,9},{9,10},{10,1... | collective-permute-start | bytes 1179656 | tf_op jit(solution)/shard_map/ppermute | solution.py:22
  78.6 4.6 %collective-permute-start.7 = (bf16[384,512]{1,0:T(8,128)(2,1)}, bf16[384,512]{1,0:T(8,128)(2,1)S(1)}, u32[]{:S(2)}, u32[]{:S(2)}) collective-permute-start(bf16[384,512]{1,0:T(8,128)(2,1)} %collective-permute-done.5), channel_id=1, source_target_pairs={{0,7},{1,0},{2,1},{3,2},{4,3},{5,4},{6,5},{7,6},{8,15},{9,8},{10,9... | collective-permute-start | bytes 1179656 | tf_op jit(solution)/shard_map/ppermute | solution.py:22
  83.2 1.1 constant_dynamic-update-slice_fusion.6
  84.3 1.0 constant_dynamic-update-slice_fusion.5
  85.3 1.1 constant_dynamic-update-slice_fusion.4
  86.5 1.0 constant_dynamic-update-slice_fusion.3
  87.5 2.8 %collective-permute-done.6 = bf16[384,512]{1,0:T(8,128)(2,1)S(1)} collective-permute-done((bf16[384,512]{1,0:T(8,128)(2,1)}, bf16[384,512]{1,0:T(8,128)(2,1)S(1)}, u32[]{:S(2)}, u32[]{:S(2)}) %collective-permute-start.6) | collective-permute-done | bytes 393248 | tf_op jit(solution)/shard_map/ppermute | solution.py:22
  90.3 1.9 %collective-permute-start.8 = (bf16[192,512]{1,0:T(8,128)(2,1)S(1)}, bf16[192,512]{1,0:T(8,128)(2,1)S(1)}, u32[]{:S(2)}, u32[]{:S(2)}) collective-permute-start(bf16[192,512]{1,0:T(8,128)(2,1)S(1)} %slice.76), channel_id=1, source_target_pairs={{0,1},{1,2},{2,3},{3,4},{4,5},{5,6},{6,7},{7,0},{8,9},{9,10},{10,1... | collective-permute-start | bytes 589832 | tf_op jit(solution)/shard_map/ppermute | solution.py:22
  92.3 4.6 %collective-permute-start.9 = (bf16[192,512]{1,0:T(8,128)(2,1)S(1)}, bf16[192,512]{1,0:T(8,128)(2,1)S(1)}, u32[]{:S(2)}, u32[]{:S(2)}) collective-permute-start(bf16[192,512]{1,0:T(8,128)(2,1)S(1)} %slice.77), channel_id=1, source_target_pairs={{0,7},{1,0},{2,1},{3,2},{4,3},{5,4},{6,5},{7,6},{8,15},{9,8},{10,9... | collective-permute-start | bytes 589832 | tf_op jit(solution)/shard_map/ppermute | solution.py:22
  97.0 1.8 %collective-permute-done.8 = bf16[192,512]{1,0:T(8,128)(2,1)S(1)} collective-permute-done((bf16[192,512]{1,0:T(8,128)(2,1)S(1)}, bf16[192,512]{1,0:T(8,128)(2,1)S(1)}, u32[]{:S(2)}, u32[]{:S(2)}) %collective-permute-start.8) | collective-permute-done | bytes 196640 | tf_op jit(solution)/shard_map/ppermute | solution.py:22
  98.8 0.7 collective-permute-done.9
  100.1 6.0 %all-gather.2.cloned.1.call-done.weights_hbm = bf16[4096,1536]{1,0:T(8,128)(2,1)} async-done(((bf16[256,1536]{1,0:T(8,128)(2,1)}), bf16[4096,1536]{1,0:T(8,128)(2,1)}) %all-gather.2.cloned.1.call-update) | async-done | bytes 12582928 | tf_op jit(solution)/shard_map/all_gather | solution.py:145
  106.1 9.0 %shard_map.55 = (bf16[8,144,512]{2,1,0:T(8,128)(2,1)S(1)}, bf16[8,64,512]{2,1,0:T(8,128)(2,1)}) custom-call(bf16[384,4096]{1,0:T(8,128)(2,1)S(1)} %constant_dynamic-update-slice_fusion.8.acts_ref, bf16[4096,1536]{1,0:T(8,128)(2,1)} %all-gather.2.cloned.1.call-done.weights_hbm, f32[192,1]{1,0:T(8,128)S(1)} %copy.7.inv_rms_ref), custom_call_target="tpu_custom_call" | custom-call | flops 3623878656 | bytes 17301504 | tf_op jit(solution)/shard_map/pallas_call | solution.py:113
  115.1 1.0 copy-done.1
  116.2 38.2 %all_to_all.10 = bf16[8,144,512]{2,1,0:T(8,128)(2,1)S(1)} all-to-all(bf16[8,144,512]{2,1,0:T(8,128)(2,1)} %copy-done.1), channel_id=1, replica_groups=mesh['y'=8,'x'=4,'core'=2,'tp'=8] {'tp'}, dimensions={0} | all-to-all | bytes 2359296 | tf_op jit(solution)/shard_map/all_to_all | solution.py:198
  155.5 1.4 fusion
  (56 shorter events, 4.7 us)
Async XLA Ops:
  6.5 20.6 %copy-start = (bf16[192,512]{1,0:T(8,128)(2,1)S(1)}, bf16[192,512]{1,0:T(8,128)(2,1)}, u32[]{:S(2)}) copy-start(bf16[192,512]{1,0:T(8,128)(2,1)} %param.7) | copy-start | bytes 589828
  6.5 99.6 %all-gather.2.cloned.1.call-start = ((), (), s32[]{:S(2)}) async-start(), calls=%async_computation.2 | async-start | bytes 13369344 | tf_op jit(solution)/shard_map/all_gather | solution.py:145
  27.3 18.9 %copy-start.2 = (f32[192,512]{1,0:T(8,128)}, f32[192,512]{1,0:T(8,128)S(1)}, u32[]{:S(2)}) copy-start(f32[192,512]{1,0:T(8,128)S(1)} %fusion.17) | copy-start | bytes 1179652
  28.6 17.6 %copy-start.4 = (f32[192,512]{1,0:T(8,128)}, f32[192,512]{1,0:T(8,128)S(1)}, u32[]{:S(2)}) copy-start(f32[192,512]{1,0:T(8,128)S(1)} %fusion.18) | copy-start | bytes 1179652
  28.6 13.5 %collective-permute-start = (f32[1,1280]{1,0:T(1,128)S(1)}, f32[1,1280]{1,0:T(1,128)S(1)}, u32[]{:S(2)}, u32[]{:S(2)}) collective-permute-start(f32[1,1280]{1,0:T(1,128)S(1)} %reshape_maximum_fusion.2), channel_id=1, source_target_pairs={{8,0},{16,8},{24,16},{32,24},{40,32},{48,40},{56,48},{64,56},{72,6... | collective-permute-start | bytes 15368 | tf_op jit(solution)/shard_map/ppermute | solution.py:17
  40.2 3.2 %collective-permute-start.1 = (f32[1,1280]{1,0:T(1,128)S(1)}, f32[1,1280]{1,0:T(1,128)S(1)}, u32[]{:S(2)}, u32[]{:S(2)}) collective-permute-start(f32[1,1280]{1,0:T(1,128)S(1)} %reshape_maximum_fusion), channel_id=1, source_target_pairs={{0,8},{8,16},{16,24},{24,32},{32,40},{40,48},{48,56},{56,64},{64,7... | collective-permute-start | bytes 15368 | tf_op jit(solution)/shard_map/ppermute | solution.py:17
  46.7 15.5 %collective-permute-start.2 = (bf16[384,512]{1,0:T(8,128)(2,1)S(1)}, bf16[384,512]{1,0:T(8,128)(2,1)}, u32[]{:S(2)}, u32[]{:S(2)}) collective-permute-start(bf16[384,512]{1,0:T(8,128)(2,1)S(1)} %get-tuple-element.13), channel_id=1, source_target_pairs={{0,1},{1,2},{2,3},{3,4},{4,5},{5,6},{6,7},{7,0},{8,9},{9,10},{10,1... | collective-permute-start | bytes 1179656 | tf_op jit(solution)/shard_map/ppermute | solution.py:22
  48.6 15.5 %collective-permute-start.3 = (bf16[384,512]{1,0:T(8,128)(2,1)S(1)}, bf16[384,512]{1,0:T(8,128)(2,1)}, u32[]{:S(2)}, u32[]{:S(2)}) collective-permute-start(bf16[384,512]{1,0:T(8,128)(2,1)S(1)} %get-tuple-element.13), channel_id=1, source_target_pairs={{0,7},{1,0},{2,1},{3,2},{4,3},{5,4},{6,5},{7,6},{8,15},{9,8},{10,9... | collective-permute-start | bytes 1179656 | tf_op jit(solution)/shard_map/ppermute | solution.py:22
  62.1 14.5 %collective-permute-start.4 = (bf16[384,512]{1,0:T(8,128)(2,1)}, bf16[384,512]{1,0:T(8,128)(2,1)}, u32[]{:S(2)}, u32[]{:S(2)}) collective-permute-start(bf16[384,512]{1,0:T(8,128)(2,1)} %collective-permute-done.2), channel_id=1, source_target_pairs={{0,1},{1,2},{2,3},{3,4},{4,5},{5,6},{6,7},{7,0},{8,9},{9,10},{10,1... | collective-permute-start | bytes 1179656 | tf_op jit(solution)/shard_map/ppermute | solution.py:22
  64.1 14.5 %collective-permute-start.5 = (bf16[384,512]{1,0:T(8,128)(2,1)}, bf16[384,512]{1,0:T(8,128)(2,1)}, u32[]{:S(2)}, u32[]{:S(2)}) collective-permute-start(bf16[384,512]{1,0:T(8,128)(2,1)} %collective-permute-done.3), channel_id=1, source_target_pairs={{0,7},{1,0},{2,1},{3,2},{4,3},{5,4},{6,5},{7,6},{8,15},{9,8},{10,9... | collective-permute-start | bytes 1179656 | tf_op jit(solution)/shard_map/ppermute | solution.py:22
  76.6 13.7 %collective-permute-start.6 = (bf16[384,512]{1,0:T(8,128)(2,1)}, bf16[384,512]{1,0:T(8,128)(2,1)S(1)}, u32[]{:S(2)}, u32[]{:S(2)}) collective-permute-start(bf16[384,512]{1,0:T(8,128)(2,1)} %collective-permute-done.4), channel_id=1, source_target_pairs={{0,1},{1,2},{2,3},{3,4},{4,5},{5,6},{6,7},{7,0},{8,9},{9,10},{10,1... | collective-permute-start | bytes 1179656 | tf_op jit(solution)/shard_map/ppermute | solution.py:22
  78.6 13.7 %collective-permute-start.7 = (bf16[384,512]{1,0:T(8,128)(2,1)}, bf16[384,512]{1,0:T(8,128)(2,1)S(1)}, u32[]{:S(2)}, u32[]{:S(2)}) collective-permute-start(bf16[384,512]{1,0:T(8,128)(2,1)} %collective-permute-done.5), channel_id=1, source_target_pairs={{0,7},{1,0},{2,1},{3,2},{4,3},{5,4},{6,5},{7,6},{8,15},{9,8},{10,9... | collective-permute-start | bytes 1179656 | tf_op jit(solution)/shard_map/ppermute | solution.py:22
  90.3 8.4 %collective-permute-start.8 = (bf16[192,512]{1,0:T(8,128)(2,1)S(1)}, bf16[192,512]{1,0:T(8,128)(2,1)S(1)}, u32[]{:S(2)}, u32[]{:S(2)}) collective-permute-start(bf16[192,512]{1,0:T(8,128)(2,1)S(1)} %slice.76), channel_id=1, source_target_pairs={{0,1},{1,2},{2,3},{3,4},{4,5},{5,6},{6,7},{7,0},{8,9},{9,10},{10,1... | collective-permute-start | bytes 589832 | tf_op jit(solution)/shard_map/ppermute | solution.py:22
  92.3 7.2 %collective-permute-start.9 = (bf16[192,512]{1,0:T(8,128)(2,1)S(1)}, bf16[192,512]{1,0:T(8,128)(2,1)S(1)}, u32[]{:S(2)}, u32[]{:S(2)}) collective-permute-start(bf16[192,512]{1,0:T(8,128)(2,1)S(1)} %slice.77), channel_id=1, source_target_pairs={{0,7},{1,0},{2,1},{3,2},{4,3},{5,4},{6,5},{7,6},{8,15},{9,8},{10,9... | collective-permute-start | bytes 589832 | tf_op jit(solution)/shard_map/ppermute | solution.py:22
  115.1 1.0 copy-start.1
  154.3 1.0 copy-start.3
  154.3 1.1 copy-start.5
  154.4 1.2 copy-start.6
Sparse Core Ops, SparseCore 0:
  21.0 85.0 all-gather.1

commit v5 on v4

--- a/solution.py
+++ b/solution.py
@@ -44,38 +44,39 @@
 
 
 def block_kernel(acts_ref, weights_hbm, inv_rms_ref, out_ref, rest_ref, weights_ref, mixed_ref, sems):
-    rows, depth = inv_rms_ref.shape[0], weights_ref.shape[0]
-    hidden = weights_ref.shape[1] // 2
+    rows = inv_rms_ref.shape[0]
+    hidden = weights_ref.shape[-1] // 2
     blocks, kept, width = out_ref.shape
-    chunk = depth // blocks
-    count_y, count_x, count_core = sizes
-    part = depth // (count_y * count_x * count_core)
-    copies = []
-    for y in range(count_y):
-        for core in range(count_core):
-            for x in range(count_x):
-                there = ((y * count_core + core) * count_x + x) * part
-                here = ((y * count_x + x) * count_core + core) * part
-                copies.append(
-                    pltpu.make_async_copy(
-                        weights_hbm.at[pl.ds(there, part)],
-                        weights_ref.at[pl.ds(here, part)],
-                        sems.at[len(copies)],
-                    )
-                )
-    for copy in copies:
-        copy.start()
+    copies = [
+        [
+            pltpu.make_async_copy(
+                weights_hbm.at[y, core], weights_ref.at[y, :, core], sems.at[y, core]
+            )
+            for core in range(weights_hbm.shape[1])
+        ]
+        for y in range(weights_hbm.shape[0])
+    ]
+    for pair in copies:
+        for copy in pair:
+            copy.start()
     per_chunk = len(copies) // blocks
+
+    def chunk(k, columns):
+        own = weights_ref[k * per_chunk : (k + 1) * per_chunk, :, :, :, columns]
+        return own.reshape(width, hidden)
+
+    first, second = slice(0, hidden), slice(hidden, 2 * hidden)
     up_proj = back_proj = jnp.zeros((rows, hidden), jnp.float32)
     for k in range(blocks):
-        for copy in copies[k * per_chunk : (k + 1) * per_chunk]:
-            copy.wait()
-        at = pl.ds(k * chunk, chunk)
+        for pair in copies[k * per_chunk : (k + 1) * per_chunk]:
+            for copy in pair:
+                copy.wait()
+        at = pl.ds(k * width, width)
         up_proj += jnp.dot(
-            acts_ref[:rows, at], weights_ref[at, :hidden], preferred_element_type=jnp.float32
+            acts_ref[:rows, at], chunk(k, first), preferred_element_type=jnp.float32
         )
         back_proj += jnp.dot(
-            acts_ref[rows:, at], weights_ref[at, hidden:], preferred_element_type=jnp.float32
+            acts_ref[rows:, at], chunk(k, second), preferred_element_type=jnp.float32
         )
     up_proj = up_proj * inv_rms_ref[...]
     sigmoid_up = jax.nn.sigmoid(up_proj)
@@ -96,7 +97,7 @@
     for block in range(blocks):
         term = lax.dot_general(
             grad_hidden,
-            weights_ref[pl.ds(block * width, width), :hidden],
+            chunk(block, first),
             (((1,), (1,)), ((), ())),
             preferred_element_type=jnp.float32,
         )
@@ -110,6 +111,8 @@
     rows, depth = gathered.shape[0] // 2, gathered.shape[1]
     hidden = weights.shape[1] // 2
     blocks = depth // width
+    count_y, count_x, count_core = sizes
+    part = depth // (count_y * count_x * count_core)
     return pl.pallas_call(
         block_kernel,
         in_specs=[
@@ -123,9 +126,9 @@
             jax.ShapeDtypeStruct((blocks, rows - kept + 16, width), jnp.bfloat16),
         ],
         scratch_shapes=[
-            pltpu.VMEM(weights.shape, jnp.bfloat16),
+            pltpu.VMEM((count_y, count_x, count_core, part, 2 * hidden), jnp.bfloat16),
             pltpu.VMEM((16, width), jnp.float32),
-            pltpu.SemaphoreType.DMA((sizes[0] * sizes[1] * sizes[2],)),
+            pltpu.SemaphoreType.DMA((count_y, count_core)),
         ],
         compiler_params=pltpu.CompilerParams(vmem_limit_bytes=40 * 1024 * 1024),
         cost_estimate=pl.CostEstimate(
@@ -133,7 +136,7 @@
             bytes_accessed=2 * (2 * rows * depth + 2 * depth * hidden + rows * depth),
             transcendentals=rows * hidden,
         ),
-    )(gathered, weights, inv_rms)
+    )(gathered, weights.reshape(count_y, count_core, count_x, part, 2 * hidden), inv_rms)
 
 
 def body(byte_acts, upstream, segment_ids, first_weight, second_weight):
@@ -197,7 +200,9 @@
     def exchanged(a):
         return lax.all_to_all(a, "tp", split_axis=0, concat_axis=0, tiled=True).astype(jnp.float32)
 
-    terms = exchanged(sent)
+    terms = lax.all_to_all(sent, "tp", split_axis=0, concat_axis=0, tiled=True)
+    terms, rest = lax.optimization_barrier((terms, rest))
+    terms = terms.astype(jnp.float32)
     rest_grad = lax.cond(
         last_slot >= kept - 8,
         lambda a: jnp.sum(exchanged(a), axis=0)[8:],

time: 165 us -> 165 us (level)
  blocking collectives: 51.5 us -> 13.3 us
  waiting for transfers between devices: 26 us -> 58.2 us
  starting transfers between devices: 40.3 us -> 47.4 us
    all_to_all x1 -> x0, blocking collectives: 38.2 us -> none  [exchanged(): lax.all_to_all(a, 'tp', split_axis=0, concat_axis=0, tiled=True)]
    all_to_all x0 -> x1, waiting for transfers between devices: none -> 32 us  [body(): terms = lax.all_to_all(sent, 'tp', split_axis=0, concat_axis=0, tiled=True)]
    all_to_all x0 -> x1, starting transfers between devices: none -> 7.1 us  [body(): terms = lax.all_to_all(sent, 'tp', split_axis=0, concat_axis=0, tiled=True)]
  transfers between devices with their start and end apart: 11 -> 12, of which waited for: 6 -> 7; matrix products, arithmetic and copies ran while one was open for 9% -> 9% of each run, Pallas kernels for 0% -> 0%
where the time goes in v5:
time: 165 us
  waiting for transfers between devices  58.2 us (35%)
  starting transfers between devices  47.4 us (29%)
  between operations  17.8 us (11%)
  blocking collectives  13.3 us (8%)
  local copies, waits for them, and re-layouts  11.3 us (7%)
  Pallas kernels  8.53 us (5%)
  other arithmetic  5.02 us (3%)
  matrix products  2.86 us (2%)
    all_to_all x1, waiting for transfers between devices, body(): terms = lax.all_to_all(sent, 'tp', split_axis=0, concat_axis=0, tiled=True)  32 us
    ppermute x8, starting transfers between devices, turned(): lax.ppermute(shard, 'tp', [(i, (i + by) % count) for i in range(count)])  28.2 us
    ppermute x8, waiting for transfers between devices, turned(): lax.ppermute(shard, 'tp', [(i, (i + by) % count) for i in range(count)])  20.1 us
    all_gather x1, blocking collectives, body(): weights = lax.all_gather(weights, 'x', axis=0, tiled=True)  13.3 us
    ppermute x2, starting transfers between devices, shifted(): return lax.ppermute(shard, axis, pairs)  12 us
    pallas_call x1, Pallas kernels, block_terms(): pl.pallas_call(block_kernel, in_specs=[pl.BlockSpec(memory_space=pltpu.VM...  8.53 us
    all_to_all x1, starting transfers between devices, body(): terms = lax.all_to_all(sent, 'tp', split_axis=0, concat_axis=0, tiled=True)  7.1 us
    all_gather x1, waiting for transfers between devices, body(): weights = lax.all_gather(weights, ('y', 'core'), axis=0, tiled=True)  6.09 us
  transfers between devices with their start and end apart: 12, of which 7 were waited for; matrix products, arithmetic and copies ran while one was open for 9% of the time, Pallas kernels for 0%

profile of v5, /device:TPU:1, one launch (start us, length us, event | category | flops | bytes accessed | tf_op | source)
XLA Modules:
  0.0 164.6 jit_solution(11197979638270376635)
XLA Ops:
  6.5 1.0 pad_maximum_fusion.1
  7.5 13.3 %all_gather.6 = bf16[256,1536]{1,0:T(8,128)(2,1)} all-gather(bf16[64,1536]{1,0:T(8,128)(2,1)S(1)} %pad_maximum_fusion.1), channel_id=1, replica_groups=mesh['y'=8,'x'=4,'core'=2,'tp'=8] {'x'}, dimensions={0}, use_global_device_ids=true | all-gather | bytes 983040 | tf_op jit(solution)/shard_map/all_gather | solution.py:147
  20.9 1.4 fusion.34
  24.2 1.3 broadcast_subtract_fusion
  27.3 1.3 fusion.18
  28.6 10.1 %collective-permute-start = (f32[1,1280]{1,0:T(1,128)S(1)}, f32[1,1280]{1,0:T(1,128)S(1)}, u32[]{:S(2)}, u32[]{:S(2)}) collective-permute-start(f32[1,1280]{1,0:T(1,128)S(1)} %reshape_maximum_fusion.2), channel_id=1, source_target_pairs={{8,0},{16,8},{24,16},{32,24},{40,32},{48,40},{56,48},{64,56},{72,6... | collective-permute-start | bytes 15368 | tf_op jit(solution)/shard_map/ppermute | solution.py:17
  39.3 0.7 add.164
  40.1 1.9 %collective-permute-start.1 = (f32[1,1280]{1,0:T(1,128)S(1)}, f32[1,1280]{1,0:T(1,128)S(1)}, u32[]{:S(2)}, u32[]{:S(2)}) collective-permute-start(f32[1,1280]{1,0:T(1,128)S(1)} %reshape_maximum_fusion), channel_id=1, source_target_pairs={{0,8},{8,16},{16,24},{24,32},{32,40},{40,48},{48,56},{56,64},{64,7... | collective-permute-start | bytes 15368 | tf_op jit(solution)/shard_map/ppermute | solution.py:17
  44.6 1.3 add_maximum_fusion
  46.6 1.9 %collective-permute-start.2 = (bf16[384,512]{1,0:T(8,128)(2,1)S(1)}, bf16[384,512]{1,0:T(8,128)(2,1)}, u32[]{:S(2)}, u32[]{:S(2)}) collective-permute-start(bf16[384,512]{1,0:T(8,128)(2,1)S(1)} %get-tuple-element.17), channel_id=1, source_target_pairs={{0,1},{1,2},{2,3},{3,4},{4,5},{5,6},{6,7},{7,0},{8,9},{9,10},{10,1... | collective-permute-start | bytes 1179656 | tf_op jit(solution)/shard_map/ppermute | solution.py:22
  48.5 6.5 %collective-permute-start.3 = (bf16[384,512]{1,0:T(8,128)(2,1)S(1)}, bf16[384,512]{1,0:T(8,128)(2,1)}, u32[]{:S(2)}, u32[]{:S(2)}) collective-permute-start(bf16[384,512]{1,0:T(8,128)(2,1)S(1)} %get-tuple-element.17), channel_id=1, source_target_pairs={{0,7},{1,0},{2,1},{3,2},{4,3},{5,4},{6,5},{7,6},{8,15},{9,8},{10,9... | collective-permute-start | bytes 1179656 | tf_op jit(solution)/shard_map/ppermute | solution.py:22
  55.1 7.0 %collective-permute-done.2 = bf16[384,512]{1,0:T(8,128)(2,1)} collective-permute-done((bf16[384,512]{1,0:T(8,128)(2,1)S(1)}, bf16[384,512]{1,0:T(8,128)(2,1)}, u32[]{:S(2)}, u32[]{:S(2)}) %collective-permute-start.2) | collective-permute-done | bytes 393248 | tf_op jit(solution)/shard_map/ppermute | solution.py:22
  62.1 1.9 %collective-permute-start.4 = (bf16[384,512]{1,0:T(8,128)(2,1)}, bf16[384,512]{1,0:T(8,128)(2,1)}, u32[]{:S(2)}, u32[]{:S(2)}) collective-permute-start(bf16[384,512]{1,0:T(8,128)(2,1)} %collective-permute-done.2), channel_id=1, source_target_pairs={{0,1},{1,2},{2,3},{3,4},{4,5},{5,6},{6,7},{7,0},{8,9},{9,10},{10,1... | collective-permute-start | bytes 1179656 | tf_op jit(solution)/shard_map/ppermute | solution.py:22
  64.0 4.8 %collective-permute-start.5 = (bf16[384,512]{1,0:T(8,128)(2,1)}, bf16[384,512]{1,0:T(8,128)(2,1)}, u32[]{:S(2)}, u32[]{:S(2)}) collective-permute-start(bf16[384,512]{1,0:T(8,128)(2,1)} %collective-permute-done.3), channel_id=1, source_target_pairs={{0,7},{1,0},{2,1},{3,2},{4,3},{5,4},{6,5},{7,6},{8,15},{9,8},{10,9... | collective-permute-start | bytes 1179656 | tf_op jit(solution)/shard_map/ppermute | solution.py:22
  68.9 7.7 %collective-permute-done.4 = bf16[384,512]{1,0:T(8,128)(2,1)} collective-permute-done((bf16[384,512]{1,0:T(8,128)(2,1)}, bf16[384,512]{1,0:T(8,128)(2,1)}, u32[]{:S(2)}, u32[]{:S(2)}) %collective-permute-start.4) | collective-permute-done | bytes 393248 | tf_op jit(solution)/shard_map/ppermute | solution.py:22
  76.6 1.9 %collective-permute-start.6 = (bf16[384,512]{1,0:T(8,128)(2,1)}, bf16[384,512]{1,0:T(8,128)(2,1)S(1)}, u32[]{:S(2)}, u32[]{:S(2)}) collective-permute-start(bf16[384,512]{1,0:T(8,128)(2,1)} %collective-permute-done.4), channel_id=1, source_target_pairs={{0,1},{1,2},{2,3},{3,4},{4,5},{5,6},{6,7},{7,0},{8,9},{9,10},{10,1... | collective-permute-start | bytes 1179656 | tf_op jit(solution)/shard_map/ppermute | solution.py:22
  78.5 4.6 %collective-permute-start.7 = (bf16[384,512]{1,0:T(8,128)(2,1)}, bf16[384,512]{1,0:T(8,128)(2,1)S(1)}, u32[]{:S(2)}, u32[]{:S(2)}) collective-permute-start(bf16[384,512]{1,0:T(8,128)(2,1)} %collective-permute-done.5), channel_id=1, source_target_pairs={{0,7},{1,0},{2,1},{3,2},{4,3},{5,4},{6,5},{7,6},{8,15},{9,8},{10,9... | collective-permute-start | bytes 1179656 | tf_op jit(solution)/shard_map/ppermute | solution.py:22
  83.1 1.0 constant_dynamic-update-slice_fusion.6
  84.2 1.1 constant_dynamic-update-slice_fusion.5
  85.2 1.0 constant_dynamic-update-slice_fusion.4
  86.3 1.1 constant_dynamic-update-slice_fusion.3
  87.4 2.9 %collective-permute-done.6 = bf16[384,512]{1,0:T(8,128)(2,1)S(1)} collective-permute-done((bf16[384,512]{1,0:T(8,128)(2,1)}, bf16[384,512]{1,0:T(8,128)(2,1)S(1)}, u32[]{:S(2)}, u32[]{:S(2)}) %collective-permute-start.6) | collective-permute-done | bytes 393248 | tf_op jit(solution)/shard_map/ppermute | solution.py:22
  90.3 1.9 %collective-permute-start.8 = (bf16[192,512]{1,0:T(8,128)(2,1)S(1)}, bf16[192,512]{1,0:T(8,128)(2,1)S(1)}, u32[]{:S(2)}, u32[]{:S(2)}) collective-permute-start(bf16[192,512]{1,0:T(8,128)(2,1)S(1)} %slice.76), channel_id=1, source_target_pairs={{0,1},{1,2},{2,3},{3,4},{4,5},{5,6},{6,7},{7,0},{8,9},{9,10},{10,1... | collective-permute-start | bytes 589832 | tf_op jit(solution)/shard_map/ppermute | solution.py:22
  92.2 4.6 %collective-permute-start.9 = (bf16[192,512]{1,0:T(8,128)(2,1)S(1)}, bf16[192,512]{1,0:T(8,128)(2,1)S(1)}, u32[]{:S(2)}, u32[]{:S(2)}) collective-permute-start(bf16[192,512]{1,0:T(8,128)(2,1)S(1)} %slice.77), channel_id=1, source_target_pairs={{0,7},{1,0},{2,1},{3,2},{4,3},{5,4},{6,5},{7,6},{8,15},{9,8},{10,9... | collective-permute-start | bytes 589832 | tf_op jit(solution)/shard_map/ppermute | solution.py:22
  96.9 1.8 %collective-permute-done.8 = bf16[192,512]{1,0:T(8,128)(2,1)S(1)} collective-permute-done((bf16[192,512]{1,0:T(8,128)(2,1)S(1)}, bf16[192,512]{1,0:T(8,128)(2,1)S(1)}, u32[]{:S(2)}, u32[]{:S(2)}) %collective-permute-start.8) | collective-permute-done | bytes 196640 | tf_op jit(solution)/shard_map/ppermute | solution.py:22
  98.7 0.7 collective-permute-done.9
  100.0 6.1 %all-gather.2.cloned.1.call-done = bf16[4096,1536]{1,0:T(8,128)(2,1)} async-done(((bf16[256,1536]{1,0:T(8,128)(2,1)}), bf16[4096,1536]{1,0:T(8,128)(2,1)}) %all-gather.2.cloned.1.call-update) | async-done | bytes 12582928 | tf_op jit(solution)/shard_map/all_gather | solution.py:148
  106.1 8.5 %shard_map.55 = (bf16[8,144,512]{2,1,0:T(8,128)(2,1)S(1)}, bf16[8,64,512]{2,1,0:T(8,128)(2,1)}) custom-call(bf16[384,4096]{1,0:T(8,128)(2,1)S(1)} %constant_dynamic-update-slice_fusion.8.acts_ref, bf16[8,2,4,64,1536]{4,3,2,1,0:T(8,128)(2,1)} %bitcast.16, f32[192,1]{1,0:T(8,128)S(1)} %copy.7.inv_rms_ref), custom_call_target="tpu_custom_call" | custom-call | flops 3623878656 | bytes 17301504 | tf_op jit(solution)/shard_map/pallas_call | solution.py:116
  114.6 1.0 copy-done.1
  115.7 7.1 %all-to-all-start.1 = ((bf16[8,144,512]{2,1,0:T(8,128)(2,1)}), bf16[8,144,512]{2,1,0:T(8,128)(2,1)S(1)}, u32[]{:S(2)}, u32[]{:S(2)}) async-start(bf16[8,144,512]{2,1,0:T(8,128)(2,1)} %copy-done.1), calls=%async_computation.1 | async-start | bytes 2359296 | tf_op jit(solution)/shard_map/all_to_all | solution.py:203
  122.8 32.0 %all-to-all-done.1 = bf16[8,144,512]{2,1,0:T(8,128)(2,1)S(1)} async-done(((bf16[8,144,512]{2,1,0:T(8,128)(2,1)}), bf16[8,144,512]{2,1,0:T(8,128)(2,1)S(1)}, u32[]{:S(2)}, u32[]{:S(2)}) %all-to-all-start.1) | async-done | bytes 1179680 | tf_op jit(solution)/shard_map/all_to_all | solution.py:203
  156.3 1.4 fusion
  (59 shorter events, 5.7 us)
Async XLA Ops:
  6.5 20.5 %copy-start = (bf16[192,512]{1,0:T(8,128)(2,1)S(1)}, bf16[192,512]{1,0:T(8,128)(2,1)}, u32[]{:S(2)}) copy-start(bf16[192,512]{1,0:T(8,128)(2,1)} %param.7) | copy-start | bytes 589828
  6.5 99.6 %all-gather.2.cloned.1.call-start = ((), (), s32[]{:S(2)}) async-start(), calls=%async_computation.2 | async-start | bytes 13369344 | tf_op jit(solution)/shard_map/all_gather | solution.py:148
  27.2 18.9 %copy-start.2 = (f32[192,512]{1,0:T(8,128)}, f32[192,512]{1,0:T(8,128)S(1)}, u32[]{:S(2)}) copy-start(f32[192,512]{1,0:T(8,128)S(1)} %fusion.17) | copy-start | bytes 1179652
  28.5 17.6 %copy-start.4 = (f32[192,512]{1,0:T(8,128)}, f32[192,512]{1,0:T(8,128)S(1)}, u32[]{:S(2)}) copy-start(f32[192,512]{1,0:T(8,128)S(1)} %fusion.18) | copy-start | bytes 1179652
  28.6 13.4 %collective-permute-start = (f32[1,1280]{1,0:T(1,128)S(1)}, f32[1,1280]{1,0:T(1,128)S(1)}, u32[]{:S(2)}, u32[]{:S(2)}) collective-permute-start(f32[1,1280]{1,0:T(1,128)S(1)} %reshape_maximum_fusion.2), channel_id=1, source_target_pairs={{8,0},{16,8},{24,16},{32,24},{40,32},{48,40},{56,48},{64,56},{72,6... | collective-permute-start | bytes 15368 | tf_op jit(solution)/shard_map/ppermute | solution.py:17
  40.1 3.2 %collective-permute-start.1 = (f32[1,1280]{1,0:T(1,128)S(1)}, f32[1,1280]{1,0:T(1,128)S(1)}, u32[]{:S(2)}, u32[]{:S(2)}) collective-permute-start(f32[1,1280]{1,0:T(1,128)S(1)} %reshape_maximum_fusion), channel_id=1, source_target_pairs={{0,8},{8,16},{16,24},{24,32},{32,40},{40,48},{48,56},{56,64},{64,7... | collective-permute-start | bytes 15368 | tf_op jit(solution)/shard_map/ppermute | solution.py:17
  46.6 15.5 %collective-permute-start.2 = (bf16[384,512]{1,0:T(8,128)(2,1)S(1)}, bf16[384,512]{1,0:T(8,128)(2,1)}, u32[]{:S(2)}, u32[]{:S(2)}) collective-permute-start(bf16[384,512]{1,0:T(8,128)(2,1)S(1)} %get-tuple-element.17), channel_id=1, source_target_pairs={{0,1},{1,2},{2,3},{3,4},{4,5},{5,6},{6,7},{7,0},{8,9},{9,10},{10,1... | collective-permute-start | bytes 1179656 | tf_op jit(solution)/shard_map/ppermute | solution.py:22
  48.5 15.5 %collective-permute-start.3 = (bf16[384,512]{1,0:T(8,128)(2,1)S(1)}, bf16[384,512]{1,0:T(8,128)(2,1)}, u32[]{:S(2)}, u32[]{:S(2)}) collective-permute-start(bf16[384,512]{1,0:T(8,128)(2,1)S(1)} %get-tuple-element.17), channel_id=1, source_target_pairs={{0,7},{1,0},{2,1},{3,2},{4,3},{5,4},{6,5},{7,6},{8,15},{9,8},{10,9... | collective-permute-start | bytes 1179656 | tf_op jit(solution)/shard_map/ppermute | solution.py:22
  62.1 14.5 %collective-permute-start.4 = (bf16[384,512]{1,0:T(8,128)(2,1)}, bf16[384,512]{1,0:T(8,128)(2,1)}, u32[]{:S(2)}, u32[]{:S(2)}) collective-permute-start(bf16[384,512]{1,0:T(8,128)(2,1)} %collective-permute-done.2), channel_id=1, source_target_pairs={{0,1},{1,2},{2,3},{3,4},{4,5},{5,6},{6,7},{7,0},{8,9},{9,10},{10,1... | collective-permute-start | bytes 1179656 | tf_op jit(solution)/shard_map/ppermute | solution.py:22
  64.0 14.5 %collective-permute-start.5 = (bf16[384,512]{1,0:T(8,128)(2,1)}, bf16[384,512]{1,0:T(8,128)(2,1)}, u32[]{:S(2)}, u32[]{:S(2)}) collective-permute-start(bf16[384,512]{1,0:T(8,128)(2,1)} %collective-permute-done.3), channel_id=1, source_target_pairs={{0,7},{1,0},{2,1},{3,2},{4,3},{5,4},{6,5},{7,6},{8,15},{9,8},{10,9... | collective-permute-start | bytes 1179656 | tf_op jit(solution)/shard_map/ppermute | solution.py:22
  76.6 13.7 %collective-permute-start.6 = (bf16[384,512]{1,0:T(8,128)(2,1)}, bf16[384,512]{1,0:T(8,128)(2,1)S(1)}, u32[]{:S(2)}, u32[]{:S(2)}) collective-permute-start(bf16[384,512]{1,0:T(8,128)(2,1)} %collective-permute-done.4), channel_id=1, source_target_pairs={{0,1},{1,2},{2,3},{3,4},{4,5},{5,6},{6,7},{7,0},{8,9},{9,10},{10,1... | collective-permute-start | bytes 1179656 | tf_op jit(solution)/shard_map/ppermute | solution.py:22
  78.5 13.7 %collective-permute-start.7 = (bf16[384,512]{1,0:T(8,128)(2,1)}, bf16[384,512]{1,0:T(8,128)(2,1)S(1)}, u32[]{:S(2)}, u32[]{:S(2)}) collective-permute-start(bf16[384,512]{1,0:T(8,128)(2,1)} %collective-permute-done.5), channel_id=1, source_target_pairs={{0,7},{1,0},{2,1},{3,2},{4,3},{5,4},{6,5},{7,6},{8,15},{9,8},{10,9... | collective-permute-start | bytes 1179656 | tf_op jit(solution)/shard_map/ppermute | solution.py:22
  90.3 8.4 %collective-permute-start.8 = (bf16[192,512]{1,0:T(8,128)(2,1)S(1)}, bf16[192,512]{1,0:T(8,128)(2,1)S(1)}, u32[]{:S(2)}, u32[]{:S(2)}) collective-permute-start(bf16[192,512]{1,0:T(8,128)(2,1)S(1)} %slice.76), channel_id=1, source_target_pairs={{0,1},{1,2},{2,3},{3,4},{4,5},{5,6},{6,7},{7,0},{8,9},{9,10},{10,1... | collective-permute-start | bytes 589832 | tf_op jit(solution)/shard_map/ppermute | solution.py:22
  92.2 7.2 %collective-permute-start.9 = (bf16[192,512]{1,0:T(8,128)(2,1)S(1)}, bf16[192,512]{1,0:T(8,128)(2,1)S(1)}, u32[]{:S(2)}, u32[]{:S(2)}) collective-permute-start(bf16[192,512]{1,0:T(8,128)(2,1)S(1)} %slice.77), channel_id=1, source_target_pairs={{0,7},{1,0},{2,1},{3,2},{4,3},{5,4},{6,5},{7,6},{8,15},{9,8},{10,9... | collective-permute-start | bytes 589832 | tf_op jit(solution)/shard_map/ppermute | solution.py:22
  114.6 1.1 copy-start.1
  115.7 39.1 %all-to-all-start.1 = ((bf16[8,144,512]{2,1,0:T(8,128)(2,1)}), bf16[8,144,512]{2,1,0:T(8,128)(2,1)S(1)}, u32[]{:S(2)}, u32[]{:S(2)}) async-start(bf16[8,144,512]{2,1,0:T(8,128)(2,1)} %copy-done.1), calls=%async_computation.1 | async-start | bytes 2359296 | tf_op jit(solution)/shard_map/all_to_all | solution.py:203
  122.8 32.7 %copy-start.6 = (bf16[8,64,512]{2,1,0:T(8,128)(2,1)S(1)}, bf16[8,64,512]{2,1,0:T(8,128)(2,1)}, u32[]{:S(2)}) copy-start(bf16[8,64,512]{2,1,0:T(8,128)(2,1)} %get-tuple-element.16) | copy-start | bytes 1572868
  155.1 1.0 copy-start.3
  155.2 1.1 copy-start.5
  155.2 1.2 copy-start.7
Sparse Core Ops, SparseCore 0:
  21.0 85.0 all-gather.1

commit v6 on v5

--- a/solution.py
+++ b/solution.py
@@ -1,3 +1,5 @@
+import functools
+
 import jax
 import jax.numpy as jnp
 from jax import lax
@@ -43,7 +45,9 @@
     return put(whole, bottom, half, me + count // 2)
 
 
-def block_kernel(acts_ref, weights_hbm, inv_rms_ref, out_ref, rest_ref, weights_ref, mixed_ref, sems):
+def block_kernel(
+    acts_ref, weights_hbm, inv_rms_ref, out_hbm, rest_hbm, weights_ref, mixed_ref, out_ref, rest_ref, sems, out_sems
+):
     rows = inv_rms_ref.shape[0]
     hidden = weights_ref.shape[-1] // 2
     blocks, kept, width = out_ref.shape
@@ -94,6 +98,7 @@
     mixed_ref[...] = jnp.zeros_like(mixed_ref)
     mixed_ref[8:, :rows] = jnp.concatenate([high, dots - high], axis=0)
     even = kept - 16
+    results = []
     for block in range(blocks):
         term = lax.dot_general(
             grad_hidden,
@@ -105,6 +110,12 @@
         out_ref[block, :even] = term[:even].astype(jnp.bfloat16)
         out_ref[block, even:] = mixed_ref[...].astype(jnp.bfloat16)
         rest_ref[block] = term[even:].astype(jnp.bfloat16)
+        results.append(pltpu.make_async_copy(out_ref.at[block], out_hbm.at[block], out_sems.at[0, block]))
+        results.append(pltpu.make_async_copy(rest_ref.at[block], rest_hbm.at[block], out_sems.at[1, block]))
+        results[-2].start()
+        results[-1].start()
+    for copy in results:
+        copy.wait()
 
 
 def block_terms(gathered, weights, inv_rms, width, kept):
@@ -120,15 +131,18 @@
             pl.BlockSpec(memory_space=pl.ANY),
             pl.BlockSpec(memory_space=pltpu.VMEM),
         ],
-        out_specs=[pl.BlockSpec(memory_space=pltpu.VMEM)] * 2,
+        out_specs=[pl.BlockSpec(memory_space=pltpu.HBM)] * 2,
         out_shape=[
-            pltpu.VMEM((blocks, kept, width), jnp.bfloat16),
+            jax.ShapeDtypeStruct((blocks, kept, width), jnp.bfloat16),
             jax.ShapeDtypeStruct((blocks, rows - kept + 16, width), jnp.bfloat16),
         ],
         scratch_shapes=[
             pltpu.VMEM((count_y, count_x, count_core, part, 2 * hidden), jnp.bfloat16),
             pltpu.VMEM((16, width), jnp.float32),
+            pltpu.VMEM((blocks, kept, width), jnp.bfloat16),
+            pltpu.VMEM((blocks, rows - kept + 16, width), jnp.bfloat16),
             pltpu.SemaphoreType.DMA((count_y, count_core)),
+            pltpu.SemaphoreType.DMA((2, blocks)),
         ],
         compiler_params=pltpu.CompilerParams(vmem_limit_bytes=40 * 1024 * 1024),
         cost_estimate=pl.CostEstimate(
@@ -139,57 +153,142 @@
     )(gathered, weights.reshape(count_y, count_core, count_x, part, 2 * hidden), inv_rms)
 
 
+def sums_kernel(ids_ref, ids_row_ref, acts_ref, upstream_ref, seg_ref, grad_ref, count_ref, first_ref, last_ref):
+    rows, width = acts_ref.shape
+    base_id, last_id = ids_ref[0], ids_ref[rows - 1]
+    slot = lax.broadcasted_iota(jnp.int32, (rows, rows), 0)
+    member = (slot == ids_row_ref[...] - base_id).astype(jnp.float32)
+    member_b = member.astype(jnp.bfloat16)
+    seg_ref[...] = jnp.dot(member_b, acts_ref[...], preferred_element_type=jnp.float32)
+    grad_ref[...] = jnp.dot(member_b, upstream_ref[...], preferred_element_type=jnp.float32)
+    count_ref[...] = jnp.sum(member, axis=1, keepdims=True)
+    for edge_ref, at, segment in ((first_ref, 0, base_id), (last_ref, last_id - base_id, last_id)):
+        edge_ref[:, :width] = seg_ref[pl.ds(at, 1), :]
+        edge_ref[:, width : 2 * width] = grad_ref[pl.ds(at, 1), :]
+        count = jnp.sum(jnp.where(slot[:, :1] == at, count_ref[...], 0.0), axis=0, keepdims=True)
+        edge_ref[:, 2 * width : 2 * width + 128] = jnp.broadcast_to(count, (1, 128))
+        edge_ref[:, 2 * width + 128 :] = jnp.full((1, 128), (segment + 1).astype(jnp.float32))
+
+
+def joined_kernel(
+    ids_ref, seg_ref, grad_ref, count_ref, tail_ref, head_ref, both_ref, pooled_ref, sums_ref, safe_ref
+):
+    rows, width = seg_ref.shape
+    base_id, last_id = ids_ref[0], ids_ref[rows - 1]
+    slot = lax.broadcasted_iota(jnp.int32, (rows, 1), 0)
+
+    def pick(edge_ref, at, segment):
+        matched = edge_ref[:, 2 * width + 128 : 2 * width + 129] == (segment + 1).astype(jnp.float32)
+        return jnp.where((slot == at) & matched, 1.0, 0.0)
+
+    tail_pick = pick(tail_ref, last_id - base_id, last_id)
+    head_pick = pick(head_ref, 0, base_id)
+
+    def joined(own_ref, at):
+        return own_ref[...] + tail_pick * tail_ref[:, at] + head_pick * head_ref[:, at]
+
+    counts = joined(count_ref, slice(2 * width, 2 * width + 1))
+    safe = jnp.maximum(counts, 1.0)
+    pooled = joined(seg_ref, slice(0, width)) / safe
+    sums = joined(grad_ref, slice(width, 2 * width))
+    both_ref[:rows] = pooled.astype(jnp.bfloat16)
+    both_ref[rows:] = sums.astype(jnp.bfloat16)
+    pooled_ref[...] = pooled
+    sums_ref[...] = sums
+    safe_ref[...] = safe
+
+
+def last_kernel(
+    model_width,
+    ids_ref,
+    ids_column_ref,
+    terms_ref,
+    rest_ref,
+    pooled_ref,
+    sums_ref,
+    safe_ref,
+    inv_rms_ref,
+    upstream_ref,
+    out_ref,
+    share_ref,
+):
+    rows = pooled_ref.shape[0]
+    blocks, kept, _ = terms_ref.shape
+    even = kept - 16
+    norm_grad = terms_ref[0, :even].astype(jnp.float32)
+    mixed = terms_ref[0, even:].astype(jnp.float32)
+    for block in range(1, blocks):
+        norm_grad += terms_ref[block, :even].astype(jnp.float32)
+        mixed += terms_ref[block, even:].astype(jnp.float32)
+    dots = mixed[8:9, :rows] + mixed[12:13, :rows]
+    slot = lax.broadcasted_iota(jnp.int32, (rows, rows), 1)
+    diagonal = lax.broadcasted_iota(jnp.int32, (rows, rows), 0) == slot
+    norm_dot = jnp.sum(jnp.where(diagonal, dots, 0.0), axis=1, keepdims=True)
+
+    def share(at, norm_grad):
+        inv_rms = inv_rms_ref[at]
+        normed = pooled_ref[at] * inv_rms
+        mean = norm_dot[at] * (1.0 / model_width)
+        pooled_grad = sums_ref[at] + inv_rms * (norm_grad - normed * mean)
+        share_ref[at] = pooled_grad / safe_ref[at]
+
+    share(slice(0, even), norm_grad)
+    share(slice(even, even + 8), mixed[:8])
+    share(slice(even + 8, rows), rest_ref[...])
+    member = (slot == ids_column_ref[...] - ids_ref[0]).astype(jnp.float32).astype(jnp.bfloat16)
+    left = share_ref[...]
+    spread = upstream_ref[...].astype(jnp.float32)
+    parts = []
+    for _ in range(3):
+        part = left.astype(jnp.bfloat16)
+        left = left - part.astype(jnp.float32)
+        parts.append(jnp.dot(member, part, preferred_element_type=jnp.float32))
+    out_ref[...] = (spread + ((parts[2] + parts[1]) + parts[0])).astype(jnp.bfloat16)
+
+
+def on_core(kernel, out_shape, *operands, scratch=()):
+    vmem = pl.BlockSpec(memory_space=pltpu.VMEM)
+    return pl.pallas_call(
+        kernel,
+        in_specs=[pl.BlockSpec(memory_space=pltpu.SMEM)] + [vmem] * (len(operands) - 1),
+        out_specs=jax.tree.map(lambda _: vmem, out_shape),
+        out_shape=out_shape,
+        scratch_shapes=scratch,
+        compiler_params=pltpu.CompilerParams(vmem_limit_bytes=24 * 1024 * 1024),
+    )(*operands)
+
+
 def body(byte_acts, upstream, segment_ids, first_weight, second_weight):
-    byte_rows = segment_ids.shape[0]
-    width = byte_acts.shape[1]
+    byte_rows, width = byte_acts.shape
     model_width = width * lax.axis_size("tp")
     weights = jnp.concatenate([first_weight, second_weight], axis=1)
     weights = lax.all_gather(weights, "x", axis=0, tiled=True)
     weights = lax.all_gather(weights, ("y", "core"), axis=0, tiled=True)
 
-    base_id = segment_ids[0]
-    last_id = segment_ids[byte_rows - 1]
-    slot_of = segment_ids - base_id
-    slot_index = jnp.arange(byte_rows, dtype=jnp.int32)
-    member = slot_index[:, None] == slot_of[None, :]
-    member_b = member.astype(jnp.bfloat16)
-    seg_sums = jnp.dot(member_b, byte_acts, preferred_element_type=jnp.float32)
-    grad_sums = jnp.dot(member_b, upstream, preferred_element_type=jnp.float32)
-    counts = jnp.sum(member.astype(jnp.float32), axis=1)
-
-    last_slot = last_id - base_id
-
-    def packed(slot, segment):
-        at = lambda a: lax.dynamic_slice_in_dim(a, slot, 1, 0)
-        tag = jnp.zeros((1, 128), jnp.float32) + (segment + 1).astype(jnp.float32)
-        count = jnp.zeros((1, 128), jnp.float32) + at(counts)
-        return jnp.concatenate([at(seg_sums), at(grad_sums), count, tag], axis=1)
-
-    tail = shifted(packed(0, base_id), seq, -1)
-    head = shifted(packed(last_slot, last_id), seq, 1)
-
-    def pick(slot, segment, row):
-        matched = row[0, 2 * width + 128] == (segment + 1).astype(jnp.float32)
-        return ((slot_index == slot) & matched).astype(jnp.float32)
-
-    tail_pick, head_pick = pick(last_slot, last_id, tail), pick(0, base_id, head)
-
-    def joined(own, begin, end):
-        return (
-            own
-            + tail_pick[:, None] * tail[:, begin:end]
-            + head_pick[:, None] * head[:, begin:end]
-        )
-
-    seg_sums = joined(seg_sums, 0, width)
-    grad_sums = joined(grad_sums, width, 2 * width)
-    counts = counts + tail_pick * tail[0, 2 * width] + head_pick * head[0, 2 * width]
-    safe_counts = jnp.maximum(counts, 1.0)
-    pooled = seg_sums / safe_counts[:, None]
-
-    gathered = ring_gather(
-        jnp.concatenate([pooled.astype(jnp.bfloat16), grad_sums.astype(jnp.bfloat16)], axis=0)
-    )
+    def array(rows, columns, dtype=jnp.float32):
+        return jax.ShapeDtypeStruct((rows, columns), dtype)
+
+    whole, column, edge = array(byte_rows, width), array(byte_rows, 1), array(1, 2 * width + 256)
+    seg_sums, grad_sums, counts, first, last = on_core(
+        sums_kernel,
+        [whole, whole, column, edge, edge],
+        segment_ids,
+        segment_ids.reshape(1, byte_rows),
+        byte_acts,
+        upstream,
+    )
+    tail, head = shifted(first, seq, -1), shifted(last, seq, 1)
+    both, pooled, grad_sums, safe_counts = on_core(
+        joined_kernel,
+        [array(2 * byte_rows, width, jnp.bfloat16), whole, whole, column],
+        segment_ids,
+        seg_sums,
+        grad_sums,
+        counts,
+        tail,
+        head,
+    )
+    gathered = ring_gather(both)
     pooled_b = gathered[:byte_rows]
     square_sums = jnp.sum(jnp.square(pooled_b.astype(jnp.float32)), axis=1)
     inv_rms = lax.rsqrt(square_sums / model_width + epsilon)[:, None]
@@ -198,33 +297,29 @@
     sent, rest = block_terms(gathered, weights, inv_rms, width, kept)
 
     def exchanged(a):
-        return lax.all_to_all(a, "tp", split_axis=0, concat_axis=0, tiled=True).astype(jnp.float32)
-
-    terms = lax.all_to_all(sent, "tp", split_axis=0, concat_axis=0, tiled=True)
-    terms, rest = lax.optimization_barrier((terms, rest))
-    terms = terms.astype(jnp.float32)
+        return lax.all_to_all(a, "tp", split_axis=0, concat_axis=0, tiled=True)
+
+    terms, rest = lax.optimization_barrier((exchanged(sent), rest))
     rest_grad = lax.cond(
-        last_slot >= kept - 8,
-        lambda a: jnp.sum(exchanged(a), axis=0)[8:],
+        segment_ids[byte_rows - 1] - segment_ids[0] >= kept - 8,
+        lambda a: jnp.sum(exchanged(a).astype(jnp.float32), axis=0)[8:],
         lambda a: jnp.zeros((byte_rows - kept + 8, width), jnp.float32),
         rest,
     )
-    norm_grad = jnp.concatenate([jnp.sum(terms[:, : kept - 8], axis=0), rest_grad], axis=0)
-    norm_dot = jnp.sum(
-        terms[:, kept - 8, :byte_rows] + terms[:, kept - 4, :byte_rows], axis=0
-    )
-    normed = pooled * inv_rms
-    pooled_grad = grad_sums + inv_rms * (
-        norm_grad - normed * (norm_dot / model_width)[:, None]
-    )
-    byte_share = pooled_grad / safe_counts[:, None]
-    spread = jnp.dot(
-        member.astype(jnp.float32).T,
-        byte_share,
-        precision=lax.Precision.HIGHEST,
-        preferred_element_type=jnp.float32,
-    )
-    return (upstream.astype(jnp.float32) + spread).astype(jnp.bfloat16)
+    return on_core(
+        functools.partial(last_kernel, model_width),
+        array(byte_rows, width, jnp.bfloat16),
+        segment_ids,
+        segment_ids.reshape(byte_rows, 1),
+        terms,
+        rest_grad,
+        pooled,
+        grad_sums,
+        safe_counts,
+        inv_rms,
+        upstream,
+        scratch=[pltpu.VMEM((byte_rows, width), jnp.float32)],
+    )
 
 
 def solution(mesh):

time: 165 us -> 167 us (1.012)
  Pallas kernels: 8.53 us -> 14.9 us
  waiting for transfers between devices: 58.2 us -> 62.9 us
  other arithmetic: 5.02 us -> 1.36 us
  matrix products: 2.86 us -> 0 us
  between operations: 17.8 us -> 15 us
    all_gather x1, waiting for transfers between devices: 6.09 us -> 12.2 us  [body(): weights = lax.all_gather(weights, ('y', 'core'), axis=0, tiled=True)]
    unnamed x16 -> x26, local copies, waits for them, and re-layouts: 1.88 us -> 6.37 us
    pallas_call x0 -> x3, Pallas kernels: none -> 3.47 us  [on_core(): pl.pallas_call(kernel, in_specs=[pl.BlockSpec(memory_space=pltpu.SMEM)] +...]
    pallas_call x1, Pallas kernels: 8.53 us -> 11.4 us  [block_terms(): pl.pallas_call(block_kernel, in_specs=[pl.BlockSpec(memory_space=pltpu.VM...]
    dot_general x3 -> x0, matrix products: 2.86 us -> none  [the longest x1 1.39 us: body(): jnp.dot(member.astype(jnp.float32).T, byte_share, precision=lax.Precision...]
    slice x5 -> x1, local copies, waits for them, and re-layouts: 2.58 us -> 0.61 us  [body(): segment_ids[0]]
    all_to_all x1, waiting for transfers between devices: 32 us -> 30.1 us  [exchanged(): return lax.all_to_all(a, 'tp', split_axis=0, concat_axis=0, tiled=True)]
    dynamic_update_slice x8 -> x9, local copies, waits for them, and re-layouts: 4.31 us -> 4.36 us  [put(): lax.dynamic_update_slice(whole, part, (row, lax.rem(owner + count, count)...]
  transfers between devices with their start and end apart: 12 -> 12, of which waited for: 7 -> 8; matrix products, arithmetic and copies ran while one was open for 9% -> 4% of each run, Pallas kernels for 0% -> 1%
where the time goes in v6:
time: 167 us
  waiting for transfers between devices  62.9 us (38%)
  starting transfers between devices  47.1 us (28%)
  between operations  15 us (9%)
  Pallas kernels  14.9 us (9%)
  blocking collectives  13.3 us (8%)
  local copies, waits for them, and re-layouts  12 us (7%)
    all_to_all x1, waiting for transfers between devices, exchanged(): return lax.all_to_all(a, 'tp', split_axis=0, concat_axis=0, tiled=True)  30.1 us
    ppermute x8, starting transfers between devices, turned(): lax.ppermute(shard, 'tp', [(i, (i + by) % count) for i in range(count)])  27.8 us
    ppermute x8, waiting for transfers between devices, turned(): lax.ppermute(shard, 'tp', [(i, (i + by) % count) for i in range(count)])  19.5 us
    all_gather x1, blocking collectives, body(): weights = lax.all_gather(weights, 'x', axis=0, tiled=True)  13.3 us
    all_gather x1, waiting for transfers between devices, body(): weights = lax.all_gather(weights, ('y', 'core'), axis=0, tiled=True)  12.2 us
    ppermute x2, starting transfers between devices, shifted(): return lax.ppermute(shard, axis, pairs)  12 us
    pallas_call x1, Pallas kernels, block_terms(): pl.pallas_call(block_kernel, in_specs=[pl.BlockSpec(memory_space=pltpu.VM...  11.4 us
    all_to_all x1, starting transfers between devices, exchanged(): return lax.all_to_all(a, 'tp', split_axis=0, concat_axis=0, tiled=True)  7.24 us
  transfers between devices with their start and end apart: 12, of which 8 were waited for; matrix products, arithmetic and copies ran while one was open for 4% of the time, Pallas kernels for 1%

profile of v6, /device:TPU:1, one launch (start us, length us, event | category | flops | bytes accessed | tf_op | source)
XLA Modules:
  0.0 166.6 jit_solution(7211560348884239077)
XLA Ops:
  6.5 1.0 pad_maximum_fusion
  7.5 13.3 %all_gather.6 = bf16[256,1536]{1,0:T(8,128)(2,1)} all-gather(bf16[64,1536]{1,0:T(8,128)(2,1)S(1)} %pad_maximum_fusion), channel_id=1, replica_groups=mesh['y'=8,'x'=4,'core'=2,'tp'=8] {'x'}, dimensions={0}, use_global_device_ids=true | all-gather | bytes 983040 | tf_op jit(solution)/shard_map/all_gather | solution.py:265
  20.9 0.9 copy-done.1
  21.8 0.9 copy-done.7
  23.4 0.8 shard_map.55
  24.2 10.1 %collective-permute-start = (f32[1,1280]{1,0:T(1,128)S(1)}, f32[1,1280]{1,0:T(1,128)S(1)}, u32[]{:S(2)}, u32[]{:S(2)}) collective-permute-start(f32[1,1280]{1,0:T(1,128)S(1)} %get-tuple-element.25), channel_id=1, source_target_pairs={{8,0},{16,8},{24,16},{32,24},{40,32},{48,40},{56,48},{64,56},{72,6... | collective-permute-start | bytes 15368 | tf_op jit(solution)/shard_map/ppermute | solution.py:19
  34.4 1.9 %collective-permute-start.1 = (f32[1,1280]{1,0:T(1,128)S(1)}, f32[1,1280]{1,0:T(1,128)S(1)}, u32[]{:S(2)}, u32[]{:S(2)}) collective-permute-start(f32[1,1280]{1,0:T(1,128)S(1)} %get-tuple-element.26), channel_id=1, source_target_pairs={{0,8},{8,16},{16,24},{24,32},{32,40},{40,48},{48,56},{56,64},{64,7... | collective-permute-start | bytes 15368 | tf_op jit(solution)/shard_map/ppermute | solution.py:19
  36.3 1.1 collective-permute-done.1.head_ref
  38.1 0.8 shard_map.56
  41.0 1.9 %collective-permute-start.2 = (bf16[384,512]{1,0:T(8,128)(2,1)S(1)}, bf16[384,512]{1,0:T(8,128)(2,1)}, u32[]{:S(2)}, u32[]{:S(2)}) collective-permute-start(bf16[384,512]{1,0:T(8,128)(2,1)S(1)} %get-tuple-element.27), channel_id=1, source_target_pairs={{0,1},{1,2},{2,3},{3,4},{4,5},{5,6},{6,7},{7,0},{8,9},{9,10},{10,1... | collective-permute-start | bytes 1179656 | tf_op jit(solution)/shard_map/ppermute | solution.py:24
  42.9 6.1 %collective-permute-start.3 = (bf16[384,512]{1,0:T(8,128)(2,1)S(1)}, bf16[384,512]{1,0:T(8,128)(2,1)}, u32[]{:S(2)}, u32[]{:S(2)}) collective-permute-start(bf16[384,512]{1,0:T(8,128)(2,1)S(1)} %get-tuple-element.27), channel_id=1, source_target_pairs={{0,7},{1,0},{2,1},{3,2},{4,3},{5,4},{6,5},{7,6},{8,15},{9,8},{10,9... | collective-permute-start | bytes 1179656 | tf_op jit(solution)/shard_map/ppermute | solution.py:24
  49.1 7.1 %collective-permute-done.2 = bf16[384,512]{1,0:T(8,128)(2,1)} collective-permute-done((bf16[384,512]{1,0:T(8,128)(2,1)S(1)}, bf16[384,512]{1,0:T(8,128)(2,1)}, u32[]{:S(2)}, u32[]{:S(2)}) %collective-permute-start.2) | collective-permute-done | bytes 393248 | tf_op jit(solution)/shard_map/ppermute | solution.py:24
  56.1 1.9 %collective-permute-start.4 = (bf16[384,512]{1,0:T(8,128)(2,1)}, bf16[384,512]{1,0:T(8,128)(2,1)}, u32[]{:S(2)}, u32[]{:S(2)}) collective-permute-start(bf16[384,512]{1,0:T(8,128)(2,1)} %collective-permute-done.2), channel_id=1, source_target_pairs={{0,1},{1,2},{2,3},{3,4},{4,5},{5,6},{6,7},{7,0},{8,9},{9,10},{10,1... | collective-permute-start | bytes 1179656 | tf_op jit(solution)/shard_map/ppermute | solution.py:24
  58.1 4.8 %collective-permute-start.5 = (bf16[384,512]{1,0:T(8,128)(2,1)}, bf16[384,512]{1,0:T(8,128)(2,1)}, u32[]{:S(2)}, u32[]{:S(2)}) collective-permute-start(bf16[384,512]{1,0:T(8,128)(2,1)} %collective-permute-done.3), channel_id=1, source_target_pairs={{0,7},{1,0},{2,1},{3,2},{4,3},{5,4},{6,5},{7,6},{8,15},{9,8},{10,9... | collective-permute-start | bytes 1179656 | tf_op jit(solution)/shard_map/ppermute | solution.py:24
  63.4 7.2 %collective-permute-done.4 = bf16[384,512]{1,0:T(8,128)(2,1)} collective-permute-done((bf16[384,512]{1,0:T(8,128)(2,1)}, bf16[384,512]{1,0:T(8,128)(2,1)}, u32[]{:S(2)}, u32[]{:S(2)}) %collective-permute-start.4) | collective-permute-done | bytes 393248 | tf_op jit(solution)/shard_map/ppermute | solution.py:24
  70.6 1.9 %collective-permute-start.6 = (bf16[384,512]{1,0:T(8,128)(2,1)}, bf16[384,512]{1,0:T(8,128)(2,1)S(1)}, u32[]{:S(2)}, u32[]{:S(2)}) collective-permute-start(bf16[384,512]{1,0:T(8,128)(2,1)} %collective-permute-done.4), channel_id=1, source_target_pairs={{0,1},{1,2},{2,3},{3,4},{4,5},{5,6},{6,7},{7,0},{8,9},{9,10},{10,1... | collective-permute-start | bytes 1179656 | tf_op jit(solution)/shard_map/ppermute | solution.py:24
  72.5 4.6 %collective-permute-start.7 = (bf16[384,512]{1,0:T(8,128)(2,1)}, bf16[384,512]{1,0:T(8,128)(2,1)S(1)}, u32[]{:S(2)}, u32[]{:S(2)}) collective-permute-start(bf16[384,512]{1,0:T(8,128)(2,1)} %collective-permute-done.5), channel_id=1, source_target_pairs={{0,7},{1,0},{2,1},{3,2},{4,3},{5,4},{6,5},{7,6},{8,15},{9,8},{10,9... | collective-permute-start | bytes 1179656 | tf_op jit(solution)/shard_map/ppermute | solution.py:24
  77.1 1.0 constant_dynamic-update-slice_fusion.6
  78.2 1.0 constant_dynamic-update-slice_fusion.5
  79.2 1.1 constant_dynamic-update-slice_fusion.4
  80.3 1.0 constant_dynamic-update-slice_fusion.3
  81.3 2.8 %collective-permute-done.6 = bf16[384,512]{1,0:T(8,128)(2,1)S(1)} collective-permute-done((bf16[384,512]{1,0:T(8,128)(2,1)}, bf16[384,512]{1,0:T(8,128)(2,1)S(1)}, u32[]{:S(2)}, u32[]{:S(2)}) %collective-permute-start.6) | collective-permute-done | bytes 393248 | tf_op jit(solution)/shard_map/ppermute | solution.py:24
  84.2 1.9 %collective-permute-start.8 = (bf16[192,512]{1,0:T(8,128)(2,1)S(1)}, bf16[192,512]{1,0:T(8,128)(2,1)S(1)}, u32[]{:S(2)}, u32[]{:S(2)}) collective-permute-start(bf16[192,512]{1,0:T(8,128)(2,1)S(1)} %slice.24), channel_id=1, source_target_pairs={{0,1},{1,2},{2,3},{3,4},{4,5},{5,6},{6,7},{7,0},{8,9},{9,10},{10,1... | collective-permute-start | bytes 589832 | tf_op jit(solution)/shard_map/ppermute | solution.py:24
  86.1 4.6 %collective-permute-start.9 = (bf16[192,512]{1,0:T(8,128)(2,1)S(1)}, bf16[192,512]{1,0:T(8,128)(2,1)S(1)}, u32[]{:S(2)}, u32[]{:S(2)}) collective-permute-start(bf16[192,512]{1,0:T(8,128)(2,1)S(1)} %slice.25), channel_id=1, source_target_pairs={{0,7},{1,0},{2,1},{3,2},{4,3},{5,4},{6,5},{7,6},{8,15},{9,8},{10,9... | collective-permute-start | bytes 589832 | tf_op jit(solution)/shard_map/ppermute | solution.py:24
  90.8 1.7 %collective-permute-done.8 = bf16[192,512]{1,0:T(8,128)(2,1)S(1)} collective-permute-done((bf16[192,512]{1,0:T(8,128)(2,1)S(1)}, bf16[192,512]{1,0:T(8,128)(2,1)S(1)}, u32[]{:S(2)}, u32[]{:S(2)}) %collective-permute-start.8) | collective-permute-done | bytes 196640 | tf_op jit(solution)/shard_map/ppermute | solution.py:24
  92.6 0.8 collective-permute-done.9
  93.9 12.2 %all-gather.2.cloned.1.call-done = bf16[4096,1536]{1,0:T(8,128)(2,1)} async-done(((bf16[256,1536]{1,0:T(8,128)(2,1)}), bf16[4096,1536]{1,0:T(8,128)(2,1)}) %all-gather.2.cloned.1.call-update) | async-done | bytes 12582928 | tf_op jit(solution)/shard_map/all_gather | solution.py:266
  106.1 11.4 %shard_map.57 = (bf16[8,144,512]{2,1,0:T(8,128)(2,1)S(1)}, bf16[8,64,512]{2,1,0:T(8,128)(2,1)}) custom-call(bf16[384,4096]{1,0:T(8,128)(2,1)S(1)} %constant_dynamic-update-slice_fusion.8.acts_ref, bf16[8,2,4,64,1536]{4,3,2,1,0:T(8,128)(2,1)} %bitcast.7, f32[192,1]{1,0:T(8,128)S(1)} %copy.6.inv_rms_ref), custom_call_target="tpu_custom_call" | custom-call | flops 3623878656 | bytes 17301504 | tf_op jit(solution)/shard_map/pallas_call | solution.py:127
  117.5 1.0 copy-done
  118.5 7.2 %all-to-all-start.1 = ((bf16[8,144,512]{2,1,0:T(8,128)(2,1)}), bf16[8,144,512]{2,1,0:T(8,128)(2,1)S(1)}, u32[]{:S(2)}, u32[]{:S(2)}) async-start(bf16[8,144,512]{2,1,0:T(8,128)(2,1)} %copy-done), calls=%async_computation.1 | async-start | bytes 2359296 | tf_op jit(solution)/shard_map/all_to_all | solution.py:300
  127.7 30.1 %all-to-all-done.1.terms_ref = bf16[8,144,512]{2,1,0:T(8,128)(2,1)S(1)} async-done(((bf16[8,144,512]{2,1,0:T(8,128)(2,1)}), bf16[8,144,512]{2,1,0:T(8,128)(2,1)S(1)}, u32[]{:S(2)}, u32[]{:S(2)}) %all-to-all-start.1) | async-done | bytes 1179680 | tf_op jit(solution)/shard_map/all_to_all | solution.py:300
  157.9 1.9 %shard_map.58 = bf16[192,512]{1,0:T(8,128)(2,1)} custom-call(s32[192]{0:T(256)S(1)} %copy-done.12, s32[192,1]{1,0:T(8,128)S(1)} %copy.7.ids_column_ref, bf16[8,144,512]{2,1,0:T(8,128)(2,1)S(1)} %all-to-all-done.1.terms_ref, f32[56,512]{1,0:T(8,128)S(1)} %get-tuple-element.37.rest_ref, f32[192,512]{1,0:T(8,128)S(1)} %copy-done.4, f32[192,512]{1,0:T(8,128)S(1)} %copy-done.6, ...), custom_call_target="tpu_custom_call" | custom-call | tf_op jit(solution)/shard_map/pallas_call | solution.py:251
  (44 shorter events, 5.4 us)
Async XLA Ops:
  6.5 99.5 %all-gather.2.cloned.1.call-start = ((), (), s32[]{:S(2)}) async-start(), calls=%async_computation.2 | async-start | bytes 13369344 | tf_op jit(solution)/shard_map/all_gather | solution.py:266
  20.9 0.9 copy-start.1
  21.8 0.9 copy-start.7
  22.7 0.7 copy-start.10
  24.2 12.1 %collective-permute-start = (f32[1,1280]{1,0:T(1,128)S(1)}, f32[1,1280]{1,0:T(1,128)S(1)}, u32[]{:S(2)}, u32[]{:S(2)}) collective-permute-start(f32[1,1280]{1,0:T(1,128)S(1)} %get-tuple-element.25), channel_id=1, source_target_pairs={{8,0},{16,8},{24,16},{32,24},{40,32},{48,40},{56,48},{64,56},{72,6... | collective-permute-start | bytes 15368 | tf_op jit(solution)/shard_map/ppermute | solution.py:19
  34.4 3.1 %collective-permute-start.1 = (f32[1,1280]{1,0:T(1,128)S(1)}, f32[1,1280]{1,0:T(1,128)S(1)}, u32[]{:S(2)}, u32[]{:S(2)}) collective-permute-start(f32[1,1280]{1,0:T(1,128)S(1)} %get-tuple-element.26), channel_id=1, source_target_pairs={{0,8},{8,16},{16,24},{24,32},{32,40},{40,48},{48,56},{56,64},{64,7... | collective-permute-start | bytes 15368 | tf_op jit(solution)/shard_map/ppermute | solution.py:19
  37.4 0.7 copy-start.11
  38.9 0.7 copy-start.3
  39.6 0.7 copy-start.5
  40.4 0.6 copy-start.8
  41.0 15.1 %collective-permute-start.2 = (bf16[384,512]{1,0:T(8,128)(2,1)S(1)}, bf16[384,512]{1,0:T(8,128)(2,1)}, u32[]{:S(2)}, u32[]{:S(2)}) collective-permute-start(bf16[384,512]{1,0:T(8,128)(2,1)S(1)} %get-tuple-element.27), channel_id=1, source_target_pairs={{0,1},{1,2},{2,3},{3,4},{4,5},{5,6},{6,7},{7,0},{8,9},{9,10},{10,1... | collective-permute-start | bytes 1179656 | tf_op jit(solution)/shard_map/ppermute | solution.py:24
  42.9 15.1 %collective-permute-start.3 = (bf16[384,512]{1,0:T(8,128)(2,1)S(1)}, bf16[384,512]{1,0:T(8,128)(2,1)}, u32[]{:S(2)}, u32[]{:S(2)}) collective-permute-start(bf16[384,512]{1,0:T(8,128)(2,1)S(1)} %get-tuple-element.27), channel_id=1, source_target_pairs={{0,7},{1,0},{2,1},{3,2},{4,3},{5,4},{6,5},{7,6},{8,15},{9,8},{10,9... | collective-permute-start | bytes 1179656 | tf_op jit(solution)/shard_map/ppermute | solution.py:24
  56.1 14.4 %collective-permute-start.4 = (bf16[384,512]{1,0:T(8,128)(2,1)}, bf16[384,512]{1,0:T(8,128)(2,1)}, u32[]{:S(2)}, u32[]{:S(2)}) collective-permute-start(bf16[384,512]{1,0:T(8,128)(2,1)} %collective-permute-done.2), channel_id=1, source_target_pairs={{0,1},{1,2},{2,3},{3,4},{4,5},{5,6},{6,7},{7,0},{8,9},{9,10},{10,1... | collective-permute-start | bytes 1179656 | tf_op jit(solution)/shard_map/ppermute | solution.py:24
  58.1 14.4 %collective-permute-start.5 = (bf16[384,512]{1,0:T(8,128)(2,1)}, bf16[384,512]{1,0:T(8,128)(2,1)}, u32[]{:S(2)}, u32[]{:S(2)}) collective-permute-start(bf16[384,512]{1,0:T(8,128)(2,1)} %collective-permute-done.3), channel_id=1, source_target_pairs={{0,7},{1,0},{2,1},{3,2},{4,3},{5,4},{6,5},{7,6},{8,15},{9,8},{10,9... | collective-permute-start | bytes 1179656 | tf_op jit(solution)/shard_map/ppermute | solution.py:24
  70.6 13.6 %collective-permute-start.6 = (bf16[384,512]{1,0:T(8,128)(2,1)}, bf16[384,512]{1,0:T(8,128)(2,1)S(1)}, u32[]{:S(2)}, u32[]{:S(2)}) collective-permute-start(bf16[384,512]{1,0:T(8,128)(2,1)} %collective-permute-done.4), channel_id=1, source_target_pairs={{0,1},{1,2},{2,3},{3,4},{4,5},{5,6},{6,7},{7,0},{8,9},{9,10},{10,1... | collective-permute-start | bytes 1179656 | tf_op jit(solution)/shard_map/ppermute | solution.py:24
  72.5 13.6 %collective-permute-start.7 = (bf16[384,512]{1,0:T(8,128)(2,1)}, bf16[384,512]{1,0:T(8,128)(2,1)S(1)}, u32[]{:S(2)}, u32[]{:S(2)}) collective-permute-start(bf16[384,512]{1,0:T(8,128)(2,1)} %collective-permute-done.5), channel_id=1, source_target_pairs={{0,7},{1,0},{2,1},{3,2},{4,3},{5,4},{6,5},{7,6},{8,15},{9,8},{10,9... | collective-permute-start | bytes 1179656 | tf_op jit(solution)/shard_map/ppermute | solution.py:24
  84.2 8.4 %collective-permute-start.8 = (bf16[192,512]{1,0:T(8,128)(2,1)S(1)}, bf16[192,512]{1,0:T(8,128)(2,1)S(1)}, u32[]{:S(2)}, u32[]{:S(2)}) collective-permute-start(bf16[192,512]{1,0:T(8,128)(2,1)S(1)} %slice.24), channel_id=1, source_target_pairs={{0,1},{1,2},{2,3},{3,4},{4,5},{5,6},{6,7},{7,0},{8,9},{9,10},{10,1... | collective-permute-start | bytes 589832 | tf_op jit(solution)/shard_map/ppermute | solution.py:24
  86.1 7.2 %collective-permute-start.9 = (bf16[192,512]{1,0:T(8,128)(2,1)S(1)}, bf16[192,512]{1,0:T(8,128)(2,1)S(1)}, u32[]{:S(2)}, u32[]{:S(2)}) collective-permute-start(bf16[192,512]{1,0:T(8,128)(2,1)S(1)} %slice.25), channel_id=1, source_target_pairs={{0,7},{1,0},{2,1},{3,2},{4,3},{5,4},{6,5},{7,6},{8,15},{9,8},{10,9... | collective-permute-start | bytes 589832 | tf_op jit(solution)/shard_map/ppermute | solution.py:24
  106.1 19.7 %copy-start.12 = (s32[192]{0:T(256)S(1)}, s32[192]{0:T(256)}, u32[]{:S(2)}) copy-start(s32[192]{0:T(256)} %ids_ref.5) | copy-start | bytes 2308
  117.5 1.0 copy-start
  118.5 39.3 %copy-start.2 = (bf16[192,512]{1,0:T(8,128)(2,1)S(1)}, bf16[192,512]{1,0:T(8,128)(2,1)}, u32[]{:S(2)}) copy-start(bf16[192,512]{1,0:T(8,128)(2,1)} %upstream_ref.3) | copy-start | bytes 589828
  118.5 39.3 %copy-start.4 = (f32[192,512]{1,0:T(8,128)S(1)}, f32[192,512]{1,0:T(8,128)}, u32[]{:S(2)}) copy-start(f32[192,512]{1,0:T(8,128)} %copy-done.3) | copy-start | bytes 1179652
  118.5 39.3 %copy-start.6 = (f32[192,512]{1,0:T(8,128)S(1)}, f32[192,512]{1,0:T(8,128)}, u32[]{:S(2)}) copy-start(f32[192,512]{1,0:T(8,128)} %copy-done.5) | copy-start | bytes 1179652
  118.5 39.3 %copy-start.9 = (f32[192,1]{1,0:T(8,128)S(1)}, f32[192,1]{1,0:T(8,128)}, u32[]{:S(2)}) copy-start(f32[192,1]{1,0:T(8,128)} %copy-done.8) | copy-start | bytes 2308
  118.5 39.3 %all-to-all-start.1 = ((bf16[8,144,512]{2,1,0:T(8,128)(2,1)}), bf16[8,144,512]{2,1,0:T(8,128)(2,1)S(1)}, u32[]{:S(2)}, u32[]{:S(2)}) async-start(bf16[8,144,512]{2,1,0:T(8,128)(2,1)} %copy-done), calls=%async_computation.1 | async-start | bytes 2359296 | tf_op jit(solution)/shard_map/all_to_all | solution.py:300
Sparse Core Ops, SparseCore 0:
  21.0 85.0 all-gather.1

commit v7 on v6

--- a/solution.py
+++ b/solution.py
@@ -110,10 +110,9 @@
         out_ref[block, :even] = term[:even].astype(jnp.bfloat16)
         out_ref[block, even:] = mixed_ref[...].astype(jnp.bfloat16)
         rest_ref[block] = term[even:].astype(jnp.bfloat16)
-        results.append(pltpu.make_async_copy(out_ref.at[block], out_hbm.at[block], out_sems.at[0, block]))
-        results.append(pltpu.make_async_copy(rest_ref.at[block], rest_hbm.at[block], out_sems.at[1, block]))
-        results[-2].start()
-        results[-1].start()
+        for i, (here, there) in enumerate(((out_ref, out_hbm), (rest_ref, rest_hbm))):
+            results.append(pltpu.make_async_copy(here.at[block], there.at[block], out_sems.at[i, block]))
+            results[-1].start()
     for copy in results:
         copy.wait()
 
@@ -133,8 +132,8 @@
         ],
         out_specs=[pl.BlockSpec(memory_space=pltpu.HBM)] * 2,
         out_shape=[
-            jax.ShapeDtypeStruct((blocks, kept, width), jnp.bfloat16),
-            jax.ShapeDtypeStruct((blocks, rows - kept + 16, width), jnp.bfloat16),
+            pltpu.HBM((blocks, kept, width), jnp.bfloat16),
+            pltpu.HBM((blocks, rows - kept + 16, width), jnp.bfloat16),
         ],
         scratch_shapes=[
             pltpu.VMEM((count_y, count_x, count_core, part, 2 * hidden), jnp.bfloat16),
@@ -247,11 +246,14 @@
 
 
 def on_core(kernel, out_shape, *operands, scratch=()):
-    vmem = pl.BlockSpec(memory_space=pltpu.VMEM)
+    def whole(a):
+        return pl.BlockSpec(a.shape, lambda i: (0,) * len(a.shape))
+
     return pl.pallas_call(
         kernel,
-        in_specs=[pl.BlockSpec(memory_space=pltpu.SMEM)] + [vmem] * (len(operands) - 1),
-        out_specs=jax.tree.map(lambda _: vmem, out_shape),
+        grid=(1,),
+        in_specs=[pl.BlockSpec(memory_space=pltpu.SMEM)] + [whole(a) for a in operands[1:]],
+        out_specs=jax.tree.map(whole, out_shape),
         out_shape=out_shape,
         scratch_shapes=scratch,
         compiler_params=pltpu.CompilerParams(vmem_limit_bytes=24 * 1024 * 1024),

time: 167 us -> 163 us (0.976)
  Pallas kernels: 14.9 us -> 12 us
  local copies, waits for them, and re-layouts: 12 us -> 10.3 us
    pallas_call x1, Pallas kernels: 11.4 us -> 8.52 us  [block_terms(): pl.pallas_call(block_kernel, in_specs=[pl.BlockSpec(memory_space=pltpu.VM...]
    unnamed x26 -> x22, local copies, waits for them, and re-layouts: 6.37 us -> 4.66 us
where the time goes in v7:
time: 163 us
  waiting for transfers between devices  63.6 us (39%)
  starting transfers between devices  47.1 us (29%)
  between operations  15 us (9%)
  blocking collectives  13.3 us (8%)
  Pallas kernels  12 us (7%)
  local copies, waits for them, and re-layouts  10.3 us (6%)
    all_to_all x1, waiting for transfers between devices, exchanged(): return lax.all_to_all(a, 'tp', split_axis=0, concat_axis=0, tiled=True)  30.1 us
    ppermute x8, starting transfers between devices, turned(): lax.ppermute(shard, 'tp', [(i, (i + by) % count) for i in range(count)])  27.8 us
    ppermute x8, waiting for transfers between devices, turned(): lax.ppermute(shard, 'tp', [(i, (i + by) % count) for i in range(count)])  19.5 us
    all_gather x1, blocking collectives, body(): weights = lax.all_gather(weights, 'x', axis=0, tiled=True)  13.3 us
    all_gather x1, waiting for transfers between devices, body(): weights = lax.all_gather(weights, ('y', 'core'), axis=0, tiled=True)  12.8 us
    ppermute x2, starting transfers between devices, shifted(): return lax.ppermute(shard, axis, pairs)  12 us
    pallas_call x1, Pallas kernels, block_terms(): pl.pallas_call(block_kernel, in_specs=[pl.BlockSpec(memory_space=pltpu.VM...  8.52 us
    all_to_all x1, starting transfers between devices, exchanged(): return lax.all_to_all(a, 'tp', split_axis=0, concat_axis=0, tiled=True)  7.24 us
  transfers between devices with their start and end apart: 12, of which 8 were waited for; matrix products, arithmetic and copies ran while one was open for 4% of the time, Pallas kernels for 1%

profile of v7, /device:TPU:1, one launch (start us, length us, event | category | flops | bytes accessed | tf_op | source)
XLA Modules:
  0.0 162.7 jit_solution(17295693064410569195)
XLA Ops:
  6.5 1.0 pad_maximum_fusion
  7.5 13.3 %all_gather.6 = bf16[256,1536]{1,0:T(8,128)(2,1)} all-gather(bf16[64,1536]{1,0:T(8,128)(2,1)S(1)} %pad_maximum_fusion), channel_id=1, replica_groups=mesh['y'=8,'x'=4,'core'=2,'tp'=8] {'x'}, dimensions={0}, use_global_device_ids=true | all-gather | bytes 983040 | tf_op jit(solution)/shard_map/all_gather | solution.py:267
  20.9 0.9 copy-done
  21.8 0.9 copy-done.6
  23.4 0.8 shard_map.55
  24.2 10.1 %collective-permute-start = (f32[1,1280]{1,0:T(1,128)S(1)}, f32[1,1280]{1,0:T(1,128)S(1)}, u32[]{:S(2)}, u32[]{:S(2)}) collective-permute-start(f32[1,1280]{1,0:T(1,128)S(1)} %get-tuple-element.25), channel_id=1, source_target_pairs={{8,0},{16,8},{24,16},{32,24},{40,32},{48,40},{56,48},{64,56},{72,6... | collective-permute-start | bytes 15368 | tf_op jit(solution)/shard_map/ppermute | solution.py:19
  34.4 1.9 %collective-permute-start.1 = (f32[1,1280]{1,0:T(1,128)S(1)}, f32[1,1280]{1,0:T(1,128)S(1)}, u32[]{:S(2)}, u32[]{:S(2)}) collective-permute-start(f32[1,1280]{1,0:T(1,128)S(1)} %get-tuple-element.26), channel_id=1, source_target_pairs={{0,8},{8,16},{16,24},{24,32},{32,40},{40,48},{48,56},{56,64},{64,7... | collective-permute-start | bytes 15368 | tf_op jit(solution)/shard_map/ppermute | solution.py:19
  36.3 1.1 collective-permute-done.1.head_ref
  37.4 0.8 shard_map.56
  39.0 0.7 copy-done.4
  40.3 1.9 %collective-permute-start.2 = (bf16[384,512]{1,0:T(8,128)(2,1)S(1)}, bf16[384,512]{1,0:T(8,128)(2,1)}, u32[]{:S(2)}, u32[]{:S(2)}) collective-permute-start(bf16[384,512]{1,0:T(8,128)(2,1)S(1)} %get-tuple-element.27), channel_id=1, source_target_pairs={{0,1},{1,2},{2,3},{3,4},{4,5},{5,6},{6,7},{7,0},{8,9},{9,10},{10,1... | collective-permute-start | bytes 1179656 | tf_op jit(solution)/shard_map/ppermute | solution.py:24
  42.3 6.1 %collective-permute-start.3 = (bf16[384,512]{1,0:T(8,128)(2,1)S(1)}, bf16[384,512]{1,0:T(8,128)(2,1)}, u32[]{:S(2)}, u32[]{:S(2)}) collective-permute-start(bf16[384,512]{1,0:T(8,128)(2,1)S(1)} %get-tuple-element.27), channel_id=1, source_target_pairs={{0,7},{1,0},{2,1},{3,2},{4,3},{5,4},{6,5},{7,6},{8,15},{9,8},{10,9... | collective-permute-start | bytes 1179656 | tf_op jit(solution)/shard_map/ppermute | solution.py:24
  48.4 7.1 %collective-permute-done.2 = bf16[384,512]{1,0:T(8,128)(2,1)} collective-permute-done((bf16[384,512]{1,0:T(8,128)(2,1)S(1)}, bf16[384,512]{1,0:T(8,128)(2,1)}, u32[]{:S(2)}, u32[]{:S(2)}) %collective-permute-start.2) | collective-permute-done | bytes 393248 | tf_op jit(solution)/shard_map/ppermute | solution.py:24
  55.5 1.9 %collective-permute-start.4 = (bf16[384,512]{1,0:T(8,128)(2,1)}, bf16[384,512]{1,0:T(8,128)(2,1)}, u32[]{:S(2)}, u32[]{:S(2)}) collective-permute-start(bf16[384,512]{1,0:T(8,128)(2,1)} %collective-permute-done.2), channel_id=1, source_target_pairs={{0,1},{1,2},{2,3},{3,4},{4,5},{5,6},{6,7},{7,0},{8,9},{9,10},{10,1... | collective-permute-start | bytes 1179656 | tf_op jit(solution)/shard_map/ppermute | solution.py:24
  57.4 4.8 %collective-permute-start.5 = (bf16[384,512]{1,0:T(8,128)(2,1)}, bf16[384,512]{1,0:T(8,128)(2,1)}, u32[]{:S(2)}, u32[]{:S(2)}) collective-permute-start(bf16[384,512]{1,0:T(8,128)(2,1)} %collective-permute-done.3), channel_id=1, source_target_pairs={{0,7},{1,0},{2,1},{3,2},{4,3},{5,4},{6,5},{7,6},{8,15},{9,8},{10,9... | collective-permute-start | bytes 1179656 | tf_op jit(solution)/shard_map/ppermute | solution.py:24
  62.7 7.2 %collective-permute-done.4 = bf16[384,512]{1,0:T(8,128)(2,1)} collective-permute-done((bf16[384,512]{1,0:T(8,128)(2,1)}, bf16[384,512]{1,0:T(8,128)(2,1)}, u32[]{:S(2)}, u32[]{:S(2)}) %collective-permute-start.4) | collective-permute-done | bytes 393248 | tf_op jit(solution)/shard_map/ppermute | solution.py:24
  69.9 1.9 %collective-permute-start.6 = (bf16[384,512]{1,0:T(8,128)(2,1)}, bf16[384,512]{1,0:T(8,128)(2,1)S(1)}, u32[]{:S(2)}, u32[]{:S(2)}) collective-permute-start(bf16[384,512]{1,0:T(8,128)(2,1)} %collective-permute-done.4), channel_id=1, source_target_pairs={{0,1},{1,2},{2,3},{3,4},{4,5},{5,6},{6,7},{7,0},{8,9},{9,10},{10,1... | collective-permute-start | bytes 1179656 | tf_op jit(solution)/shard_map/ppermute | solution.py:24
  71.8 4.6 %collective-permute-start.7 = (bf16[384,512]{1,0:T(8,128)(2,1)}, bf16[384,512]{1,0:T(8,128)(2,1)S(1)}, u32[]{:S(2)}, u32[]{:S(2)}) collective-permute-start(bf16[384,512]{1,0:T(8,128)(2,1)} %collective-permute-done.5), channel_id=1, source_target_pairs={{0,7},{1,0},{2,1},{3,2},{4,3},{5,4},{6,5},{7,6},{8,15},{9,8},{10,9... | collective-permute-start | bytes 1179656 | tf_op jit(solution)/shard_map/ppermute | solution.py:24
  76.4 1.0 constant_dynamic-update-slice_fusion.6
  77.5 1.1 constant_dynamic-update-slice_fusion.5
  78.6 1.0 constant_dynamic-update-slice_fusion.4
  79.6 1.1 constant_dynamic-update-slice_fusion.3
  80.7 2.8 %collective-permute-done.6 = bf16[384,512]{1,0:T(8,128)(2,1)S(1)} collective-permute-done((bf16[384,512]{1,0:T(8,128)(2,1)}, bf16[384,512]{1,0:T(8,128)(2,1)S(1)}, u32[]{:S(2)}, u32[]{:S(2)}) %collective-permute-start.6) | collective-permute-done | bytes 393248 | tf_op jit(solution)/shard_map/ppermute | solution.py:24
  83.5 1.9 %collective-permute-start.8 = (bf16[192,512]{1,0:T(8,128)(2,1)S(1)}, bf16[192,512]{1,0:T(8,128)(2,1)S(1)}, u32[]{:S(2)}, u32[]{:S(2)}) collective-permute-start(bf16[192,512]{1,0:T(8,128)(2,1)S(1)} %slice.24), channel_id=1, source_target_pairs={{0,1},{1,2},{2,3},{3,4},{4,5},{5,6},{6,7},{7,0},{8,9},{9,10},{10,1... | collective-permute-start | bytes 589832 | tf_op jit(solution)/shard_map/ppermute | solution.py:24
  85.5 4.6 %collective-permute-start.9 = (bf16[192,512]{1,0:T(8,128)(2,1)S(1)}, bf16[192,512]{1,0:T(8,128)(2,1)S(1)}, u32[]{:S(2)}, u32[]{:S(2)}) collective-permute-start(bf16[192,512]{1,0:T(8,128)(2,1)S(1)} %slice.25), channel_id=1, source_target_pairs={{0,7},{1,0},{2,1},{3,2},{4,3},{5,4},{6,5},{7,6},{8,15},{9,8},{10,9... | collective-permute-start | bytes 589832 | tf_op jit(solution)/shard_map/ppermute | solution.py:24
  90.2 1.7 %collective-permute-done.8 = bf16[192,512]{1,0:T(8,128)(2,1)S(1)} collective-permute-done((bf16[192,512]{1,0:T(8,128)(2,1)S(1)}, bf16[192,512]{1,0:T(8,128)(2,1)S(1)}, u32[]{:S(2)}, u32[]{:S(2)}) %collective-permute-start.8) | collective-permute-done | bytes 196640 | tf_op jit(solution)/shard_map/ppermute | solution.py:24
  91.9 0.8 collective-permute-done.9
  93.2 12.8 %all-gather.2.cloned.1.call-done = bf16[4096,1536]{1,0:T(8,128)(2,1)} async-done(((bf16[256,1536]{1,0:T(8,128)(2,1)}), bf16[4096,1536]{1,0:T(8,128)(2,1)}) %all-gather.2.cloned.1.call-update) | async-done | bytes 12582928 | tf_op jit(solution)/shard_map/all_gather | solution.py:268
  106.1 8.5 %shard_map.57 = (bf16[8,144,512]{2,1,0:T(8,128)(2,1)}, bf16[8,64,512]{2,1,0:T(8,128)(2,1)}) custom-call(bf16[384,4096]{1,0:T(8,128)(2,1)S(1)} %constant_dynamic-update-slice_fusion.8.acts_ref, bf16[8,2,4,64,1536]{4,3,2,1,0:T(8,128)(2,1)} %bitcast.7, f32[192,1]{1,0:T(8,128)S(1)} %copy.6.inv_rms_ref), custom_call_target="tpu_custom_call" | custom-call | flops 3623878656 | bytes 17301504 | tf_op jit(solution)/shard_map/pallas_call | solution.py:126
  114.6 7.2 %all-to-all-start.1 = ((bf16[8,144,512]{2,1,0:T(8,128)(2,1)}), bf16[8,144,512]{2,1,0:T(8,128)(2,1)S(1)}, u32[]{:S(2)}, u32[]{:S(2)}) async-start(bf16[8,144,512]{2,1,0:T(8,128)(2,1)} %get-tuple-element.28), calls=%async_computation.1 | async-start | bytes 2359296 | tf_op jit(solution)/shard_map/all_to_all | solution.py:302
  123.9 30.1 %all-to-all-done.1.terms_ref = bf16[8,144,512]{2,1,0:T(8,128)(2,1)S(1)} async-done(((bf16[8,144,512]{2,1,0:T(8,128)(2,1)}), bf16[8,144,512]{2,1,0:T(8,128)(2,1)S(1)}, u32[]{:S(2)}, u32[]{:S(2)}) %all-to-all-start.1) | async-done | bytes 1179680 | tf_op jit(solution)/shard_map/all_to_all | solution.py:302
  154.0 1.9 %shard_map.58 = bf16[192,512]{1,0:T(8,128)(2,1)} custom-call(s32[192]{0:T(256)S(1)} %copy-done.10, s32[192,1]{1,0:T(8,128)S(1)} %copy.7.ids_column_ref, bf16[8,144,512]{2,1,0:T(8,128)(2,1)S(1)} %all-to-all-done.1.terms_ref, f32[56,512]{1,0:T(8,128)S(1)} %get-tuple-element.37.rest_ref, f32[192,512]{1,0:T(8,128)S(1)} %copy-done.3, f32[192,512]{1,0:T(8,128)S(1)} %copy-done.5, ...), custom_call_target="tpu_custom_call" | custom-call | tf_op jit(solution)/shard_map/pallas_call | solution.py:252
  (40 shorter events, 3.9 us)
Async XLA Ops:
  6.5 99.5 %all-gather.2.cloned.1.call-start = ((), (), s32[]{:S(2)}) async-start(), calls=%async_computation.2 | async-start | bytes 13369344 | tf_op jit(solution)/shard_map/all_gather | solution.py:268
  20.9 0.9 copy-start
  21.8 0.9 copy-start.6
  22.7 0.7 copy-start.9
  24.2 12.1 %collective-permute-start = (f32[1,1280]{1,0:T(1,128)S(1)}, f32[1,1280]{1,0:T(1,128)S(1)}, u32[]{:S(2)}, u32[]{:S(2)}) collective-permute-start(f32[1,1280]{1,0:T(1,128)S(1)} %get-tuple-element.25), channel_id=1, source_target_pairs={{8,0},{16,8},{24,16},{32,24},{40,32},{48,40},{56,48},{64,56},{72,6... | collective-permute-start | bytes 15368 | tf_op jit(solution)/shard_map/ppermute | solution.py:19
  34.4 3.1 %collective-permute-start.1 = (f32[1,1280]{1,0:T(1,128)S(1)}, f32[1,1280]{1,0:T(1,128)S(1)}, u32[]{:S(2)}, u32[]{:S(2)}) collective-permute-start(f32[1,1280]{1,0:T(1,128)S(1)} %get-tuple-element.26), channel_id=1, source_target_pairs={{0,8},{8,16},{16,24},{24,32},{32,40},{40,48},{48,56},{56,64},{64,7... | collective-permute-start | bytes 15368 | tf_op jit(solution)/shard_map/ppermute | solution.py:19
  38.2 0.7 copy-start.2
  39.0 0.7 copy-start.4
  39.7 0.6 copy-start.7
  40.3 15.1 %collective-permute-start.2 = (bf16[384,512]{1,0:T(8,128)(2,1)S(1)}, bf16[384,512]{1,0:T(8,128)(2,1)}, u32[]{:S(2)}, u32[]{:S(2)}) collective-permute-start(bf16[384,512]{1,0:T(8,128)(2,1)S(1)} %get-tuple-element.27), channel_id=1, source_target_pairs={{0,1},{1,2},{2,3},{3,4},{4,5},{5,6},{6,7},{7,0},{8,9},{9,10},{10,1... | collective-permute-start | bytes 1179656 | tf_op jit(solution)/shard_map/ppermute | solution.py:24
  42.3 15.1 %collective-permute-start.3 = (bf16[384,512]{1,0:T(8,128)(2,1)S(1)}, bf16[384,512]{1,0:T(8,128)(2,1)}, u32[]{:S(2)}, u32[]{:S(2)}) collective-permute-start(bf16[384,512]{1,0:T(8,128)(2,1)S(1)} %get-tuple-element.27), channel_id=1, source_target_pairs={{0,7},{1,0},{2,1},{3,2},{4,3},{5,4},{6,5},{7,6},{8,15},{9,8},{10,9... | collective-permute-start | bytes 1179656 | tf_op jit(solution)/shard_map/ppermute | solution.py:24
  55.5 14.4 %collective-permute-start.4 = (bf16[384,512]{1,0:T(8,128)(2,1)}, bf16[384,512]{1,0:T(8,128)(2,1)}, u32[]{:S(2)}, u32[]{:S(2)}) collective-permute-start(bf16[384,512]{1,0:T(8,128)(2,1)} %collective-permute-done.2), channel_id=1, source_target_pairs={{0,1},{1,2},{2,3},{3,4},{4,5},{5,6},{6,7},{7,0},{8,9},{9,10},{10,1... | collective-permute-start | bytes 1179656 | tf_op jit(solution)/shard_map/ppermute | solution.py:24
  57.4 14.4 %collective-permute-start.5 = (bf16[384,512]{1,0:T(8,128)(2,1)}, bf16[384,512]{1,0:T(8,128)(2,1)}, u32[]{:S(2)}, u32[]{:S(2)}) collective-permute-start(bf16[384,512]{1,0:T(8,128)(2,1)} %collective-permute-done.3), channel_id=1, source_target_pairs={{0,7},{1,0},{2,1},{3,2},{4,3},{5,4},{6,5},{7,6},{8,15},{9,8},{10,9... | collective-permute-start | bytes 1179656 | tf_op jit(solution)/shard_map/ppermute | solution.py:24
  69.9 13.6 %collective-permute-start.6 = (bf16[384,512]{1,0:T(8,128)(2,1)}, bf16[384,512]{1,0:T(8,128)(2,1)S(1)}, u32[]{:S(2)}, u32[]{:S(2)}) collective-permute-start(bf16[384,512]{1,0:T(8,128)(2,1)} %collective-permute-done.4), channel_id=1, source_target_pairs={{0,1},{1,2},{2,3},{3,4},{4,5},{5,6},{6,7},{7,0},{8,9},{9,10},{10,1... | collective-permute-start | bytes 1179656 | tf_op jit(solution)/shard_map/ppermute | solution.py:24
  71.8 13.6 %collective-permute-start.7 = (bf16[384,512]{1,0:T(8,128)(2,1)}, bf16[384,512]{1,0:T(8,128)(2,1)S(1)}, u32[]{:S(2)}, u32[]{:S(2)}) collective-permute-start(bf16[384,512]{1,0:T(8,128)(2,1)} %collective-permute-done.5), channel_id=1, source_target_pairs={{0,7},{1,0},{2,1},{3,2},{4,3},{5,4},{6,5},{7,6},{8,15},{9,8},{10,9... | collective-permute-start | bytes 1179656 | tf_op jit(solution)/shard_map/ppermute | solution.py:24
  83.5 8.4 %collective-permute-start.8 = (bf16[192,512]{1,0:T(8,128)(2,1)S(1)}, bf16[192,512]{1,0:T(8,128)(2,1)S(1)}, u32[]{:S(2)}, u32[]{:S(2)}) collective-permute-start(bf16[192,512]{1,0:T(8,128)(2,1)S(1)} %slice.24), channel_id=1, source_target_pairs={{0,1},{1,2},{2,3},{3,4},{4,5},{5,6},{6,7},{7,0},{8,9},{9,10},{10,1... | collective-permute-start | bytes 589832 | tf_op jit(solution)/shard_map/ppermute | solution.py:24
  85.5 7.2 %collective-permute-start.9 = (bf16[192,512]{1,0:T(8,128)(2,1)S(1)}, bf16[192,512]{1,0:T(8,128)(2,1)S(1)}, u32[]{:S(2)}, u32[]{:S(2)}) collective-permute-start(bf16[192,512]{1,0:T(8,128)(2,1)S(1)} %slice.25), channel_id=1, source_target_pairs={{0,7},{1,0},{2,1},{3,2},{4,3},{5,4},{6,5},{7,6},{8,15},{9,8},{10,9... | collective-permute-start | bytes 589832 | tf_op jit(solution)/shard_map/ppermute | solution.py:24
  106.1 15.8 %copy-start.10 = (s32[192]{0:T(256)S(1)}, s32[192]{0:T(256)}, u32[]{:S(2)}) copy-start(s32[192]{0:T(256)} %ids_ref.5) | copy-start | bytes 2308
  114.6 39.4 %copy-start.1 = (bf16[192,512]{1,0:T(8,128)(2,1)S(1)}, bf16[192,512]{1,0:T(8,128)(2,1)}, u32[]{:S(2)}) copy-start(bf16[192,512]{1,0:T(8,128)(2,1)} %upstream_ref.3) | copy-start | bytes 589828
  114.6 39.4 %copy-start.3 = (f32[192,512]{1,0:T(8,128)S(1)}, f32[192,512]{1,0:T(8,128)}, u32[]{:S(2)}) copy-start(f32[192,512]{1,0:T(8,128)} %copy-done.2) | copy-start | bytes 1179652
  114.6 39.4 %copy-start.5 = (f32[192,512]{1,0:T(8,128)S(1)}, f32[192,512]{1,0:T(8,128)}, u32[]{:S(2)}) copy-start(f32[192,512]{1,0:T(8,128)} %copy-done.4) | copy-start | bytes 1179652
  114.6 39.4 %copy-start.8 = (f32[192,1]{1,0:T(8,128)S(1)}, f32[192,1]{1,0:T(8,128)}, u32[]{:S(2)}) copy-start(f32[192,1]{1,0:T(8,128)} %copy-done.7) | copy-start | bytes 2308
  114.6 39.3 %all-to-all-start.1 = ((bf16[8,144,512]{2,1,0:T(8,128)(2,1)}), bf16[8,144,512]{2,1,0:T(8,128)(2,1)S(1)}, u32[]{:S(2)}, u32[]{:S(2)}) async-start(bf16[8,144,512]{2,1,0:T(8,128)(2,1)} %get-tuple-element.28), calls=%async_computation.1 | async-start | bytes 2359296 | tf_op jit(solution)/shard_map/all_to_all | solution.py:302
Sparse Core Ops, SparseCore 0:
  21.0 85.0 all-gather.1

commit v8 on v7

--- a/solution.py
+++ b/solution.py
@@ -46,7 +46,7 @@
 
 
 def block_kernel(
-    acts_ref, weights_hbm, inv_rms_ref, out_hbm, rest_hbm, weights_ref, mixed_ref, out_ref, rest_ref, sems, out_sems
+    acts_ref, weights_hbm, inv_rms_ref, out_hbm, rest_hbm, weights_ref, turned_ref, mixed_ref, out_ref, rest_ref, sems, out_sems
 ):
     rows = inv_rms_ref.shape[0]
     hidden = weights_ref.shape[-1] // 2
@@ -76,9 +76,9 @@
             for copy in pair:
                 copy.wait()
         at = pl.ds(k * width, width)
-        up_proj += jnp.dot(
-            acts_ref[:rows, at], chunk(k, first), preferred_element_type=jnp.float32
-        )
+        own = chunk(k, first)
+        up_proj += jnp.dot(acts_ref[:rows, at], own, preferred_element_type=jnp.float32)
+        turned_ref[k] = own.T
         back_proj += jnp.dot(
             acts_ref[rows:, at], chunk(k, second), preferred_element_type=jnp.float32
         )
@@ -100,12 +100,7 @@
     even = kept - 16
     results = []
     for block in range(blocks):
-        term = lax.dot_general(
-            grad_hidden,
-            chunk(block, first),
-            (((1,), (1,)), ((), ())),
-            preferred_element_type=jnp.float32,
-        )
+        term = jnp.dot(grad_hidden, turned_ref[block], preferred_element_type=jnp.float32)
         mixed_ref[:8] = term[even : even + 8]
         out_ref[block, :even] = term[:even].astype(jnp.bfloat16)
         out_ref[block, even:] = mixed_ref[...].astype(jnp.bfloat16)
@@ -137,6 +132,7 @@
         ],
         scratch_shapes=[
             pltpu.VMEM((count_y, count_x, count_core, part, 2 * hidden), jnp.bfloat16),
+            pltpu.VMEM((blocks, hidden, width), jnp.bfloat16),
             pltpu.VMEM((16, width), jnp.float32),
             pltpu.VMEM((blocks, kept, width), jnp.bfloat16),
             pltpu.VMEM((blocks, rows - kept + 16, width), jnp.bfloat16),
@@ -238,11 +234,11 @@
     left = share_ref[...]
     spread = upstream_ref[...].astype(jnp.float32)
     parts = []
-    for _ in range(3):
+    for _ in range(2):
         part = left.astype(jnp.bfloat16)
         left = left - part.astype(jnp.float32)
         parts.append(jnp.dot(member, part, preferred_element_type=jnp.float32))
-    out_ref[...] = (spread + ((parts[2] + parts[1]) + parts[0])).astype(jnp.bfloat16)
+    out_ref[...] = (spread + (parts[1] + parts[0])).astype(jnp.bfloat16)
 
 
 def on_core(kernel, out_shape, *operands, scratch=()):

time: 163 us -> 163 us (level)
  no operation moved by 1% of the time
where the time goes in v8:
time: 163 us; the launch traced here: 162 us
  waiting for transfers between devices  63.6 us (39%)
  starting transfers between devices  47.1 us (29%)
  between operations  15 us (9%)
  blocking collectives  13.3 us (8%)
  Pallas kernels  11.3 us (7%)
  local copies, waits for them, and re-layouts  10.3 us (6%)
    all_to_all x1, waiting for transfers between devices, exchanged(): return lax.all_to_all(a, 'tp', split_axis=0, concat_axis=0, tiled=True)  30.1 us
    ppermute x8, starting transfers between devices, turned(): lax.ppermute(shard, 'tp', [(i, (i + by) % count) for i in range(count)])  27.8 us
    ppermute x8, waiting for transfers between devices, turned(): lax.ppermute(shard, 'tp', [(i, (i + by) % count) for i in range(count)])  19.5 us
    all_gather x1, blocking collectives, body(): weights = lax.all_gather(weights, 'x', axis=0, tiled=True)  13.3 us
    all_gather x1, waiting for transfers between devices, body(): weights = lax.all_gather(weights, ('y', 'core'), axis=0, tiled=True)  12.8 us
    ppermute x2, starting transfers between devices, shifted(): return lax.ppermute(shard, axis, pairs)  12 us
    pallas_call x1, Pallas kernels, block_terms(): pl.pallas_call(block_kernel, in_specs=[pl.BlockSpec(memory_space=pltpu.VM...  7.88 us
    all_to_all x1, starting transfers between devices, exchanged(): return lax.all_to_all(a, 'tp', split_axis=0, concat_axis=0, tiled=True)  7.24 us
  transfers between devices with their start and end apart: 12, of which 8 were waited for; matrix products, arithmetic and copies ran while one was open for 4% of the time, Pallas kernels for 1%

profile of v8, /device:TPU:1, one launch (start us, length us, event | category | flops | bytes accessed | tf_op | source)
XLA Modules:
  0.0 162.0 jit_solution(6018527729215403986)
XLA Ops:
  6.5 1.0 pad_maximum_fusion
  7.5 13.3 %all_gather.6 = bf16[256,1536]{1,0:T(8,128)(2,1)} all-gather(bf16[64,1536]{1,0:T(8,128)(2,1)S(1)} %pad_maximum_fusion), channel_id=1, replica_groups=mesh['y'=8,'x'=4,'core'=2,'tp'=8] {'x'}, dimensions={0}, use_global_device_ids=true | all-gather | bytes 983040 | tf_op jit(solution)/shard_map/all_gather | solution.py:263
  20.9 0.9 copy-done
  21.8 0.9 copy-done.6
  23.4 0.8 shard_map.55
  24.2 10.1 %collective-permute-start = (f32[1,1280]{1,0:T(1,128)S(1)}, f32[1,1280]{1,0:T(1,128)S(1)}, u32[]{:S(2)}, u32[]{:S(2)}) collective-permute-start(f32[1,1280]{1,0:T(1,128)S(1)} %get-tuple-element.25), channel_id=1, source_target_pairs={{8,0},{16,8},{24,16},{32,24},{40,32},{48,40},{56,48},{64,56},{72,6... | collective-permute-start | bytes 15368 | tf_op jit(solution)/shard_map/ppermute | solution.py:19
  34.4 1.9 %collective-permute-start.1 = (f32[1,1280]{1,0:T(1,128)S(1)}, f32[1,1280]{1,0:T(1,128)S(1)}, u32[]{:S(2)}, u32[]{:S(2)}) collective-permute-start(f32[1,1280]{1,0:T(1,128)S(1)} %get-tuple-element.26), channel_id=1, source_target_pairs={{0,8},{8,16},{16,24},{24,32},{32,40},{40,48},{48,56},{56,64},{64,7... | collective-permute-start | bytes 15368 | tf_op jit(solution)/shard_map/ppermute | solution.py:19
  36.3 1.1 collective-permute-done.1.head_ref
  37.4 0.8 shard_map.56
  39.0 0.7 copy-done.4
  40.3 1.9 %collective-permute-start.2 = (bf16[384,512]{1,0:T(8,128)(2,1)S(1)}, bf16[384,512]{1,0:T(8,128)(2,1)}, u32[]{:S(2)}, u32[]{:S(2)}) collective-permute-start(bf16[384,512]{1,0:T(8,128)(2,1)S(1)} %get-tuple-element.27), channel_id=1, source_target_pairs={{0,1},{1,2},{2,3},{3,4},{4,5},{5,6},{6,7},{7,0},{8,9},{9,10},{10,1... | collective-permute-start | bytes 1179656 | tf_op jit(solution)/shard_map/ppermute | solution.py:24
  42.3 6.1 %collective-permute-start.3 = (bf16[384,512]{1,0:T(8,128)(2,1)S(1)}, bf16[384,512]{1,0:T(8,128)(2,1)}, u32[]{:S(2)}, u32[]{:S(2)}) collective-permute-start(bf16[384,512]{1,0:T(8,128)(2,1)S(1)} %get-tuple-element.27), channel_id=1, source_target_pairs={{0,7},{1,0},{2,1},{3,2},{4,3},{5,4},{6,5},{7,6},{8,15},{9,8},{10,9... | collective-permute-start | bytes 1179656 | tf_op jit(solution)/shard_map/ppermute | solution.py:24
  48.4 7.1 %collective-permute-done.2 = bf16[384,512]{1,0:T(8,128)(2,1)} collective-permute-done((bf16[384,512]{1,0:T(8,128)(2,1)S(1)}, bf16[384,512]{1,0:T(8,128)(2,1)}, u32[]{:S(2)}, u32[]{:S(2)}) %collective-permute-start.2) | collective-permute-done | bytes 393248 | tf_op jit(solution)/shard_map/ppermute | solution.py:24
  55.5 1.9 %collective-permute-start.4 = (bf16[384,512]{1,0:T(8,128)(2,1)}, bf16[384,512]{1,0:T(8,128)(2,1)}, u32[]{:S(2)}, u32[]{:S(2)}) collective-permute-start(bf16[384,512]{1,0:T(8,128)(2,1)} %collective-permute-done.2), channel_id=1, source_target_pairs={{0,1},{1,2},{2,3},{3,4},{4,5},{5,6},{6,7},{7,0},{8,9},{9,10},{10,1... | collective-permute-start | bytes 1179656 | tf_op jit(solution)/shard_map/ppermute | solution.py:24
  57.4 4.8 %collective-permute-start.5 = (bf16[384,512]{1,0:T(8,128)(2,1)}, bf16[384,512]{1,0:T(8,128)(2,1)}, u32[]{:S(2)}, u32[]{:S(2)}) collective-permute-start(bf16[384,512]{1,0:T(8,128)(2,1)} %collective-permute-done.3), channel_id=1, source_target_pairs={{0,7},{1,0},{2,1},{3,2},{4,3},{5,4},{6,5},{7,6},{8,15},{9,8},{10,9... | collective-permute-start | bytes 1179656 | tf_op jit(solution)/shard_map/ppermute | solution.py:24
  62.7 7.2 %collective-permute-done.4 = bf16[384,512]{1,0:T(8,128)(2,1)} collective-permute-done((bf16[384,512]{1,0:T(8,128)(2,1)}, bf16[384,512]{1,0:T(8,128)(2,1)}, u32[]{:S(2)}, u32[]{:S(2)}) %collective-permute-start.4) | collective-permute-done | bytes 393248 | tf_op jit(solution)/shard_map/ppermute | solution.py:24
  69.9 1.9 %collective-permute-start.6 = (bf16[384,512]{1,0:T(8,128)(2,1)}, bf16[384,512]{1,0:T(8,128)(2,1)S(1)}, u32[]{:S(2)}, u32[]{:S(2)}) collective-permute-start(bf16[384,512]{1,0:T(8,128)(2,1)} %collective-permute-done.4), channel_id=1, source_target_pairs={{0,1},{1,2},{2,3},{3,4},{4,5},{5,6},{6,7},{7,0},{8,9},{9,10},{10,1... | collective-permute-start | bytes 1179656 | tf_op jit(solution)/shard_map/ppermute | solution.py:24
  71.8 4.6 %collective-permute-start.7 = (bf16[384,512]{1,0:T(8,128)(2,1)}, bf16[384,512]{1,0:T(8,128)(2,1)S(1)}, u32[]{:S(2)}, u32[]{:S(2)}) collective-permute-start(bf16[384,512]{1,0:T(8,128)(2,1)} %collective-permute-done.5), channel_id=1, source_target_pairs={{0,7},{1,0},{2,1},{3,2},{4,3},{5,4},{6,5},{7,6},{8,15},{9,8},{10,9... | collective-permute-start | bytes 1179656 | tf_op jit(solution)/shard_map/ppermute | solution.py:24
  76.4 1.0 constant_dynamic-update-slice_fusion.6
  77.5 1.1 constant_dynamic-update-slice_fusion.5
  78.6 1.0 constant_dynamic-update-slice_fusion.4
  79.6 1.1 constant_dynamic-update-slice_fusion.3
  80.7 2.8 %collective-permute-done.6 = bf16[384,512]{1,0:T(8,128)(2,1)S(1)} collective-permute-done((bf16[384,512]{1,0:T(8,128)(2,1)}, bf16[384,512]{1,0:T(8,128)(2,1)S(1)}, u32[]{:S(2)}, u32[]{:S(2)}) %collective-permute-start.6) | collective-permute-done | bytes 393248 | tf_op jit(solution)/shard_map/ppermute | solution.py:24
  83.5 1.9 %collective-permute-start.8 = (bf16[192,512]{1,0:T(8,128)(2,1)S(1)}, bf16[192,512]{1,0:T(8,128)(2,1)S(1)}, u32[]{:S(2)}, u32[]{:S(2)}) collective-permute-start(bf16[192,512]{1,0:T(8,128)(2,1)S(1)} %slice.24), channel_id=1, source_target_pairs={{0,1},{1,2},{2,3},{3,4},{4,5},{5,6},{6,7},{7,0},{8,9},{9,10},{10,1... | collective-permute-start | bytes 589832 | tf_op jit(solution)/shard_map/ppermute | solution.py:24
  85.5 4.6 %collective-permute-start.9 = (bf16[192,512]{1,0:T(8,128)(2,1)S(1)}, bf16[192,512]{1,0:T(8,128)(2,1)S(1)}, u32[]{:S(2)}, u32[]{:S(2)}) collective-permute-start(bf16[192,512]{1,0:T(8,128)(2,1)S(1)} %slice.25), channel_id=1, source_target_pairs={{0,7},{1,0},{2,1},{3,2},{4,3},{5,4},{6,5},{7,6},{8,15},{9,8},{10,9... | collective-permute-start | bytes 589832 | tf_op jit(solution)/shard_map/ppermute | solution.py:24
  90.2 1.7 %collective-permute-done.8 = bf16[192,512]{1,0:T(8,128)(2,1)S(1)} collective-permute-done((bf16[192,512]{1,0:T(8,128)(2,1)S(1)}, bf16[192,512]{1,0:T(8,128)(2,1)S(1)}, u32[]{:S(2)}, u32[]{:S(2)}) %collective-permute-start.8) | collective-permute-done | bytes 196640 | tf_op jit(solution)/shard_map/ppermute | solution.py:24
  91.9 0.8 collective-permute-done.9
  93.2 12.8 %all-gather.2.cloned.1.call-done = bf16[4096,1536]{1,0:T(8,128)(2,1)} async-done(((bf16[256,1536]{1,0:T(8,128)(2,1)}), bf16[4096,1536]{1,0:T(8,128)(2,1)}) %all-gather.2.cloned.1.call-update) | async-done | bytes 12582928 | tf_op jit(solution)/shard_map/all_gather | solution.py:264
  106.1 7.9 %shard_map.57 = (bf16[8,144,512]{2,1,0:T(8,128)(2,1)}, bf16[8,64,512]{2,1,0:T(8,128)(2,1)}) custom-call(bf16[384,4096]{1,0:T(8,128)(2,1)S(1)} %constant_dynamic-update-slice_fusion.8.acts_ref, bf16[8,2,4,64,1536]{4,3,2,1,0:T(8,128)(2,1)} %bitcast.7, f32[192,1]{1,0:T(8,128)S(1)} %copy.6.inv_rms_ref), custom_call_target="tpu_custom_call" | custom-call | flops 3623878656 | bytes 17301504 | tf_op jit(solution)/shard_map/pallas_call | solution.py:121
  114.0 7.2 %all-to-all-start.1 = ((bf16[8,144,512]{2,1,0:T(8,128)(2,1)}), bf16[8,144,512]{2,1,0:T(8,128)(2,1)S(1)}, u32[]{:S(2)}, u32[]{:S(2)}) async-start(bf16[8,144,512]{2,1,0:T(8,128)(2,1)} %get-tuple-element.28), calls=%async_computation.1 | async-start | bytes 2359296 | tf_op jit(solution)/shard_map/all_to_all | solution.py:298
  123.2 30.1 %all-to-all-done.1.terms_ref = bf16[8,144,512]{2,1,0:T(8,128)(2,1)S(1)} async-done(((bf16[8,144,512]{2,1,0:T(8,128)(2,1)}), bf16[8,144,512]{2,1,0:T(8,128)(2,1)S(1)}, u32[]{:S(2)}, u32[]{:S(2)}) %all-to-all-start.1) | async-done | bytes 1179680 | tf_op jit(solution)/shard_map/all_to_all | solution.py:298
  153.3 1.8 %shard_map.58 = bf16[192,512]{1,0:T(8,128)(2,1)} custom-call(s32[192]{0:T(256)S(1)} %copy-done.10, s32[192,1]{1,0:T(8,128)S(1)} %copy.7.ids_column_ref, bf16[8,144,512]{2,1,0:T(8,128)(2,1)S(1)} %all-to-all-done.1.terms_ref, f32[56,512]{1,0:T(8,128)S(1)} %get-tuple-element.37.rest_ref, f32[192,512]{1,0:T(8,128)S(1)} %copy-done.3, f32[192,512]{1,0:T(8,128)S(1)} %copy-done.5, ...), custom_call_target="tpu_custom_call" | custom-call | tf_op jit(solution)/shard_map/pallas_call | solution.py:248
  (40 shorter events, 3.9 us)
Async XLA Ops:
  6.5 99.5 %all-gather.2.cloned.1.call-start = ((), (), s32[]{:S(2)}) async-start(), calls=%async_computation.2 | async-start | bytes 13369344 | tf_op jit(solution)/shard_map/all_gather | solution.py:264
  20.9 0.9 copy-start
  21.8 0.9 copy-start.6
  22.7 0.7 copy-start.9
  24.2 12.1 %collective-permute-start = (f32[1,1280]{1,0:T(1,128)S(1)}, f32[1,1280]{1,0:T(1,128)S(1)}, u32[]{:S(2)}, u32[]{:S(2)}) collective-permute-start(f32[1,1280]{1,0:T(1,128)S(1)} %get-tuple-element.25), channel_id=1, source_target_pairs={{8,0},{16,8},{24,16},{32,24},{40,32},{48,40},{56,48},{64,56},{72,6... | collective-permute-start | bytes 15368 | tf_op jit(solution)/shard_map/ppermute | solution.py:19
  34.4 3.1 %collective-permute-start.1 = (f32[1,1280]{1,0:T(1,128)S(1)}, f32[1,1280]{1,0:T(1,128)S(1)}, u32[]{:S(2)}, u32[]{:S(2)}) collective-permute-start(f32[1,1280]{1,0:T(1,128)S(1)} %get-tuple-element.26), channel_id=1, source_target_pairs={{0,8},{8,16},{16,24},{24,32},{32,40},{40,48},{48,56},{56,64},{64,7... | collective-permute-start | bytes 15368 | tf_op jit(solution)/shard_map/ppermute | solution.py:19
  38.2 0.7 copy-start.2
  39.0 0.7 copy-start.4
  39.7 0.6 copy-start.7
  40.3 15.1 %collective-permute-start.2 = (bf16[384,512]{1,0:T(8,128)(2,1)S(1)}, bf16[384,512]{1,0:T(8,128)(2,1)}, u32[]{:S(2)}, u32[]{:S(2)}) collective-permute-start(bf16[384,512]{1,0:T(8,128)(2,1)S(1)} %get-tuple-element.27), channel_id=1, source_target_pairs={{0,1},{1,2},{2,3},{3,4},{4,5},{5,6},{6,7},{7,0},{8,9},{9,10},{10,1... | collective-permute-start | bytes 1179656 | tf_op jit(solution)/shard_map/ppermute | solution.py:24
  42.3 15.1 %collective-permute-start.3 = (bf16[384,512]{1,0:T(8,128)(2,1)S(1)}, bf16[384,512]{1,0:T(8,128)(2,1)}, u32[]{:S(2)}, u32[]{:S(2)}) collective-permute-start(bf16[384,512]{1,0:T(8,128)(2,1)S(1)} %get-tuple-element.27), channel_id=1, source_target_pairs={{0,7},{1,0},{2,1},{3,2},{4,3},{5,4},{6,5},{7,6},{8,15},{9,8},{10,9... | collective-permute-start | bytes 1179656 | tf_op jit(solution)/shard_map/ppermute | solution.py:24
  55.5 14.4 %collective-permute-start.4 = (bf16[384,512]{1,0:T(8,128)(2,1)}, bf16[384,512]{1,0:T(8,128)(2,1)}, u32[]{:S(2)}, u32[]{:S(2)}) collective-permute-start(bf16[384,512]{1,0:T(8,128)(2,1)} %collective-permute-done.2), channel_id=1, source_target_pairs={{0,1},{1,2},{2,3},{3,4},{4,5},{5,6},{6,7},{7,0},{8,9},{9,10},{10,1... | collective-permute-start | bytes 1179656 | tf_op jit(solution)/shard_map/ppermute | solution.py:24
  57.4 14.4 %collective-permute-start.5 = (bf16[384,512]{1,0:T(8,128)(2,1)}, bf16[384,512]{1,0:T(8,128)(2,1)}, u32[]{:S(2)}, u32[]{:S(2)}) collective-permute-start(bf16[384,512]{1,0:T(8,128)(2,1)} %collective-permute-done.3), channel_id=1, source_target_pairs={{0,7},{1,0},{2,1},{3,2},{4,3},{5,4},{6,5},{7,6},{8,15},{9,8},{10,9... | collective-permute-start | bytes 1179656 | tf_op jit(solution)/shard_map/ppermute | solution.py:24
  69.9 13.6 %collective-permute-start.6 = (bf16[384,512]{1,0:T(8,128)(2,1)}, bf16[384,512]{1,0:T(8,128)(2,1)S(1)}, u32[]{:S(2)}, u32[]{:S(2)}) collective-permute-start(bf16[384,512]{1,0:T(8,128)(2,1)} %collective-permute-done.4), channel_id=1, source_target_pairs={{0,1},{1,2},{2,3},{3,4},{4,5},{5,6},{6,7},{7,0},{8,9},{9,10},{10,1... | collective-permute-start | bytes 1179656 | tf_op jit(solution)/shard_map/ppermute | solution.py:24
  71.8 13.6 %collective-permute-start.7 = (bf16[384,512]{1,0:T(8,128)(2,1)}, bf16[384,512]{1,0:T(8,128)(2,1)S(1)}, u32[]{:S(2)}, u32[]{:S(2)}) collective-permute-start(bf16[384,512]{1,0:T(8,128)(2,1)} %collective-permute-done.5), channel_id=1, source_target_pairs={{0,7},{1,0},{2,1},{3,2},{4,3},{5,4},{6,5},{7,6},{8,15},{9,8},{10,9... | collective-permute-start | bytes 1179656 | tf_op jit(solution)/shard_map/ppermute | solution.py:24
  83.5 8.4 %collective-permute-start.8 = (bf16[192,512]{1,0:T(8,128)(2,1)S(1)}, bf16[192,512]{1,0:T(8,128)(2,1)S(1)}, u32[]{:S(2)}, u32[]{:S(2)}) collective-permute-start(bf16[192,512]{1,0:T(8,128)(2,1)S(1)} %slice.24), channel_id=1, source_target_pairs={{0,1},{1,2},{2,3},{3,4},{4,5},{5,6},{6,7},{7,0},{8,9},{9,10},{10,1... | collective-permute-start | bytes 589832 | tf_op jit(solution)/shard_map/ppermute | solution.py:24
  85.5 7.2 %collective-permute-start.9 = (bf16[192,512]{1,0:T(8,128)(2,1)S(1)}, bf16[192,512]{1,0:T(8,128)(2,1)S(1)}, u32[]{:S(2)}, u32[]{:S(2)}) collective-permute-start(bf16[192,512]{1,0:T(8,128)(2,1)S(1)} %slice.25), channel_id=1, source_target_pairs={{0,7},{1,0},{2,1},{3,2},{4,3},{5,4},{6,5},{7,6},{8,15},{9,8},{10,9... | collective-permute-start | bytes 589832 | tf_op jit(solution)/shard_map/ppermute | solution.py:24
  106.1 15.2 %copy-start.10 = (s32[192]{0:T(256)S(1)}, s32[192]{0:T(256)}, u32[]{:S(2)}) copy-start(s32[192]{0:T(256)} %ids_ref.5) | copy-start | bytes 2308
  113.9 39.4 %copy-start.1 = (bf16[192,512]{1,0:T(8,128)(2,1)S(1)}, bf16[192,512]{1,0:T(8,128)(2,1)}, u32[]{:S(2)}) copy-start(bf16[192,512]{1,0:T(8,128)(2,1)} %upstream_ref.3) | copy-start | bytes 589828
  114.0 39.4 %copy-start.3 = (f32[192,512]{1,0:T(8,128)S(1)}, f32[192,512]{1,0:T(8,128)}, u32[]{:S(2)}) copy-start(f32[192,512]{1,0:T(8,128)} %copy-done.2) | copy-start | bytes 1179652
  114.0 39.4 %copy-start.5 = (f32[192,512]{1,0:T(8,128)S(1)}, f32[192,512]{1,0:T(8,128)}, u32[]{:S(2)}) copy-start(f32[192,512]{1,0:T(8,128)} %copy-done.4) | copy-start | bytes 1179652
  114.0 39.4 %copy-start.8 = (f32[192,1]{1,0:T(8,128)S(1)}, f32[192,1]{1,0:T(8,128)}, u32[]{:S(2)}) copy-start(f32[192,1]{1,0:T(8,128)} %copy-done.7) | copy-start | bytes 2308
  114.0 39.3 %all-to-all-start.1 = ((bf16[8,144,512]{2,1,0:T(8,128)(2,1)}), bf16[8,144,512]{2,1,0:T(8,128)(2,1)S(1)}, u32[]{:S(2)}, u32[]{:S(2)}) async-start(bf16[8,144,512]{2,1,0:T(8,128)(2,1)} %get-tuple-element.28), calls=%async_computation.1 | async-start | bytes 2359296 | tf_op jit(solution)/shard_map/all_to_all | solution.py:298
Sparse Core Ops, SparseCore 0:
  21.0 85.0 all-gather.1

commit v9 on v8

--- a/solution.py
+++ b/solution.py
@@ -49,12 +49,12 @@
     acts_ref, weights_hbm, inv_rms_ref, out_hbm, rest_hbm, weights_ref, turned_ref, mixed_ref, out_ref, rest_ref, sems, out_sems
 ):
     rows = inv_rms_ref.shape[0]
-    hidden = weights_ref.shape[-1] // 2
+    hidden = weights_ref.shape[-1]
     blocks, kept, width = out_ref.shape
     copies = [
         [
             pltpu.make_async_copy(
-                weights_hbm.at[y, core], weights_ref.at[y, :, core], sems.at[y, core]
+                weights_hbm.at[y, core], weights_ref.at[y, :, :, core], sems.at[y, core]
             )
             for core in range(weights_hbm.shape[1])
         ]
@@ -65,35 +65,36 @@
             copy.start()
     per_chunk = len(copies) // blocks
 
-    def chunk(k, columns):
-        own = weights_ref[k * per_chunk : (k + 1) * per_chunk, :, :, :, columns]
-        return own.reshape(width, hidden)
-
-    first, second = slice(0, hidden), slice(hidden, 2 * hidden)
+    def chunk(k, which):
+        return weights_ref[k * per_chunk : (k + 1) * per_chunk, :, which].reshape(width, hidden)
+
     up_proj = back_proj = jnp.zeros((rows, hidden), jnp.float32)
     for k in range(blocks):
         for pair in copies[k * per_chunk : (k + 1) * per_chunk]:
             for copy in pair:
                 copy.wait()
         at = pl.ds(k * width, width)
-        own = chunk(k, first)
+        own = chunk(k, 0)
         up_proj += jnp.dot(acts_ref[:rows, at], own, preferred_element_type=jnp.float32)
         turned_ref[k] = own.T
         back_proj += jnp.dot(
-            acts_ref[rows:, at], chunk(k, second), preferred_element_type=jnp.float32
+            acts_ref[rows:, at], chunk(k, 1), preferred_element_type=jnp.float32
         )
     up_proj = up_proj * inv_rms_ref[...]
     sigmoid_up = jax.nn.sigmoid(up_proj)
     grad_hidden = (back_proj * sigmoid_up * (1.0 + up_proj * (1.0 - sigmoid_up))).astype(
         jnp.bfloat16
     )
-    dots = lax.dot_general(
-        jnp.ones((4, hidden), jnp.float32),
-        grad_hidden.astype(jnp.float32) * up_proj,
-        (((1,), (1,)), ((), ())),
-        precision=lax.Precision.HIGHEST,
-        preferred_element_type=jnp.float32,
-    )
+    product = grad_hidden.astype(jnp.float32) * up_proj
+    ones = jnp.ones((16, hidden), jnp.bfloat16)
+    dots = jnp.zeros((16, rows), jnp.float32)
+    for _ in range(2):
+        part = product.astype(jnp.bfloat16)
+        product = product - part.astype(jnp.float32)
+        dots += lax.dot_general(
+            ones, part, (((1,), (1,)), ((), ())), preferred_element_type=jnp.float32
+        )
+    dots = dots[:4]
     high = dots.astype(jnp.bfloat16).astype(jnp.float32)
     mixed_ref[...] = jnp.zeros_like(mixed_ref)
     mixed_ref[8:, :rows] = jnp.concatenate([high, dots - high], axis=0)
@@ -114,7 +115,7 @@
 
 def block_terms(gathered, weights, inv_rms, width, kept):
     rows, depth = gathered.shape[0] // 2, gathered.shape[1]
-    hidden = weights.shape[1] // 2
+    hidden = weights.shape[1]
     blocks = depth // width
     count_y, count_x, count_core = sizes
     part = depth // (count_y * count_x * count_core)
@@ -131,7 +132,7 @@
             pltpu.HBM((blocks, rows - kept + 16, width), jnp.bfloat16),
         ],
         scratch_shapes=[
-            pltpu.VMEM((count_y, count_x, count_core, part, 2 * hidden), jnp.bfloat16),
+            pltpu.VMEM((count_y, count_x, 2, count_core, part, hidden), jnp.bfloat16),
             pltpu.VMEM((blocks, hidden, width), jnp.bfloat16),
             pltpu.VMEM((16, width), jnp.float32),
             pltpu.VMEM((blocks, kept, width), jnp.bfloat16),
@@ -145,7 +146,7 @@
             bytes_accessed=2 * (2 * rows * depth + 2 * depth * hidden + rows * depth),
             transcendentals=rows * hidden,
         ),
-    )(gathered, weights.reshape(count_y, count_core, count_x, part, 2 * hidden), inv_rms)
+    )(gathered, weights.reshape(count_y, count_core, count_x, 2, part, hidden), inv_rms)
 
 
 def sums_kernel(ids_ref, ids_row_ref, acts_ref, upstream_ref, seg_ref, grad_ref, count_ref, first_ref, last_ref):
@@ -259,7 +260,7 @@
 def body(byte_acts, upstream, segment_ids, first_weight, second_weight):
     byte_rows, width = byte_acts.shape
     model_width = width * lax.axis_size("tp")
-    weights = jnp.concatenate([first_weight, second_weight], axis=1)
+    weights = jnp.concatenate([first_weight, second_weight], axis=0)
     weights = lax.all_gather(weights, "x", axis=0, tiled=True)
     weights = lax.all_gather(weights, ("y", "core"), axis=0, tiled=True)
 

time: 163 us -> 162 us (level)
  no operation moved by 1% of the time
where the time goes in v9:
time: 162 us
  waiting for transfers between devices  63.6 us (39%)
  starting transfers between devices  47.1 us (29%)
  between operations  15 us (9%)
  blocking collectives  13.3 us (8%)
  Pallas kernels  11 us (7%)
  local copies, waits for them, and re-layouts  10.3 us (6%)
    all_to_all x1, waiting for transfers between devices, exchanged(): return lax.all_to_all(a, 'tp', split_axis=0, concat_axis=0, tiled=True)  30.1 us
    ppermute x8, starting transfers between devices, turned(): lax.ppermute(shard, 'tp', [(i, (i + by) % count) for i in range(count)])  27.8 us
    ppermute x8, waiting for transfers between devices, turned(): lax.ppermute(shard, 'tp', [(i, (i + by) % count) for i in range(count)])  19.5 us
    all_gather x1, blocking collectives, body(): weights = lax.all_gather(weights, 'x', axis=0, tiled=True)  13.3 us
    all_gather x1, waiting for transfers between devices, body(): weights = lax.all_gather(weights, ('y', 'core'), axis=0, tiled=True)  12.8 us
    ppermute x2, starting transfers between devices, shifted(): return lax.ppermute(shard, axis, pairs)  12 us
    pallas_call x1, Pallas kernels, block_terms(): pl.pallas_call(block_kernel, in_specs=[pl.BlockSpec(memory_space=pltpu.VM...  7.55 us
    all_to_all x1, starting transfers between devices, exchanged(): return lax.all_to_all(a, 'tp', split_axis=0, concat_axis=0, tiled=True)  7.24 us
  transfers between devices with their start and end apart: 12, of which 8 were waited for; matrix products, arithmetic and copies ran while one was open for 4% of the time, Pallas kernels for 1%

profile of v9, /device:TPU:1, one launch (start us, length us, event | category | flops | bytes accessed | tf_op | source)
XLA Modules:
  0.0 161.6 jit_solution(9326791801503598587)
XLA Ops:
  6.5 1.0 pad_maximum_fusion
  7.5 13.3 %all_gather.6 = bf16[512,768]{1,0:T(8,128)(2,1)} all-gather(bf16[128,768]{1,0:T(8,128)(2,1)S(1)} %pad_maximum_fusion), channel_id=1, replica_groups=mesh['y'=8,'x'=4,'core'=2,'tp'=8] {'x'}, dimensions={0}, use_global_device_ids=true | all-gather | bytes 983040 | tf_op jit(solution)/shard_map/all_gather | solution.py:264
  20.9 0.9 copy-done
  21.8 0.9 copy-done.6
  23.4 0.8 shard_map.55
  24.2 10.1 %collective-permute-start = (f32[1,1280]{1,0:T(1,128)S(1)}, f32[1,1280]{1,0:T(1,128)S(1)}, u32[]{:S(2)}, u32[]{:S(2)}) collective-permute-start(f32[1,1280]{1,0:T(1,128)S(1)} %get-tuple-element.25), channel_id=1, source_target_pairs={{8,0},{16,8},{24,16},{32,24},{40,32},{48,40},{56,48},{64,56},{72,6... | collective-permute-start | bytes 15368 | tf_op jit(solution)/shard_map/ppermute | solution.py:19
  34.4 1.9 %collective-permute-start.1 = (f32[1,1280]{1,0:T(1,128)S(1)}, f32[1,1280]{1,0:T(1,128)S(1)}, u32[]{:S(2)}, u32[]{:S(2)}) collective-permute-start(f32[1,1280]{1,0:T(1,128)S(1)} %get-tuple-element.26), channel_id=1, source_target_pairs={{0,8},{8,16},{16,24},{24,32},{32,40},{40,48},{48,56},{56,64},{64,7... | collective-permute-start | bytes 15368 | tf_op jit(solution)/shard_map/ppermute | solution.py:19
  36.3 1.1 collective-permute-done.1.head_ref
  37.4 0.8 shard_map.56
  39.0 0.7 copy-done.4
  40.3 1.9 %collective-permute-start.2 = (bf16[384,512]{1,0:T(8,128)(2,1)S(1)}, bf16[384,512]{1,0:T(8,128)(2,1)}, u32[]{:S(2)}, u32[]{:S(2)}) collective-permute-start(bf16[384,512]{1,0:T(8,128)(2,1)S(1)} %get-tuple-element.27), channel_id=1, source_target_pairs={{0,1},{1,2},{2,3},{3,4},{4,5},{5,6},{6,7},{7,0},{8,9},{9,10},{10,1... | collective-permute-start | bytes 1179656 | tf_op jit(solution)/shard_map/ppermute | solution.py:24
  42.3 6.1 %collective-permute-start.3 = (bf16[384,512]{1,0:T(8,128)(2,1)S(1)}, bf16[384,512]{1,0:T(8,128)(2,1)}, u32[]{:S(2)}, u32[]{:S(2)}) collective-permute-start(bf16[384,512]{1,0:T(8,128)(2,1)S(1)} %get-tuple-element.27), channel_id=1, source_target_pairs={{0,7},{1,0},{2,1},{3,2},{4,3},{5,4},{6,5},{7,6},{8,15},{9,8},{10,9... | collective-permute-start | bytes 1179656 | tf_op jit(solution)/shard_map/ppermute | solution.py:24
  48.4 7.1 %collective-permute-done.2 = bf16[384,512]{1,0:T(8,128)(2,1)} collective-permute-done((bf16[384,512]{1,0:T(8,128)(2,1)S(1)}, bf16[384,512]{1,0:T(8,128)(2,1)}, u32[]{:S(2)}, u32[]{:S(2)}) %collective-permute-start.2) | collective-permute-done | bytes 393248 | tf_op jit(solution)/shard_map/ppermute | solution.py:24
  55.5 1.9 %collective-permute-start.4 = (bf16[384,512]{1,0:T(8,128)(2,1)}, bf16[384,512]{1,0:T(8,128)(2,1)}, u32[]{:S(2)}, u32[]{:S(2)}) collective-permute-start(bf16[384,512]{1,0:T(8,128)(2,1)} %collective-permute-done.2), channel_id=1, source_target_pairs={{0,1},{1,2},{2,3},{3,4},{4,5},{5,6},{6,7},{7,0},{8,9},{9,10},{10,1... | collective-permute-start | bytes 1179656 | tf_op jit(solution)/shard_map/ppermute | solution.py:24
  57.4 4.8 %collective-permute-start.5 = (bf16[384,512]{1,0:T(8,128)(2,1)}, bf16[384,512]{1,0:T(8,128)(2,1)}, u32[]{:S(2)}, u32[]{:S(2)}) collective-permute-start(bf16[384,512]{1,0:T(8,128)(2,1)} %collective-permute-done.3), channel_id=1, source_target_pairs={{0,7},{1,0},{2,1},{3,2},{4,3},{5,4},{6,5},{7,6},{8,15},{9,8},{10,9... | collective-permute-start | bytes 1179656 | tf_op jit(solution)/shard_map/ppermute | solution.py:24
  62.7 7.2 %collective-permute-done.4 = bf16[384,512]{1,0:T(8,128)(2,1)} collective-permute-done((bf16[384,512]{1,0:T(8,128)(2,1)}, bf16[384,512]{1,0:T(8,128)(2,1)}, u32[]{:S(2)}, u32[]{:S(2)}) %collective-permute-start.4) | collective-permute-done | bytes 393248 | tf_op jit(solution)/shard_map/ppermute | solution.py:24
  69.9 1.9 %collective-permute-start.6 = (bf16[384,512]{1,0:T(8,128)(2,1)}, bf16[384,512]{1,0:T(8,128)(2,1)S(1)}, u32[]{:S(2)}, u32[]{:S(2)}) collective-permute-start(bf16[384,512]{1,0:T(8,128)(2,1)} %collective-permute-done.4), channel_id=1, source_target_pairs={{0,1},{1,2},{2,3},{3,4},{4,5},{5,6},{6,7},{7,0},{8,9},{9,10},{10,1... | collective-permute-start | bytes 1179656 | tf_op jit(solution)/shard_map/ppermute | solution.py:24
  71.8 4.6 %collective-permute-start.7 = (bf16[384,512]{1,0:T(8,128)(2,1)}, bf16[384,512]{1,0:T(8,128)(2,1)S(1)}, u32[]{:S(2)}, u32[]{:S(2)}) collective-permute-start(bf16[384,512]{1,0:T(8,128)(2,1)} %collective-permute-done.5), channel_id=1, source_target_pairs={{0,7},{1,0},{2,1},{3,2},{4,3},{5,4},{6,5},{7,6},{8,15},{9,8},{10,9... | collective-permute-start | bytes 1179656 | tf_op jit(solution)/shard_map/ppermute | solution.py:24
  76.4 1.0 constant_dynamic-update-slice_fusion.6
  77.5 1.1 constant_dynamic-update-slice_fusion.5
  78.6 1.0 constant_dynamic-update-slice_fusion.4
  79.6 1.1 constant_dynamic-update-slice_fusion.3
  80.7 2.8 %collective-permute-done.6 = bf16[384,512]{1,0:T(8,128)(2,1)S(1)} collective-permute-done((bf16[384,512]{1,0:T(8,128)(2,1)}, bf16[384,512]{1,0:T(8,128)(2,1)S(1)}, u32[]{:S(2)}, u32[]{:S(2)}) %collective-permute-start.6) | collective-permute-done | bytes 393248 | tf_op jit(solution)/shard_map/ppermute | solution.py:24
  83.5 1.9 %collective-permute-start.8 = (bf16[192,512]{1,0:T(8,128)(2,1)S(1)}, bf16[192,512]{1,0:T(8,128)(2,1)S(1)}, u32[]{:S(2)}, u32[]{:S(2)}) collective-permute-start(bf16[192,512]{1,0:T(8,128)(2,1)S(1)} %slice.24), channel_id=1, source_target_pairs={{0,1},{1,2},{2,3},{3,4},{4,5},{5,6},{6,7},{7,0},{8,9},{9,10},{10,1... | collective-permute-start | bytes 589832 | tf_op jit(solution)/shard_map/ppermute | solution.py:24
  85.5 4.6 %collective-permute-start.9 = (bf16[192,512]{1,0:T(8,128)(2,1)S(1)}, bf16[192,512]{1,0:T(8,128)(2,1)S(1)}, u32[]{:S(2)}, u32[]{:S(2)}) collective-permute-start(bf16[192,512]{1,0:T(8,128)(2,1)S(1)} %slice.25), channel_id=1, source_target_pairs={{0,7},{1,0},{2,1},{3,2},{4,3},{5,4},{6,5},{7,6},{8,15},{9,8},{10,9... | collective-permute-start | bytes 589832 | tf_op jit(solution)/shard_map/ppermute | solution.py:24
  90.2 1.7 %collective-permute-done.8 = bf16[192,512]{1,0:T(8,128)(2,1)S(1)} collective-permute-done((bf16[192,512]{1,0:T(8,128)(2,1)S(1)}, bf16[192,512]{1,0:T(8,128)(2,1)S(1)}, u32[]{:S(2)}, u32[]{:S(2)}) %collective-permute-start.8) | collective-permute-done | bytes 196640 | tf_op jit(solution)/shard_map/ppermute | solution.py:24
  91.9 0.8 collective-permute-done.9
  93.2 12.8 %all-gather.2.cloned.1.call-done = bf16[8192,768]{1,0:T(8,128)(2,1)} async-done(((bf16[512,768]{1,0:T(8,128)(2,1)}), bf16[8192,768]{1,0:T(8,128)(2,1)}) %all-gather.2.cloned.1.call-update) | async-done | bytes 12582928 | tf_op jit(solution)/shard_map/all_gather | solution.py:265
  106.1 7.6 %shard_map.57 = (bf16[8,144,512]{2,1,0:T(8,128)(2,1)}, bf16[8,64,512]{2,1,0:T(8,128)(2,1)}) custom-call(bf16[384,4096]{1,0:T(8,128)(2,1)S(1)} %constant_dynamic-update-slice_fusion.8.acts_ref, bf16[8,2,4,2,64,768]{5,4,3,2,1,0:T(8,128)(2,1)} %bitcast.7, f32[192,1]{1,0:T(8,128)S(1)} %copy.6.inv_rms_ref), custom_call_target="tpu_custom_call" | custom-call | flops 3623878656 | bytes 17301504 | tf_op jit(solution)/shard_map/pallas_call | solution.py:122
  113.7 7.2 %all-to-all-start.1 = ((bf16[8,144,512]{2,1,0:T(8,128)(2,1)}), bf16[8,144,512]{2,1,0:T(8,128)(2,1)S(1)}, u32[]{:S(2)}, u32[]{:S(2)}) async-start(bf16[8,144,512]{2,1,0:T(8,128)(2,1)} %get-tuple-element.28), calls=%async_computation.1 | async-start | bytes 2359296 | tf_op jit(solution)/shard_map/all_to_all | solution.py:299
  122.9 30.1 %all-to-all-done.1.terms_ref = bf16[8,144,512]{2,1,0:T(8,128)(2,1)S(1)} async-done(((bf16[8,144,512]{2,1,0:T(8,128)(2,1)}), bf16[8,144,512]{2,1,0:T(8,128)(2,1)S(1)}, u32[]{:S(2)}, u32[]{:S(2)}) %all-to-all-start.1) | async-done | bytes 1179680 | tf_op jit(solution)/shard_map/all_to_all | solution.py:299
  153.0 1.8 %shard_map.58 = bf16[192,512]{1,0:T(8,128)(2,1)} custom-call(s32[192]{0:T(256)S(1)} %copy-done.10, s32[192,1]{1,0:T(8,128)S(1)} %copy.7.ids_column_ref, bf16[8,144,512]{2,1,0:T(8,128)(2,1)S(1)} %all-to-all-done.1.terms_ref, f32[56,512]{1,0:T(8,128)S(1)} %get-tuple-element.37.rest_ref, f32[192,512]{1,0:T(8,128)S(1)} %copy-done.3, f32[192,512]{1,0:T(8,128)S(1)} %copy-done.5, ...), custom_call_target="tpu_custom_call" | custom-call | tf_op jit(solution)/shard_map/pallas_call | solution.py:249
  (40 shorter events, 3.9 us)
Async XLA Ops:
  6.5 99.5 %all-gather.2.cloned.1.call-start = ((), (), s32[]{:S(2)}) async-start(), calls=%async_computation.2 | async-start | bytes 13369344 | tf_op jit(solution)/shard_map/all_gather | solution.py:265
  20.9 0.9 copy-start
  21.8 0.9 copy-start.6
  22.7 0.7 copy-start.9
  24.2 12.1 %collective-permute-start = (f32[1,1280]{1,0:T(1,128)S(1)}, f32[1,1280]{1,0:T(1,128)S(1)}, u32[]{:S(2)}, u32[]{:S(2)}) collective-permute-start(f32[1,1280]{1,0:T(1,128)S(1)} %get-tuple-element.25), channel_id=1, source_target_pairs={{8,0},{16,8},{24,16},{32,24},{40,32},{48,40},{56,48},{64,56},{72,6... | collective-permute-start | bytes 15368 | tf_op jit(solution)/shard_map/ppermute | solution.py:19
  34.4 3.1 %collective-permute-start.1 = (f32[1,1280]{1,0:T(1,128)S(1)}, f32[1,1280]{1,0:T(1,128)S(1)}, u32[]{:S(2)}, u32[]{:S(2)}) collective-permute-start(f32[1,1280]{1,0:T(1,128)S(1)} %get-tuple-element.26), channel_id=1, source_target_pairs={{0,8},{8,16},{16,24},{24,32},{32,40},{40,48},{48,56},{56,64},{64,7... | collective-permute-start | bytes 15368 | tf_op jit(solution)/shard_map/ppermute | solution.py:19
  38.2 0.7 copy-start.2
  39.0 0.7 copy-start.4
  39.7 0.6 copy-start.7
  40.3 15.1 %collective-permute-start.2 = (bf16[384,512]{1,0:T(8,128)(2,1)S(1)}, bf16[384,512]{1,0:T(8,128)(2,1)}, u32[]{:S(2)}, u32[]{:S(2)}) collective-permute-start(bf16[384,512]{1,0:T(8,128)(2,1)S(1)} %get-tuple-element.27), channel_id=1, source_target_pairs={{0,1},{1,2},{2,3},{3,4},{4,5},{5,6},{6,7},{7,0},{8,9},{9,10},{10,1... | collective-permute-start | bytes 1179656 | tf_op jit(solution)/shard_map/ppermute | solution.py:24
  42.3 15.1 %collective-permute-start.3 = (bf16[384,512]{1,0:T(8,128)(2,1)S(1)}, bf16[384,512]{1,0:T(8,128)(2,1)}, u32[]{:S(2)}, u32[]{:S(2)}) collective-permute-start(bf16[384,512]{1,0:T(8,128)(2,1)S(1)} %get-tuple-element.27), channel_id=1, source_target_pairs={{0,7},{1,0},{2,1},{3,2},{4,3},{5,4},{6,5},{7,6},{8,15},{9,8},{10,9... | collective-permute-start | bytes 1179656 | tf_op jit(solution)/shard_map/ppermute | solution.py:24
  55.5 14.4 %collective-permute-start.4 = (bf16[384,512]{1,0:T(8,128)(2,1)}, bf16[384,512]{1,0:T(8,128)(2,1)}, u32[]{:S(2)}, u32[]{:S(2)}) collective-permute-start(bf16[384,512]{1,0:T(8,128)(2,1)} %collective-permute-done.2), channel_id=1, source_target_pairs={{0,1},{1,2},{2,3},{3,4},{4,5},{5,6},{6,7},{7,0},{8,9},{9,10},{10,1... | collective-permute-start | bytes 1179656 | tf_op jit(solution)/shard_map/ppermute | solution.py:24
  57.4 14.4 %collective-permute-start.5 = (bf16[384,512]{1,0:T(8,128)(2,1)}, bf16[384,512]{1,0:T(8,128)(2,1)}, u32[]{:S(2)}, u32[]{:S(2)}) collective-permute-start(bf16[384,512]{1,0:T(8,128)(2,1)} %collective-permute-done.3), channel_id=1, source_target_pairs={{0,7},{1,0},{2,1},{3,2},{4,3},{5,4},{6,5},{7,6},{8,15},{9,8},{10,9... | collective-permute-start | bytes 1179656 | tf_op jit(solution)/shard_map/ppermute | solution.py:24
  69.9 13.6 %collective-permute-start.6 = (bf16[384,512]{1,0:T(8,128)(2,1)}, bf16[384,512]{1,0:T(8,128)(2,1)S(1)}, u32[]{:S(2)}, u32[]{:S(2)}) collective-permute-start(bf16[384,512]{1,0:T(8,128)(2,1)} %collective-permute-done.4), channel_id=1, source_target_pairs={{0,1},{1,2},{2,3},{3,4},{4,5},{5,6},{6,7},{7,0},{8,9},{9,10},{10,1... | collective-permute-start | bytes 1179656 | tf_op jit(solution)/shard_map/ppermute | solution.py:24
  71.8 13.6 %collective-permute-start.7 = (bf16[384,512]{1,0:T(8,128)(2,1)}, bf16[384,512]{1,0:T(8,128)(2,1)S(1)}, u32[]{:S(2)}, u32[]{:S(2)}) collective-permute-start(bf16[384,512]{1,0:T(8,128)(2,1)} %collective-permute-done.5), channel_id=1, source_target_pairs={{0,7},{1,0},{2,1},{3,2},{4,3},{5,4},{6,5},{7,6},{8,15},{9,8},{10,9... | collective-permute-start | bytes 1179656 | tf_op jit(solution)/shard_map/ppermute | solution.py:24
  83.5 8.4 %collective-permute-start.8 = (bf16[192,512]{1,0:T(8,128)(2,1)S(1)}, bf16[192,512]{1,0:T(8,128)(2,1)S(1)}, u32[]{:S(2)}, u32[]{:S(2)}) collective-permute-start(bf16[192,512]{1,0:T(8,128)(2,1)S(1)} %slice.24), channel_id=1, source_target_pairs={{0,1},{1,2},{2,3},{3,4},{4,5},{5,6},{6,7},{7,0},{8,9},{9,10},{10,1... | collective-permute-start | bytes 589832 | tf_op jit(solution)/shard_map/ppermute | solution.py:24
  85.5 7.2 %collective-permute-start.9 = (bf16[192,512]{1,0:T(8,128)(2,1)S(1)}, bf16[192,512]{1,0:T(8,128)(2,1)S(1)}, u32[]{:S(2)}, u32[]{:S(2)}) collective-permute-start(bf16[192,512]{1,0:T(8,128)(2,1)S(1)} %slice.25), channel_id=1, source_target_pairs={{0,7},{1,0},{2,1},{3,2},{4,3},{5,4},{6,5},{7,6},{8,15},{9,8},{10,9... | collective-permute-start | bytes 589832 | tf_op jit(solution)/shard_map/ppermute | solution.py:24
  106.1 14.8 %copy-start.10 = (s32[192]{0:T(256)S(1)}, s32[192]{0:T(256)}, u32[]{:S(2)}) copy-start(s32[192]{0:T(256)} %ids_ref.5) | copy-start | bytes 2308
  113.6 39.4 %copy-start.1 = (bf16[192,512]{1,0:T(8,128)(2,1)S(1)}, bf16[192,512]{1,0:T(8,128)(2,1)}, u32[]{:S(2)}) copy-start(bf16[192,512]{1,0:T(8,128)(2,1)} %upstream_ref.3) | copy-start | bytes 589828
  113.6 39.4 %copy-start.3 = (f32[192,512]{1,0:T(8,128)S(1)}, f32[192,512]{1,0:T(8,128)}, u32[]{:S(2)}) copy-start(f32[192,512]{1,0:T(8,128)} %copy-done.2) | copy-start | bytes 1179652
  113.6 39.4 %copy-start.5 = (f32[192,512]{1,0:T(8,128)S(1)}, f32[192,512]{1,0:T(8,128)}, u32[]{:S(2)}) copy-start(f32[192,512]{1,0:T(8,128)} %copy-done.4) | copy-start | bytes 1179652
  113.6 39.4 %copy-start.8 = (f32[192,1]{1,0:T(8,128)S(1)}, f32[192,1]{1,0:T(8,128)}, u32[]{:S(2)}) copy-start(f32[192,1]{1,0:T(8,128)} %copy-done.7) | copy-start | bytes 2308
  113.7 39.3 %all-to-all-start.1 = ((bf16[8,144,512]{2,1,0:T(8,128)(2,1)}), bf16[8,144,512]{2,1,0:T(8,128)(2,1)S(1)}, u32[]{:S(2)}, u32[]{:S(2)}) async-start(bf16[8,144,512]{2,1,0:T(8,128)(2,1)} %get-tuple-element.28), calls=%async_computation.1 | async-start | bytes 2359296 | tf_op jit(solution)/shard_map/all_to_all | solution.py:299
Sparse Core Ops, SparseCore 0:
  21.0 85.0 all-gather.1

commit v10 on v9

--- a/solution.py
+++ b/solution.py
@@ -194,21 +194,44 @@
     safe_ref[...] = safe
 
 
-def last_kernel(
+def membership(ids_ref, ids_column_ref, rows):
+    slot = lax.broadcasted_iota(jnp.int32, (rows, rows), 1)
+    return slot == ids_column_ref[...] - ids_ref[0]
+
+
+def spread(member, share):
+    member = member.astype(jnp.float32).astype(jnp.bfloat16)
+    high = share.astype(jnp.bfloat16)
+    low = (share - high.astype(jnp.float32)).astype(jnp.bfloat16)
+    return jnp.dot(member, low, preferred_element_type=jnp.float32) + jnp.dot(
+        member, high, preferred_element_type=jnp.float32
+    )
+
+
+def ahead_kernel(
     model_width,
     ids_ref,
     ids_column_ref,
-    terms_ref,
-    rest_ref,
     pooled_ref,
     sums_ref,
     safe_ref,
     inv_rms_ref,
     upstream_ref,
-    out_ref,
-    share_ref,
+    known_ref,
+    slope_ref,
+    scale_ref,
 ):
-    rows = pooled_ref.shape[0]
+    member = membership(ids_ref, ids_column_ref, pooled_ref.shape[0])
+    scale = inv_rms_ref[...] / safe_ref[...]
+    known_ref[...] = upstream_ref[...].astype(jnp.float32) + spread(member, sums_ref[...] / safe_ref[...])
+    slope_ref[...] = spread(member, pooled_ref[...] * (scale * inv_rms_ref[...] * (1.0 / model_width)))
+    scale_ref[...] = scale
+
+
+def last_kernel(
+    ids_ref, ids_column_ref, terms_ref, rest_ref, known_ref, slope_ref, scale_ref, out_ref, share_ref
+):
+    rows = known_ref.shape[0]
     blocks, kept, _ = terms_ref.shape
     even = kept - 16
     norm_grad = terms_ref[0, :even].astype(jnp.float32)
@@ -216,30 +239,15 @@
     for block in range(1, blocks):
         norm_grad += terms_ref[block, :even].astype(jnp.float32)
         mixed += terms_ref[block, even:].astype(jnp.float32)
+    share_ref[:even] = norm_grad * scale_ref[:even]
+    share_ref[even : even + 8] = mixed[:8] * scale_ref[even : even + 8]
+    share_ref[even + 8 :] = rest_ref[...] * scale_ref[even + 8 :]
+    member = membership(ids_ref, ids_column_ref, rows)
     dots = mixed[8:9, :rows] + mixed[12:13, :rows]
-    slot = lax.broadcasted_iota(jnp.int32, (rows, rows), 1)
-    diagonal = lax.broadcasted_iota(jnp.int32, (rows, rows), 0) == slot
-    norm_dot = jnp.sum(jnp.where(diagonal, dots, 0.0), axis=1, keepdims=True)
-
-    def share(at, norm_grad):
-        inv_rms = inv_rms_ref[at]
-        normed = pooled_ref[at] * inv_rms
-        mean = norm_dot[at] * (1.0 / model_width)
-        pooled_grad = sums_ref[at] + inv_rms * (norm_grad - normed * mean)
-        share_ref[at] = pooled_grad / safe_ref[at]
-
-    share(slice(0, even), norm_grad)
-    share(slice(even, even + 8), mixed[:8])
-    share(slice(even + 8, rows), rest_ref[...])
-    member = (slot == ids_column_ref[...] - ids_ref[0]).astype(jnp.float32).astype(jnp.bfloat16)
-    left = share_ref[...]
-    spread = upstream_ref[...].astype(jnp.float32)
-    parts = []
-    for _ in range(2):
-        part = left.astype(jnp.bfloat16)
-        left = left - part.astype(jnp.float32)
-        parts.append(jnp.dot(member, part, preferred_element_type=jnp.float32))
-    out_ref[...] = (spread + (parts[1] + parts[0])).astype(jnp.bfloat16)
+    norm_dot = jnp.sum(jnp.where(member, dots, 0.0), axis=1, keepdims=True)
+    out_ref[...] = (known_ref[...] - slope_ref[...] * norm_dot + spread(member, share_ref[...])).astype(
+        jnp.bfloat16
+    )
 
 
 def on_core(kernel, out_shape, *operands, scratch=()):
@@ -292,6 +300,19 @@
     square_sums = jnp.sum(jnp.square(pooled_b.astype(jnp.float32)), axis=1)
     inv_rms = lax.rsqrt(square_sums / model_width + epsilon)[:, None]
 
+    ids_column = segment_ids.reshape(byte_rows, 1)
+    known, slope, scale = on_core(
+        functools.partial(ahead_kernel, model_width),
+        [whole, whole, column],
+        segment_ids,
+        ids_column,
+        pooled,
+        grad_sums,
+        safe_counts,
+        inv_rms,
+        upstream,
+    )
+
     kept = 144
     sent, rest = block_terms(gathered, weights, inv_rms, width, kept)
 
@@ -306,17 +327,15 @@
         rest,
     )
     return on_core(
-        functools.partial(last_kernel, model_width),
+        last_kernel,
         array(byte_rows, width, jnp.bfloat16),
         segment_ids,
-        segment_ids.reshape(byte_rows, 1),
+        ids_column,
         terms,
         rest_grad,
-        pooled,
-        grad_sums,
-        safe_counts,
-        inv_rms,
-        upstream,
+        known,
+        slope,
+        scale,
         scratch=[pltpu.VMEM((byte_rows, width), jnp.float32)],
     )
 

time: 162 us -> 162 us (level)
  waiting for transfers between devices: 63.6 us -> 60.6 us
  local copies, waits for them, and re-layouts: 10.3 us -> 12.2 us
    all_to_all x1, waiting for transfers between devices: 30.1 us -> 27.1 us  [exchanged(): return lax.all_to_all(a, 'tp', split_axis=0, concat_axis=0, tiled=True)]
    unnamed x22, local copies, waits for them, and re-layouts: 4.66 us -> 6.64 us
    pallas_call x3 -> x4, Pallas kernels: 3.4 us -> 4.29 us  [on_core(): pl.pallas_call(kernel, grid=(1,), in_specs=[pl.BlockSpec(memory_space=plt...]
  transfers between devices with their start and end apart: 12 -> 12, of which waited for: 8 -> 8; matrix products, arithmetic and copies ran while one was open for 4% -> 4% of each run, Pallas kernels for 1% -> 2%
where the time goes in v10:
time: 162 us; the launch traced here: 161 us
  waiting for transfers between devices  60.6 us (37%)
  starting transfers between devices  47 us (29%)
  between operations  15 us (9%)
  blocking collectives  13.3 us (8%)
  local copies, waits for them, and re-layouts  12.2 us (8%)
  Pallas kernels  11.9 us (7%)
    ppermute x8, starting transfers between devices, turned(): lax.ppermute(shard, 'tp', [(i, (i + by) % count) for i in range(count)])  27.8 us
    all_to_all x1, waiting for transfers between devices, exchanged(): return lax.all_to_all(a, 'tp', split_axis=0, concat_axis=0, tiled=True)  27.1 us
    ppermute x8, waiting for transfers between devices, turned(): lax.ppermute(shard, 'tp', [(i, (i + by) % count) for i in range(count)])  19.5 us
    all_gather x1, blocking collectives, body(): weights = lax.all_gather(weights, 'x', axis=0, tiled=True)  13.3 us
    all_gather x1, waiting for transfers between devices, body(): weights = lax.all_gather(weights, ('y', 'core'), axis=0, tiled=True)  12.8 us
    ppermute x2, starting transfers between devices, shifted(): return lax.ppermute(shard, axis, pairs)  12 us
    pallas_call x1, Pallas kernels, block_terms(): pl.pallas_call(block_kernel, in_specs=[pl.BlockSpec(memory_space=pltpu.VM...  7.58 us
    all_to_all x1, starting transfers between devices, exchanged(): return lax.all_to_all(a, 'tp', split_axis=0, concat_axis=0, tiled=True)  7.11 us
  transfers between devices with their start and end apart: 12, of which 8 were waited for; matrix products, arithmetic and copies ran while one was open for 4% of the time, Pallas kernels for 2%

profile of v10, /device:TPU:1, one launch (start us, length us, event | category | flops | bytes accessed | tf_op | source)
XLA Modules:
  0.0 161.3 jit_solution(5844090138386464404)
XLA Ops:
  6.5 1.0 pad_maximum_fusion
  7.5 13.3 %all_gather.6 = bf16[512,768]{1,0:T(8,128)(2,1)} all-gather(bf16[128,768]{1,0:T(8,128)(2,1)S(1)} %pad_maximum_fusion), channel_id=1, replica_groups=mesh['y'=8,'x'=4,'core'=2,'tp'=8] {'x'}, dimensions={0}, use_global_device_ids=true | all-gather | bytes 983040 | tf_op jit(solution)/shard_map/all_gather | solution.py:272
  20.9 0.9 copy-done
  21.8 0.9 copy-done.6
  23.4 0.8 shard_map.55
  24.2 10.1 %collective-permute-start = (f32[1,1280]{1,0:T(1,128)S(1)}, f32[1,1280]{1,0:T(1,128)S(1)}, u32[]{:S(2)}, u32[]{:S(2)}) collective-permute-start(f32[1,1280]{1,0:T(1,128)S(1)} %get-tuple-element.28), channel_id=1, source_target_pairs={{8,0},{16,8},{24,16},{32,24},{40,32},{48,40},{56,48},{64,56},{72,6... | collective-permute-start | bytes 15368 | tf_op jit(solution)/shard_map/ppermute | solution.py:19
  34.4 1.9 %collective-permute-start.1 = (f32[1,1280]{1,0:T(1,128)S(1)}, f32[1,1280]{1,0:T(1,128)S(1)}, u32[]{:S(2)}, u32[]{:S(2)}) collective-permute-start(f32[1,1280]{1,0:T(1,128)S(1)} %get-tuple-element.29), channel_id=1, source_target_pairs={{0,8},{8,16},{16,24},{24,32},{32,40},{40,48},{48,56},{56,64},{64,7... | collective-permute-start | bytes 15368 | tf_op jit(solution)/shard_map/ppermute | solution.py:19
  36.3 1.1 collective-permute-done.1.head_ref
  40.4 1.9 %collective-permute-start.2 = (bf16[384,512]{1,0:T(8,128)(2,1)S(1)}, bf16[384,512]{1,0:T(8,128)(2,1)}, u32[]{:S(2)}, u32[]{:S(2)}) collective-permute-start(bf16[384,512]{1,0:T(8,128)(2,1)S(1)} %get-tuple-element.30), channel_id=1, source_target_pairs={{0,1},{1,2},{2,3},{3,4},{4,5},{5,6},{6,7},{7,0},{8,9},{9,10},{10,1... | collective-permute-start | bytes 1179656 | tf_op jit(solution)/shard_map/ppermute | solution.py:24
  42.3 6.1 %collective-permute-start.3 = (bf16[384,512]{1,0:T(8,128)(2,1)S(1)}, bf16[384,512]{1,0:T(8,128)(2,1)}, u32[]{:S(2)}, u32[]{:S(2)}) collective-permute-start(bf16[384,512]{1,0:T(8,128)(2,1)S(1)} %get-tuple-element.30), channel_id=1, source_target_pairs={{0,7},{1,0},{2,1},{3,2},{4,3},{5,4},{6,5},{7,6},{8,15},{9,8},{10,9... | collective-permute-start | bytes 1179656 | tf_op jit(solution)/shard_map/ppermute | solution.py:24
  48.4 7.1 %collective-permute-done.2 = bf16[384,512]{1,0:T(8,128)(2,1)} collective-permute-done((bf16[384,512]{1,0:T(8,128)(2,1)S(1)}, bf16[384,512]{1,0:T(8,128)(2,1)}, u32[]{:S(2)}, u32[]{:S(2)}) %collective-permute-start.2) | collective-permute-done | bytes 393248 | tf_op jit(solution)/shard_map/ppermute | solution.py:24
  55.5 1.9 %collective-permute-start.4 = (bf16[384,512]{1,0:T(8,128)(2,1)}, bf16[384,512]{1,0:T(8,128)(2,1)}, u32[]{:S(2)}, u32[]{:S(2)}) collective-permute-start(bf16[384,512]{1,0:T(8,128)(2,1)} %collective-permute-done.2), channel_id=1, source_target_pairs={{0,1},{1,2},{2,3},{3,4},{4,5},{5,6},{6,7},{7,0},{8,9},{9,10},{10,1... | collective-permute-start | bytes 1179656 | tf_op jit(solution)/shard_map/ppermute | solution.py:24
  57.4 4.8 %collective-permute-start.5 = (bf16[384,512]{1,0:T(8,128)(2,1)}, bf16[384,512]{1,0:T(8,128)(2,1)}, u32[]{:S(2)}, u32[]{:S(2)}) collective-permute-start(bf16[384,512]{1,0:T(8,128)(2,1)} %collective-permute-done.3), channel_id=1, source_target_pairs={{0,7},{1,0},{2,1},{3,2},{4,3},{5,4},{6,5},{7,6},{8,15},{9,8},{10,9... | collective-permute-start | bytes 1179656 | tf_op jit(solution)/shard_map/ppermute | solution.py:24
  62.7 7.2 %collective-permute-done.4 = bf16[384,512]{1,0:T(8,128)(2,1)} collective-permute-done((bf16[384,512]{1,0:T(8,128)(2,1)}, bf16[384,512]{1,0:T(8,128)(2,1)}, u32[]{:S(2)}, u32[]{:S(2)}) %collective-permute-start.4) | collective-permute-done | bytes 393248 | tf_op jit(solution)/shard_map/ppermute | solution.py:24
  69.9 1.9 %collective-permute-start.6 = (bf16[384,512]{1,0:T(8,128)(2,1)}, bf16[384,512]{1,0:T(8,128)(2,1)S(1)}, u32[]{:S(2)}, u32[]{:S(2)}) collective-permute-start(bf16[384,512]{1,0:T(8,128)(2,1)} %collective-permute-done.4), channel_id=1, source_target_pairs={{0,1},{1,2},{2,3},{3,4},{4,5},{5,6},{6,7},{7,0},{8,9},{9,10},{10,1... | collective-permute-start | bytes 1179656 | tf_op jit(solution)/shard_map/ppermute | solution.py:24
  71.8 4.6 %collective-permute-start.7 = (bf16[384,512]{1,0:T(8,128)(2,1)}, bf16[384,512]{1,0:T(8,128)(2,1)S(1)}, u32[]{:S(2)}, u32[]{:S(2)}) collective-permute-start(bf16[384,512]{1,0:T(8,128)(2,1)} %collective-permute-done.5), channel_id=1, source_target_pairs={{0,7},{1,0},{2,1},{3,2},{4,3},{5,4},{6,5},{7,6},{8,15},{9,8},{10,9... | collective-permute-start | bytes 1179656 | tf_op jit(solution)/shard_map/ppermute | solution.py:24
  76.5 1.0 constant_dynamic-update-slice_fusion.6
  77.5 1.1 constant_dynamic-update-slice_fusion.5
  78.6 1.0 constant_dynamic-update-slice_fusion.4
  79.6 1.1 constant_dynamic-update-slice_fusion.3
  80.7 2.8 %collective-permute-done.6 = bf16[384,512]{1,0:T(8,128)(2,1)S(1)} collective-permute-done((bf16[384,512]{1,0:T(8,128)(2,1)}, bf16[384,512]{1,0:T(8,128)(2,1)S(1)}, u32[]{:S(2)}, u32[]{:S(2)}) %collective-permute-start.6) | collective-permute-done | bytes 393248 | tf_op jit(solution)/shard_map/ppermute | solution.py:24
  83.5 1.9 %collective-permute-start.8 = (bf16[192,512]{1,0:T(8,128)(2,1)S(1)}, bf16[192,512]{1,0:T(8,128)(2,1)S(1)}, u32[]{:S(2)}, u32[]{:S(2)}) collective-permute-start(bf16[192,512]{1,0:T(8,128)(2,1)S(1)} %slice.24), channel_id=1, source_target_pairs={{0,1},{1,2},{2,3},{3,4},{4,5},{5,6},{6,7},{7,0},{8,9},{9,10},{10,1... | collective-permute-start | bytes 589832 | tf_op jit(solution)/shard_map/ppermute | solution.py:24
  85.5 4.6 %collective-permute-start.9 = (bf16[192,512]{1,0:T(8,128)(2,1)S(1)}, bf16[192,512]{1,0:T(8,128)(2,1)S(1)}, u32[]{:S(2)}, u32[]{:S(2)}) collective-permute-start(bf16[192,512]{1,0:T(8,128)(2,1)S(1)} %slice.25), channel_id=1, source_target_pairs={{0,7},{1,0},{2,1},{3,2},{4,3},{5,4},{6,5},{7,6},{8,15},{9,8},{10,9... | collective-permute-start | bytes 589832 | tf_op jit(solution)/shard_map/ppermute | solution.py:24
  90.2 1.7 %collective-permute-done.8 = bf16[192,512]{1,0:T(8,128)(2,1)S(1)} collective-permute-done((bf16[192,512]{1,0:T(8,128)(2,1)S(1)}, bf16[192,512]{1,0:T(8,128)(2,1)S(1)}, u32[]{:S(2)}, u32[]{:S(2)}) %collective-permute-start.8) | collective-permute-done | bytes 196640 | tf_op jit(solution)/shard_map/ppermute | solution.py:24
  93.2 12.8 %all-gather.2.cloned.1.call-done = bf16[8192,768]{1,0:T(8,128)(2,1)} async-done(((bf16[512,768]{1,0:T(8,128)(2,1)}), bf16[8192,768]{1,0:T(8,128)(2,1)}) %all-gather.2.cloned.1.call-update) | async-done | bytes 12582928 | tf_op jit(solution)/shard_map/all_gather | solution.py:273
  106.1 7.6 %shard_map.57 = (bf16[8,144,512]{2,1,0:T(8,128)(2,1)}, bf16[8,64,512]{2,1,0:T(8,128)(2,1)}) custom-call(bf16[384,4096]{1,0:T(8,128)(2,1)S(1)} %constant_dynamic-update-slice_fusion.8.acts_ref, bf16[8,2,4,2,64,768]{5,4,3,2,1,0:T(8,128)(2,1)} %bitcast.7, f32[192,1]{1,0:T(8,128)S(1)} %copy.6.inv_rms_ref), custom_call_target="tpu_custom_call" | custom-call | flops 3623878656 | bytes 17301504 | tf_op jit(solution)/shard_map/pallas_call | solution.py:122
  113.6 7.1 %all-to-all-start.1 = ((bf16[8,144,512]{2,1,0:T(8,128)(2,1)}), bf16[8,144,512]{2,1,0:T(8,128)(2,1)S(1)}, u32[]{:S(2)}, u32[]{:S(2)}) async-start(bf16[8,144,512]{2,1,0:T(8,128)(2,1)} %get-tuple-element.31), calls=%async_computation.1 | async-start | bytes 2359296 | tf_op jit(solution)/shard_map/all_to_all | solution.py:320
  122.7 1.0 copy-done.3
  123.7 1.0 copy-done.5
  124.7 1.0 shard_map.58
  125.7 27.1 %all-to-all-done.1.terms_ref = bf16[8,144,512]{2,1,0:T(8,128)(2,1)S(1)} async-done(((bf16[8,144,512]{2,1,0:T(8,128)(2,1)}), bf16[8,144,512]{2,1,0:T(8,128)(2,1)S(1)}, u32[]{:S(2)}, u32[]{:S(2)}) %all-to-all-start.1) | async-done | bytes 1179680 | tf_op jit(solution)/shard_map/all_to_all | solution.py:320
  152.8 1.6 %shard_map.59 = bf16[192,512]{1,0:T(8,128)(2,1)} custom-call(s32[192]{0:T(256)S(1)} %copy-done.10, s32[192,1]{1,0:T(8,128)S(1)} %copy.9.ids_column_ref, bf16[8,144,512]{2,1,0:T(8,128)(2,1)S(1)} %all-to-all-done.1.terms_ref, f32[56,512]{1,0:T(8,128)S(1)} %get-tuple-element.43.rest_ref, f32[192,512]{1,0:T(8,128)S(1)} %get-tuple-element.38.known_ref, ...), custom_call_target="tpu_custom_call" | custom-call | tf_op jit(solution)/shard_map/pallas_call | solution.py:257
  (41 shorter events, 6.2 us)
Async XLA Ops:
  6.5 99.5 %all-gather.2.cloned.1.call-start = ((), (), s32[]{:S(2)}) async-start(), calls=%async_computation.2 | async-start | bytes 13369344 | tf_op jit(solution)/shard_map/all_gather | solution.py:273
  20.9 0.9 copy-start
  21.8 0.9 copy-start.6
  22.7 0.7 copy-start.9
  24.2 12.1 %collective-permute-start = (f32[1,1280]{1,0:T(1,128)S(1)}, f32[1,1280]{1,0:T(1,128)S(1)}, u32[]{:S(2)}, u32[]{:S(2)}) collective-permute-start(f32[1,1280]{1,0:T(1,128)S(1)} %get-tuple-element.28), channel_id=1, source_target_pairs={{8,0},{16,8},{24,16},{32,24},{40,32},{48,40},{56,48},{64,56},{72,6... | collective-permute-start | bytes 15368 | tf_op jit(solution)/shard_map/ppermute | solution.py:19
  34.4 3.1 %collective-permute-start.1 = (f32[1,1280]{1,0:T(1,128)S(1)}, f32[1,1280]{1,0:T(1,128)S(1)}, u32[]{:S(2)}, u32[]{:S(2)}) collective-permute-start(f32[1,1280]{1,0:T(1,128)S(1)} %get-tuple-element.29), channel_id=1, source_target_pairs={{0,8},{8,16},{16,24},{24,32},{32,40},{40,48},{48,56},{56,64},{64,7... | collective-permute-start | bytes 15368 | tf_op jit(solution)/shard_map/ppermute | solution.py:19
  38.2 0.7 copy-start.2
  39.0 0.7 copy-start.4
  39.7 0.6 copy-start.7
  40.4 15.1 %collective-permute-start.2 = (bf16[384,512]{1,0:T(8,128)(2,1)S(1)}, bf16[384,512]{1,0:T(8,128)(2,1)}, u32[]{:S(2)}, u32[]{:S(2)}) collective-permute-start(bf16[384,512]{1,0:T(8,128)(2,1)S(1)} %get-tuple-element.30), channel_id=1, source_target_pairs={{0,1},{1,2},{2,3},{3,4},{4,5},{5,6},{6,7},{7,0},{8,9},{9,10},{10,1... | collective-permute-start | bytes 1179656 | tf_op jit(solution)/shard_map/ppermute | solution.py:24
  42.3 15.1 %collective-permute-start.3 = (bf16[384,512]{1,0:T(8,128)(2,1)S(1)}, bf16[384,512]{1,0:T(8,128)(2,1)}, u32[]{:S(2)}, u32[]{:S(2)}) collective-permute-start(bf16[384,512]{1,0:T(8,128)(2,1)S(1)} %get-tuple-element.30), channel_id=1, source_target_pairs={{0,7},{1,0},{2,1},{3,2},{4,3},{5,4},{6,5},{7,6},{8,15},{9,8},{10,9... | collective-permute-start | bytes 1179656 | tf_op jit(solution)/shard_map/ppermute | solution.py:24
  55.5 14.4 %collective-permute-start.4 = (bf16[384,512]{1,0:T(8,128)(2,1)}, bf16[384,512]{1,0:T(8,128)(2,1)}, u32[]{:S(2)}, u32[]{:S(2)}) collective-permute-start(bf16[384,512]{1,0:T(8,128)(2,1)} %collective-permute-done.2), channel_id=1, source_target_pairs={{0,1},{1,2},{2,3},{3,4},{4,5},{5,6},{6,7},{7,0},{8,9},{9,10},{10,1... | collective-permute-start | bytes 1179656 | tf_op jit(solution)/shard_map/ppermute | solution.py:24
  57.4 14.4 %collective-permute-start.5 = (bf16[384,512]{1,0:T(8,128)(2,1)}, bf16[384,512]{1,0:T(8,128)(2,1)}, u32[]{:S(2)}, u32[]{:S(2)}) collective-permute-start(bf16[384,512]{1,0:T(8,128)(2,1)} %collective-permute-done.3), channel_id=1, source_target_pairs={{0,7},{1,0},{2,1},{3,2},{4,3},{5,4},{6,5},{7,6},{8,15},{9,8},{10,9... | collective-permute-start | bytes 1179656 | tf_op jit(solution)/shard_map/ppermute | solution.py:24
  69.9 13.6 %collective-permute-start.6 = (bf16[384,512]{1,0:T(8,128)(2,1)}, bf16[384,512]{1,0:T(8,128)(2,1)S(1)}, u32[]{:S(2)}, u32[]{:S(2)}) collective-permute-start(bf16[384,512]{1,0:T(8,128)(2,1)} %collective-permute-done.4), channel_id=1, source_target_pairs={{0,1},{1,2},{2,3},{3,4},{4,5},{5,6},{6,7},{7,0},{8,9},{9,10},{10,1... | collective-permute-start | bytes 1179656 | tf_op jit(solution)/shard_map/ppermute | solution.py:24
  71.8 13.6 %collective-permute-start.7 = (bf16[384,512]{1,0:T(8,128)(2,1)}, bf16[384,512]{1,0:T(8,128)(2,1)S(1)}, u32[]{:S(2)}, u32[]{:S(2)}) collective-permute-start(bf16[384,512]{1,0:T(8,128)(2,1)} %collective-permute-done.5), channel_id=1, source_target_pairs={{0,7},{1,0},{2,1},{3,2},{4,3},{5,4},{6,5},{7,6},{8,15},{9,8},{10,9... | collective-permute-start | bytes 1179656 | tf_op jit(solution)/shard_map/ppermute | solution.py:24
  83.5 8.4 %collective-permute-start.8 = (bf16[192,512]{1,0:T(8,128)(2,1)S(1)}, bf16[192,512]{1,0:T(8,128)(2,1)S(1)}, u32[]{:S(2)}, u32[]{:S(2)}) collective-permute-start(bf16[192,512]{1,0:T(8,128)(2,1)S(1)} %slice.24), channel_id=1, source_target_pairs={{0,1},{1,2},{2,3},{3,4},{4,5},{5,6},{6,7},{7,0},{8,9},{9,10},{10,1... | collective-permute-start | bytes 589832 | tf_op jit(solution)/shard_map/ppermute | solution.py:24
  85.5 7.2 %collective-permute-start.9 = (bf16[192,512]{1,0:T(8,128)(2,1)S(1)}, bf16[192,512]{1,0:T(8,128)(2,1)S(1)}, u32[]{:S(2)}, u32[]{:S(2)}) collective-permute-start(bf16[192,512]{1,0:T(8,128)(2,1)S(1)} %slice.25), channel_id=1, source_target_pairs={{0,7},{1,0},{2,1},{3,2},{4,3},{5,4},{6,5},{7,6},{8,15},{9,8},{10,9... | collective-permute-start | bytes 589832 | tf_op jit(solution)/shard_map/ppermute | solution.py:24
  106.1 14.7 %copy-start.10 = (s32[192]{0:T(256)S(1)}, s32[192]{0:T(256)}, u32[]{:S(2)}) copy-start(s32[192]{0:T(256)} %ids_ref.7) | copy-start | bytes 2308
  106.1 16.6 %copy-start.1 = (bf16[192,512]{1,0:T(8,128)(2,1)S(1)}, bf16[192,512]{1,0:T(8,128)(2,1)}, u32[]{:S(2)}) copy-start(bf16[192,512]{1,0:T(8,128)(2,1)} %upstream_ref.3) | copy-start | bytes 589828
  106.1 16.6 %copy-start.8 = (f32[192,1]{1,0:T(8,128)S(1)}, f32[192,1]{1,0:T(8,128)}, u32[]{:S(2)}) copy-start(f32[192,1]{1,0:T(8,128)} %copy-done.7) | copy-start | bytes 2308
  113.6 39.2 %all-to-all-start.1 = ((bf16[8,144,512]{2,1,0:T(8,128)(2,1)}), bf16[8,144,512]{2,1,0:T(8,128)(2,1)S(1)}, u32[]{:S(2)}, u32[]{:S(2)}) async-start(bf16[8,144,512]{2,1,0:T(8,128)(2,1)} %get-tuple-element.31), calls=%async_computation.1 | async-start | bytes 2359296 | tf_op jit(solution)/shard_map/all_to_all | solution.py:320
  122.7 1.0 copy-start.3
  123.7 1.0 copy-start.5
Sparse Core Ops, SparseCore 0:
  21.0 85.0 all-gather.1

commit v11 on v10

--- a/solution.py
+++ b/solution.py
@@ -194,6 +194,18 @@
     safe_ref[...] = safe
 
 
+def stack_kernel(first_hbm, second_hbm, out_hbm, sems):
+    rows = first_hbm.shape[0]
+    copies = [
+        pltpu.make_async_copy(first_hbm, out_hbm.at[pl.ds(0, rows)], sems.at[0]),
+        pltpu.make_async_copy(second_hbm, out_hbm.at[pl.ds(rows, rows)], sems.at[1]),
+    ]
+    for copy in copies:
+        copy.start()
+    for copy in copies:
+        copy.wait()
+
+
 def membership(ids_ref, ids_column_ref, rows):
     slot = lax.broadcasted_iota(jnp.int32, (rows, rows), 1)
     return slot == ids_column_ref[...] - ids_ref[0]
@@ -268,7 +280,13 @@
 def body(byte_acts, upstream, segment_ids, first_weight, second_weight):
     byte_rows, width = byte_acts.shape
     model_width = width * lax.axis_size("tp")
-    weights = jnp.concatenate([first_weight, second_weight], axis=0)
+    weights = pl.pallas_call(
+        stack_kernel,
+        in_specs=[pl.BlockSpec(memory_space=pltpu.HBM)] * 2,
+        out_specs=pl.BlockSpec(memory_space=pltpu.HBM),
+        out_shape=pltpu.HBM((2 * first_weight.shape[0], first_weight.shape[1]), first_weight.dtype),
+        scratch_shapes=[pltpu.SemaphoreType.DMA((2,))],
+    )(first_weight, second_weight)
     weights = lax.all_gather(weights, "x", axis=0, tiled=True)
     weights = lax.all_gather(weights, ("y", "core"), axis=0, tiled=True)
 

time: 162 us -> 168 us (1.037)
  Pallas kernels: 11.9 us -> 19 us
    pallas_call x0 -> x1, Pallas kernels: none -> 7.07 us  [body(): pl.pallas_call(stack_kernel, in_specs=[pl.BlockSpec(memory_space=pltpu.HB...]
where the time goes in v11:
time: 168 us; the launch traced here: 167 us
  waiting for transfers between devices  60 us (36%)
  starting transfers between devices  46.8 us (28%)
  Pallas kernels  19 us (11%)
  between operations  15 us (9%)
  blocking collectives  14 us (8%)
  local copies, waits for them, and re-layouts  12.2 us (7%)
    ppermute x8, starting transfers between devices, turned(): lax.ppermute(shard, 'tp', [(i, (i + by) % count) for i in range(count)])  28 us
    all_to_all x1, waiting for transfers between devices, exchanged(): return lax.all_to_all(a, 'tp', split_axis=0, concat_axis=0, tiled=True)  27.1 us
    ppermute x8, waiting for transfers between devices, turned(): lax.ppermute(shard, 'tp', [(i, (i + by) % count) for i in range(count)])  18.3 us
    all_gather x1, blocking collectives, body(): weights = lax.all_gather(weights, 'x', axis=0, tiled=True)  14 us
    all_gather x1, waiting for transfers between devices, body(): weights = lax.all_gather(weights, ('y', 'core'), axis=0, tiled=True)  13.9 us
    ppermute x2, starting transfers between devices, shifted(): return lax.ppermute(shard, axis, pairs)  11.7 us
    pallas_call x1, Pallas kernels, block_terms(): pl.pallas_call(block_kernel, in_specs=[pl.BlockSpec(memory_space=pltpu.VM...  7.58 us
    all_to_all x1, starting transfers between devices, exchanged(): return lax.all_to_all(a, 'tp', split_axis=0, concat_axis=0, tiled=True)  7.11 us
  transfers between devices with their start and end apart: 12, of which 8 were waited for; matrix products, arithmetic and copies ran while one was open for 4% of the time, Pallas kernels for 2%

profile of v11, /device:TPU:1, one launch (start us, length us, event | category | flops | bytes accessed | tf_op | source)
XLA Modules:
  0.0 167.4 jit_solution(5516368355293690157)
XLA Ops:
  6.5 7.1 %shard_map.57 = bf16[128,768]{1,0:T(8,128)(2,1)} custom-call(bf16[64,768]{1,0:T(8,128)(2,1)} %first_hbm.1, bf16[64,768]{1,0:T(8,128)(2,1)} %second_hbm.1), custom_call_target="tpu_custom_call" | custom-call | tf_op jit(solution)/shard_map/pallas_call | solution.py:283
  13.6 14.0 %all_gather.6 = bf16[512,768]{1,0:T(8,128)(2,1)} all-gather(bf16[128,768]{1,0:T(8,128)(2,1)} %shard_map.57), channel_id=1, replica_groups=mesh['y'=8,'x'=4,'core'=2,'tp'=8] {'x'}, dimensions={0}, use_global_device_ids=true | all-gather | bytes 983040 | tf_op jit(solution)/shard_map/all_gather | solution.py:290
  27.7 0.9 copy-done
  28.6 0.9 copy-done.6
  30.2 0.8 shard_map.55
  31.1 9.5 %collective-permute-start = (f32[1,1280]{1,0:T(1,128)S(1)}, f32[1,1280]{1,0:T(1,128)S(1)}, u32[]{:S(2)}, u32[]{:S(2)}) collective-permute-start(f32[1,1280]{1,0:T(1,128)S(1)} %get-tuple-element.28), channel_id=1, source_target_pairs={{8,0},{16,8},{24,16},{32,24},{40,32},{48,40},{56,48},{64,56},{72,6... | collective-permute-start | bytes 15368 | tf_op jit(solution)/shard_map/ppermute | solution.py:19
  40.5 2.3 %collective-permute-start.1 = (f32[1,1280]{1,0:T(1,128)S(1)}, f32[1,1280]{1,0:T(1,128)S(1)}, u32[]{:S(2)}, u32[]{:S(2)}) collective-permute-start(f32[1,1280]{1,0:T(1,128)S(1)} %get-tuple-element.29), channel_id=1, source_target_pairs={{0,8},{8,16},{16,24},{24,32},{32,40},{40,48},{48,56},{56,64},{64,7... | collective-permute-start | bytes 15368 | tf_op jit(solution)/shard_map/ppermute | solution.py:19
  46.5 1.9 %collective-permute-start.2 = (bf16[384,512]{1,0:T(8,128)(2,1)S(1)}, bf16[384,512]{1,0:T(8,128)(2,1)}, u32[]{:S(2)}, u32[]{:S(2)}) collective-permute-start(bf16[384,512]{1,0:T(8,128)(2,1)S(1)} %get-tuple-element.30), channel_id=1, source_target_pairs={{0,1},{1,2},{2,3},{3,4},{4,5},{5,6},{6,7},{7,0},{8,9},{9,10},{10,1... | collective-permute-start | bytes 1179656 | tf_op jit(solution)/shard_map/ppermute | solution.py:24
  48.4 6.6 %collective-permute-start.3 = (bf16[384,512]{1,0:T(8,128)(2,1)S(1)}, bf16[384,512]{1,0:T(8,128)(2,1)}, u32[]{:S(2)}, u32[]{:S(2)}) collective-permute-start(bf16[384,512]{1,0:T(8,128)(2,1)S(1)} %get-tuple-element.30), channel_id=1, source_target_pairs={{0,7},{1,0},{2,1},{3,2},{4,3},{5,4},{6,5},{7,6},{8,15},{9,8},{10,9... | collective-permute-start | bytes 1179656 | tf_op jit(solution)/shard_map/ppermute | solution.py:24
  55.0 7.6 %collective-permute-done.2 = bf16[384,512]{1,0:T(8,128)(2,1)} collective-permute-done((bf16[384,512]{1,0:T(8,128)(2,1)S(1)}, bf16[384,512]{1,0:T(8,128)(2,1)}, u32[]{:S(2)}, u32[]{:S(2)}) %collective-permute-start.2) | collective-permute-done | bytes 393248 | tf_op jit(solution)/shard_map/ppermute | solution.py:24
  62.6 1.9 %collective-permute-start.4 = (bf16[384,512]{1,0:T(8,128)(2,1)}, bf16[384,512]{1,0:T(8,128)(2,1)}, u32[]{:S(2)}, u32[]{:S(2)}) collective-permute-start(bf16[384,512]{1,0:T(8,128)(2,1)} %collective-permute-done.2), channel_id=1, source_target_pairs={{0,1},{1,2},{2,3},{3,4},{4,5},{5,6},{6,7},{7,0},{8,9},{9,10},{10,1... | collective-permute-start | bytes 1179656 | tf_op jit(solution)/shard_map/ppermute | solution.py:24
  64.5 4.6 %collective-permute-start.5 = (bf16[384,512]{1,0:T(8,128)(2,1)}, bf16[384,512]{1,0:T(8,128)(2,1)}, u32[]{:S(2)}, u32[]{:S(2)}) collective-permute-start(bf16[384,512]{1,0:T(8,128)(2,1)} %collective-permute-done.3), channel_id=1, source_target_pairs={{0,7},{1,0},{2,1},{3,2},{4,3},{5,4},{6,5},{7,6},{8,15},{9,8},{10,9... | collective-permute-start | bytes 1179656 | tf_op jit(solution)/shard_map/ppermute | solution.py:24
  69.6 6.4 %collective-permute-done.4 = bf16[384,512]{1,0:T(8,128)(2,1)} collective-permute-done((bf16[384,512]{1,0:T(8,128)(2,1)}, bf16[384,512]{1,0:T(8,128)(2,1)}, u32[]{:S(2)}, u32[]{:S(2)}) %collective-permute-start.4) | collective-permute-done | bytes 393248 | tf_op jit(solution)/shard_map/ppermute | solution.py:24
  76.0 1.9 %collective-permute-start.6 = (bf16[384,512]{1,0:T(8,128)(2,1)}, bf16[384,512]{1,0:T(8,128)(2,1)S(1)}, u32[]{:S(2)}, u32[]{:S(2)}) collective-permute-start(bf16[384,512]{1,0:T(8,128)(2,1)} %collective-permute-done.4), channel_id=1, source_target_pairs={{0,1},{1,2},{2,3},{3,4},{4,5},{5,6},{6,7},{7,0},{8,9},{9,10},{10,1... | collective-permute-start | bytes 1179656 | tf_op jit(solution)/shard_map/ppermute | solution.py:24
  77.9 4.6 %collective-permute-start.7 = (bf16[384,512]{1,0:T(8,128)(2,1)}, bf16[384,512]{1,0:T(8,128)(2,1)S(1)}, u32[]{:S(2)}, u32[]{:S(2)}) collective-permute-start(bf16[384,512]{1,0:T(8,128)(2,1)} %collective-permute-done.5), channel_id=1, source_target_pairs={{0,7},{1,0},{2,1},{3,2},{4,3},{5,4},{6,5},{7,6},{8,15},{9,8},{10,9... | collective-permute-start | bytes 1179656 | tf_op jit(solution)/shard_map/ppermute | solution.py:24
  82.5 1.0 constant_dynamic-update-slice_fusion.6
  83.6 1.1 constant_dynamic-update-slice_fusion.5
  84.6 1.0 constant_dynamic-update-slice_fusion.4
  85.7 1.1 constant_dynamic-update-slice_fusion.3
  86.7 1.8 %collective-permute-done.6 = bf16[384,512]{1,0:T(8,128)(2,1)S(1)} collective-permute-done((bf16[384,512]{1,0:T(8,128)(2,1)}, bf16[384,512]{1,0:T(8,128)(2,1)S(1)}, u32[]{:S(2)}, u32[]{:S(2)}) %collective-permute-start.6) | collective-permute-done | bytes 393248 | tf_op jit(solution)/shard_map/ppermute | solution.py:24
  88.5 1.9 %collective-permute-start.8 = (bf16[192,512]{1,0:T(8,128)(2,1)S(1)}, bf16[192,512]{1,0:T(8,128)(2,1)S(1)}, u32[]{:S(2)}, u32[]{:S(2)}) collective-permute-start(bf16[192,512]{1,0:T(8,128)(2,1)S(1)} %slice.24), channel_id=1, source_target_pairs={{0,1},{1,2},{2,3},{3,4},{4,5},{5,6},{6,7},{7,0},{8,9},{9,10},{10,1... | collective-permute-start | bytes 589832 | tf_op jit(solution)/shard_map/ppermute | solution.py:24
  90.5 4.6 %collective-permute-start.9 = (bf16[192,512]{1,0:T(8,128)(2,1)S(1)}, bf16[192,512]{1,0:T(8,128)(2,1)S(1)}, u32[]{:S(2)}, u32[]{:S(2)}) collective-permute-start(bf16[192,512]{1,0:T(8,128)(2,1)S(1)} %slice.25), channel_id=1, source_target_pairs={{0,7},{1,0},{2,1},{3,2},{4,3},{5,4},{6,5},{7,6},{8,15},{9,8},{10,9... | collective-permute-start | bytes 589832 | tf_op jit(solution)/shard_map/ppermute | solution.py:24
  95.2 1.4 collective-permute-done.8
  96.6 1.1 collective-permute-done.9
  98.2 13.9 %all-gather.2.cloned.1.call-done = bf16[8192,768]{1,0:T(8,128)(2,1)} async-done(((bf16[512,768]{1,0:T(8,128)(2,1)}), bf16[8192,768]{1,0:T(8,128)(2,1)}) %all-gather.2.cloned.1.call-update) | async-done | bytes 12582928 | tf_op jit(solution)/shard_map/all_gather | solution.py:291
  112.1 7.6 %shard_map.58 = (bf16[8,144,512]{2,1,0:T(8,128)(2,1)}, bf16[8,64,512]{2,1,0:T(8,128)(2,1)}) custom-call(bf16[384,4096]{1,0:T(8,128)(2,1)S(1)} %constant_dynamic-update-slice_fusion.8.acts_ref, bf16[8,2,4,2,64,768]{5,4,3,2,1,0:T(8,128)(2,1)} %bitcast.7, f32[192,1]{1,0:T(8,128)S(1)} %copy.6.inv_rms_ref), custom_call_target="tpu_custom_call" | custom-call | flops 3623878656 | bytes 17301504 | tf_op jit(solution)/shard_map/pallas_call | solution.py:122
  119.7 7.1 %all-to-all-start.1 = ((bf16[8,144,512]{2,1,0:T(8,128)(2,1)}), bf16[8,144,512]{2,1,0:T(8,128)(2,1)S(1)}, u32[]{:S(2)}, u32[]{:S(2)}) async-start(bf16[8,144,512]{2,1,0:T(8,128)(2,1)} %get-tuple-element.31), calls=%async_computation.1 | async-start | bytes 2359296 | tf_op jit(solution)/shard_map/all_to_all | solution.py:338
  128.8 1.0 copy-done.3
  129.8 1.0 copy-done.5
  130.8 1.0 shard_map.59
  131.8 27.1 %all-to-all-done.1.terms_ref = bf16[8,144,512]{2,1,0:T(8,128)(2,1)S(1)} async-done(((bf16[8,144,512]{2,1,0:T(8,128)(2,1)}), bf16[8,144,512]{2,1,0:T(8,128)(2,1)S(1)}, u32[]{:S(2)}, u32[]{:S(2)}) %all-to-all-start.1) | async-done | bytes 1179680 | tf_op jit(solution)/shard_map/all_to_all | solution.py:338
  158.9 1.7 shard_map.60
  (41 shorter events, 6.2 us)
Async XLA Ops:
  6.5 105.6 %all-gather.2.cloned.1.call-start = ((), (), s32[]{:S(2)}) async-start(), calls=%async_computation.2 | async-start | bytes 13369344 | tf_op jit(solution)/shard_map/all_gather | solution.py:291
  27.7 0.9 copy-start
  28.6 0.9 copy-start.6
  29.5 0.7 copy-start.9
  31.1 11.7 %collective-permute-start = (f32[1,1280]{1,0:T(1,128)S(1)}, f32[1,1280]{1,0:T(1,128)S(1)}, u32[]{:S(2)}, u32[]{:S(2)}) collective-permute-start(f32[1,1280]{1,0:T(1,128)S(1)} %get-tuple-element.28), channel_id=1, source_target_pairs={{8,0},{16,8},{24,16},{32,24},{40,32},{48,40},{56,48},{64,56},{72,6... | collective-permute-start | bytes 15368 | tf_op jit(solution)/shard_map/ppermute | solution.py:19
  40.5 3.1 %collective-permute-start.1 = (f32[1,1280]{1,0:T(1,128)S(1)}, f32[1,1280]{1,0:T(1,128)S(1)}, u32[]{:S(2)}, u32[]{:S(2)}) collective-permute-start(f32[1,1280]{1,0:T(1,128)S(1)} %get-tuple-element.29), channel_id=1, source_target_pairs={{0,8},{8,16},{16,24},{24,32},{32,40},{40,48},{48,56},{56,64},{64,7... | collective-permute-start | bytes 15368 | tf_op jit(solution)/shard_map/ppermute | solution.py:19
  44.4 0.7 copy-start.2
  45.1 0.7 copy-start.4
  45.9 0.6 copy-start.7
  46.5 16.1 %collective-permute-start.2 = (bf16[384,512]{1,0:T(8,128)(2,1)S(1)}, bf16[384,512]{1,0:T(8,128)(2,1)}, u32[]{:S(2)}, u32[]{:S(2)}) collective-permute-start(bf16[384,512]{1,0:T(8,128)(2,1)S(1)} %get-tuple-element.30), channel_id=1, source_target_pairs={{0,1},{1,2},{2,3},{3,4},{4,5},{5,6},{6,7},{7,0},{8,9},{9,10},{10,1... | collective-permute-start | bytes 1179656 | tf_op jit(solution)/shard_map/ppermute | solution.py:24
  48.4 16.1 %collective-permute-start.3 = (bf16[384,512]{1,0:T(8,128)(2,1)S(1)}, bf16[384,512]{1,0:T(8,128)(2,1)}, u32[]{:S(2)}, u32[]{:S(2)}) collective-permute-start(bf16[384,512]{1,0:T(8,128)(2,1)S(1)} %get-tuple-element.30), channel_id=1, source_target_pairs={{0,7},{1,0},{2,1},{3,2},{4,3},{5,4},{6,5},{7,6},{8,15},{9,8},{10,9... | collective-permute-start | bytes 1179656 | tf_op jit(solution)/shard_map/ppermute | solution.py:24
  62.6 13.4 %collective-permute-start.4 = (bf16[384,512]{1,0:T(8,128)(2,1)}, bf16[384,512]{1,0:T(8,128)(2,1)}, u32[]{:S(2)}, u32[]{:S(2)}) collective-permute-start(bf16[384,512]{1,0:T(8,128)(2,1)} %collective-permute-done.2), channel_id=1, source_target_pairs={{0,1},{1,2},{2,3},{3,4},{4,5},{5,6},{6,7},{7,0},{8,9},{9,10},{10,1... | collective-permute-start | bytes 1179656 | tf_op jit(solution)/shard_map/ppermute | solution.py:24
  64.5 13.4 %collective-permute-start.5 = (bf16[384,512]{1,0:T(8,128)(2,1)}, bf16[384,512]{1,0:T(8,128)(2,1)}, u32[]{:S(2)}, u32[]{:S(2)}) collective-permute-start(bf16[384,512]{1,0:T(8,128)(2,1)} %collective-permute-done.3), channel_id=1, source_target_pairs={{0,7},{1,0},{2,1},{3,2},{4,3},{5,4},{6,5},{7,6},{8,15},{9,8},{10,9... | collective-permute-start | bytes 1179656 | tf_op jit(solution)/shard_map/ppermute | solution.py:24
  76.0 12.5 %collective-permute-start.6 = (bf16[384,512]{1,0:T(8,128)(2,1)}, bf16[384,512]{1,0:T(8,128)(2,1)S(1)}, u32[]{:S(2)}, u32[]{:S(2)}) collective-permute-start(bf16[384,512]{1,0:T(8,128)(2,1)} %collective-permute-done.4), channel_id=1, source_target_pairs={{0,1},{1,2},{2,3},{3,4},{4,5},{5,6},{6,7},{7,0},{8,9},{9,10},{10,1... | collective-permute-start | bytes 1179656 | tf_op jit(solution)/shard_map/ppermute | solution.py:24
  77.9 12.5 %collective-permute-start.7 = (bf16[384,512]{1,0:T(8,128)(2,1)}, bf16[384,512]{1,0:T(8,128)(2,1)S(1)}, u32[]{:S(2)}, u32[]{:S(2)}) collective-permute-start(bf16[384,512]{1,0:T(8,128)(2,1)} %collective-permute-done.5), channel_id=1, source_target_pairs={{0,7},{1,0},{2,1},{3,2},{4,3},{5,4},{6,5},{7,6},{8,15},{9,8},{10,9... | collective-permute-start | bytes 1179656 | tf_op jit(solution)/shard_map/ppermute | solution.py:24
  88.5 8.0 %collective-permute-start.8 = (bf16[192,512]{1,0:T(8,128)(2,1)S(1)}, bf16[192,512]{1,0:T(8,128)(2,1)S(1)}, u32[]{:S(2)}, u32[]{:S(2)}) collective-permute-start(bf16[192,512]{1,0:T(8,128)(2,1)S(1)} %slice.24), channel_id=1, source_target_pairs={{0,1},{1,2},{2,3},{3,4},{4,5},{5,6},{6,7},{7,0},{8,9},{9,10},{10,1... | collective-permute-start | bytes 589832 | tf_op jit(solution)/shard_map/ppermute | solution.py:24
  90.5 7.2 %collective-permute-start.9 = (bf16[192,512]{1,0:T(8,128)(2,1)S(1)}, bf16[192,512]{1,0:T(8,128)(2,1)S(1)}, u32[]{:S(2)}, u32[]{:S(2)}) collective-permute-start(bf16[192,512]{1,0:T(8,128)(2,1)S(1)} %slice.25), channel_id=1, source_target_pairs={{0,7},{1,0},{2,1},{3,2},{4,3},{5,4},{6,5},{7,6},{8,15},{9,8},{10,9... | collective-permute-start | bytes 589832 | tf_op jit(solution)/shard_map/ppermute | solution.py:24
  112.1 14.7 %copy-start.10 = (s32[192]{0:T(256)S(1)}, s32[192]{0:T(256)}, u32[]{:S(2)}) copy-start(s32[192]{0:T(256)} %ids_ref.7) | copy-start | bytes 2308
  112.1 16.6 %copy-start.1 = (bf16[192,512]{1,0:T(8,128)(2,1)S(1)}, bf16[192,512]{1,0:T(8,128)(2,1)}, u32[]{:S(2)}) copy-start(bf16[192,512]{1,0:T(8,128)(2,1)} %upstream_ref.3) | copy-start | bytes 589828
  112.1 16.6 %copy-start.8 = (f32[192,1]{1,0:T(8,128)S(1)}, f32[192,1]{1,0:T(8,128)}, u32[]{:S(2)}) copy-start(f32[192,1]{1,0:T(8,128)} %copy-done.7) | copy-start | bytes 2308
  119.7 39.2 %all-to-all-start.1 = ((bf16[8,144,512]{2,1,0:T(8,128)(2,1)}), bf16[8,144,512]{2,1,0:T(8,128)(2,1)S(1)}, u32[]{:S(2)}, u32[]{:S(2)}) async-start(bf16[8,144,512]{2,1,0:T(8,128)(2,1)} %get-tuple-element.31), calls=%async_computation.1 | async-start | bytes 2359296 | tf_op jit(solution)/shard_map/all_to_all | solution.py:338
  128.8 1.0 copy-start.3
  129.8 1.0 copy-start.5
Sparse Core Ops, SparseCore 0:
  27.8 84.2 all-gather.1
